TPU v7x, 32 devices: a whole 2x2x4 slice. The times are simulated.
32 devices in a mesh: dp: 8 (over z, core), vocab: 4 (over y, x).
Axes of the slice: x: 2, y: 2, z: 4, core: 2. Of those that a mesh axis runs over, the one named last changes fastest.
Arguments:
- student_hidden: bfloat16 [48, 5120], P('dp', 'vocab'), may hold values from -71 to 71
- teacher_hidden: bfloat16 [48, 4096], P('dp', 'vocab'), may hold values from -73 to 73
- student_head: bfloat16 [5632, 5120], P(('dp', 'vocab')), may hold values from -16 to 16
- teacher_head: bfloat16 [5632, 4096], P(('dp', 'vocab')), may hold values from -16 to 16
Outputs:
- hidden_grad: bfloat16 [48, 5120], P('dp', 'vocab')
- head_grad: bfloat16 [5632, 5120], P(('dp', 'vocab'))
All inputs are finite; a program needn't handle non-finite values.
Results may differ from a plain program's by a relative error of at most 0.017.
Values may be sent and summed in bfloat16 or wider, within the bound.
No kernel may reach another device: no remote copies, remote signals or barrier semaphores. Data moves between devices by JAX's collectives and lax.ppermute only.
A program may use at most 64 MiB of HBM per device.

v0:
```python
import jax
import jax.numpy as jnp
from jax import lax
from jax.sharding import PartitionSpec as P


def joined(value, axis, join):
    pieces = jax.tree.map(lambda part: lax.all_gather(part, axis), value)
    head = jax.tree.map(lambda part: part[0], pieces)
    tail = jax.tree.map(lambda part: part[1:], pieces)
    running, _ = lax.scan(lambda running, share: (join(running, share), None), head, tail)
    return running


def combine_rows(former, latter):
    student_peak = jnp.maximum(former[0], latter[0])
    former_scale = jnp.exp(former[0] - student_peak)
    latter_scale = jnp.exp(latter[0] - student_peak)
    student_total = former[1] * former_scale + latter[1] * latter_scale
    weighted = former[2] * former_scale + latter[2] * latter_scale
    teacher_peak = jnp.maximum(former[3], latter[3])
    teacher_total = former[4] * jnp.exp(former[3] - teacher_peak) + latter[4] * jnp.exp(
        latter[3] - teacher_peak
    )
    return (student_peak, student_total, weighted, teacher_peak, teacher_total)


def on_device(student_hidden, teacher_hidden, student_head, teacher_head):
    student_part, teacher_part = (
        lax.all_gather(student_hidden, "vocab", axis=1, tiled=True),
        lax.all_gather(teacher_hidden, "vocab", axis=1, tiled=True),
    )
    hidden_full = lax.all_gather(student_part, "dp", axis=0, tiled=True)
    student_logits = lax.dot_general(
        hidden_full, student_head, (((1,), (1,)), ((), ())), preferred_element_type=jnp.float32
    )
    teacher_logits = lax.dot_general(
        lax.all_gather(teacher_part, "dp", axis=0, tiled=True),
        teacher_head,
        (((1,), (1,)), ((), ())),
        preferred_element_type=jnp.float32,
    )
    local_peak = jnp.max(student_logits, axis=1, keepdims=True)
    shifted = jnp.exp(student_logits - local_peak)
    local_total = jnp.sum(shifted, axis=1, keepdims=True)
    local_weighted = jnp.sum(shifted * (student_logits - teacher_logits), axis=1, keepdims=True)
    other_peak = jnp.max(teacher_logits, axis=1, keepdims=True)
    other_total = jnp.sum(jnp.exp(teacher_logits - other_peak), axis=1, keepdims=True)
    merged = joined(
        (local_peak, local_total, local_weighted, other_peak, other_total),
        ("dp", "vocab"),
        combine_rows,
    )
    student_lse = merged[0] + jnp.log(merged[1])
    teacher_lse = merged[3] + jnp.log(merged[4])
    divergence = merged[2] / merged[1] - student_lse + teacher_lse
    log_student = student_logits - student_lse
    log_teacher = teacher_logits - teacher_lse
    probs = jnp.exp(log_student)
    gap = log_student - log_teacher
    logit_grad = (probs * (gap - divergence)).astype(jnp.bfloat16)
    partial_rows = lax.psum_scatter(
        jnp.dot(logit_grad, student_head, preferred_element_type=jnp.float32).astype(jnp.bfloat16),
        "dp",
        scatter_dimension=0,
        tiled=True,
    )
    hidden_grad = lax.psum_scatter(partial_rows, "vocab", scatter_dimension=1, tiled=True)
    head_grad = lax.dot_general(
        logit_grad, hidden_full, (((0,), (0,)), ((), ())), preferred_element_type=jnp.float32
    ).astype(jnp.bfloat16)
    return (hidden_grad, head_grad)


def solution(mesh):
    return jax.shard_map(
        on_device,
        mesh=mesh,
        in_specs=(
            P("dp", "vocab"),
            P("dp", "vocab"),
            P(("dp", "vocab"), None),
            P(("dp", "vocab"), None),
        ),
        out_specs=(P("dp", "vocab"), P(("dp", "vocab"), None)),
        check_vma=False,
    )
```

profile of v0, /device:TPU:0, one launch (start us, length us, event | category | flops | bytes accessed | tf_op | source)
XLA Modules:
  0.0 160.5 jit_solution(12754229406523222016)
XLA Ops:
  7.2 0.0 copy-start
  7.2 0.0 reduce-scatter.4.cloned.1.call-start
  7.2 10.0 %all_gather.31 = bf16[6,4096]{1,0:T(8,128)(2,1)S(1)} all-gather(bf16[6,1024]{1,0:T(8,128)(2,1)} %param.7), channel_id=1, replica_groups=mesh['dp'=8,'vocab'=4] {'vocab'}, dimensions={1}, use_global_device_ids=true | all-gather | bytes 61440 | tf_op jit(solution)/shard_map/all_gather | solution.py:31
  17.2 8.2 %all_gather.27 = bf16[6,5120]{1,0:T(8,128)(2,1)S(1)} all-gather(bf16[6,1280]{1,0:T(8,128)(2,1)} %param.6), channel_id=1, replica_groups=mesh['dp'=8,'vocab'=4] {'vocab'}, dimensions={1}, use_global_device_ids=true | all-gather | bytes 76800 | tf_op jit(solution)/shard_map/all_gather | solution.py:30
  25.4 15.4 %all-gather.6 = bf16[8,6,4096]{2,1,0:T(8,128)(2,1)S(1)} all-gather(bf16[1,6,4096]{2,1,0:T(8,128)(2,1)S(1)} %bitcast.68), channel_id=1, replica_groups=mesh['dp'=8,'vocab'=4] {'dp'}, dimensions={0}, use_global_device_ids=true | all-gather | bytes 442368 | tf_op jit(solution)/shard_map/all_gather | solution.py:38
  40.8 0.1 reshape.39
  40.9 15.2 %all-gather.5 = bf16[8,6,5120]{2,1,0:T(8,128)(2,1)S(1)} all-gather(bf16[1,6,5120]{2,1,0:T(8,128)(2,1)S(1)} %bitcast.67), channel_id=1, replica_groups=mesh['dp'=8,'vocab'=4] {'dp'}, dimensions={0}, use_global_device_ids=true | all-gather | bytes 552960 | tf_op jit(solution)/shard_map/all_gather | solution.py:33
  56.1 0.2 reshape.37
  56.3 2.0 %fusion.20 = (f32[48]{0:T(128)S(1)}, f32[48,176]{1,0:T(8,128)S(1)}) fusion(bf16[48,4096]{1,0:T(8,128)(2,1)S(1)} %reshape.39, bf16[176,4096]{1,0:T(8,128)(2,1)} %param.9), kind=kOutput, calls=%fused_computation.39 | convolution fusion | flops 69214416 | bytes 1868992 | tf_op jit(solution)/shard_map/dot_general | solution.py:37
  58.3 0.0 copy-done
  58.3 0.8 fusion.19
  59.1 0.3 dynamic-update-slice.3
  59.4 0.3 dynamic-update-slice
  59.7 0.2 multiply_reduce_fusion
  59.9 0.3 dynamic-update-slice.4
  60.2 0.3 dynamic-update-slice.2
  60.4 0.3 dynamic-update-slice.1
  60.7 39.9 %all-reduce.7 = (f32[1536]{0:T(1024)S(1)}, f32[1536]{0:T(1024)S(1)}, f32[1536]{0:T(1024)S(1)}, f32[1536]{0:T(1024)S(1)}, f32[1536]{0:T(1024)S(1)}) all-reduce(f32[1536]{0:T(1024)S(1)} %dynamic-update-slice, f32[1536]{0:T(1024)S(1)} %dynamic-update-slice.1, ...), channel_id=2, replica_groups=mesh['dp'=8,'vocab'=4] {'dp','vocab'}, use_global_device_ids=true, to_apply=%add | all-reduce | flops 7680 | bytes 61440
  100.6 0.1 slice.55
  100.7 0.1 slice.56
  100.8 0.1 slice.57
  100.9 0.1 slice.58
  100.9 0.1 slice.59
  101.0 0.1 reshape.25
  101.1 0.0 copy-start.1
  101.1 0.1 reshape.24
  101.2 0.1 reshape.23
  101.3 0.1 reshape.22
  101.4 0.1 reshape.21
  101.5 2.4 %while.18 = (s32[]{:T(128)}, f32[48,1]{0,1:T(1,128)S(1)}, f32[48,1]{0,1:T(1,128)S(1)}, f32[48,1]{0,1:T(1,128)S(1)}, f32[48,1]{0,1:T(1,128)S(1)}, /*index=5*/f32[...) while((s32[]{:T(128)}, f32[48,1]{0,1:T(1,128)S(1)}, ...), condition=%wide.region_6.7_spmd, body=%wide.region_5.6_spmd.sunk | while | flops 818 | bytes 3973 | solution.py:11
  103.9 0.1 multiply_convert_fusion
  104.0 0.4 convolution_convert_fusion.1
  104.5 19.5 %fusion = bf16[8,5120]{1,0:T(8,128)(2,1)S(1)} fusion(bf16[48,5120]{1,0:T(8,128)(2,1)S(1)} %convolution_convert_fusion.1), kind=kCustom, calls=%all-reduce-scatter | all-reduce-scatter fusion | flops 327681 | bytes 573952
  124.0 1.3 collective-permute-start
  125.3 1.3 collective-permute-start.1
  126.6 0.0 copy-done.1
  126.6 0.6 dynamic-slice.4
  127.9 0.8 collective-permute-done.1
  128.7 0.0 collective-permute-done
  128.7 0.6 concatenate
  129.3 0.7 constant_dynamic-slice_fusion.5
  129.9 0.0 reduce-scatter.4.cloned.1.call-update
  129.9 1.9 %convolution_convert_fusion = bf16[176,5120]{1,0:T(8,128)(2,1)} fusion(bf16[48,176]{1,0:T(8,128)(2,1)S(1)} %multiply_convert_fusion, bf16[48,5120]{1,0:T(8,128)(2,1)S(1)} %reshape.37), kind=kOutput, calls=%fused_computation.20 | convolution fusion | flops 87408640 | bytes 2310656 | tf_op jit(solution)/shard_map/dot_general | solution.py:69
  131.8 21.8 %reduce-scatter.4.cloned.1.call-done = bf16[6,1280]{1,0:T(8,128)(2,1)} async-done(((bf16[6,5120]{1,0:T(8,128)(2,1)}), bf16[6,1280]{1,0:T(8,128)(2,1)}) %reduce-scatter.4.cloned.1.call-update) | async-done | bytes 15376 | tf_op jit(solution)/shard_map/reduce_scatter | solution.py:68
  (103 shorter events, 1.7 us)
Async XLA Ops:
  7.2 51.2 %copy-start = (bf16[176,5120]{1,0:T(8,128)(2,1)S(1)}, bf16[176,5120]{1,0:T(8,128)(2,1)}, u32[]{:S(2)}) copy-start(bf16[176,5120]{1,0:T(8,128)(2,1)} %param.8) | copy-start | bytes 5406724
  7.2 146.5 %reduce-scatter.4.cloned.1.call-start = ((), (), s32[]{:S(2)}) async-start(), calls=%async_computation.1 | async-start | bytes 102400 | tf_op jit(solution)/shard_map/reduce_scatter | solution.py:68
  101.1 25.5 %copy-start.1 = (u32[32]{0:T(128)S(1)}, u32[32]{0:T(128)}, u32[]{:S(2)}) copy-start(u32[32]{0:T(128)} %constant.43) | copy-start | bytes 388
  124.0 4.7 %collective-permute-start = (bf16[8,5120]{1,0:T(8,128)(2,1)S(1)}, bf16[8,5120]{1,0:T(8,128)(2,1)S(1)}, u32[]{:S(2)}, u32[]{:S(2)}) collective-permute-start(bf16[8,5120]{1,0:T(8,128)(2,1)S(1)} %fusion), channel_id=1, source_target_pairs={{0,4},{4,8},{8,12},{12,16},{16,20},{20,24},{24,28},{1,5},{5,9},{9,... | collective-permute-start | bytes 245768
  125.3 3.3 %collective-permute-start.1 = (bf16[6,5120]{1,0:T(8,128)(2,1)S(1)}, bf16[6,5120]{1,0:T(8,128)(2,1)S(1)}, u32[]{:S(2)}, u32[]{:S(2)}) collective-permute-start(bf16[6,5120]{1,0:T(8,128)(2,1)S(1)} %slice.60), channel_id=1, source_target_pairs={{0,8},{4,12},{8,16},{12,20},{16,24},{20,28},{1,9},{5,13},{9,17},{1... | collective-permute-start | bytes 184328
Sparse Core Ops, SparseCore 0:
  130.1 23.5 reduce-scatter.3
where the time goes:
time: 161 us; the launch traced here: 160 us
  blocking collectives  108 us (67%)
  waiting for transfers between devices  22.6 us (14%)
  between operations  14.9 us (9%)
  matrix products  5.14 us (3%)
  local copies, waits for them, and re-layouts  4.41 us (3%)
  starting transfers between devices  2.63 us (2%)
  other arithmetic  1.91 us (1%)
    unnamed x2, blocking collectives  59.4 us
    reduce_scatter x1, waiting for transfers between devices, on_device(): lax.psum_scatter(partial_rows, 'vocab', scatter_dimension=1, tiled=True)  21.8 us
    all_gather x1, blocking collectives, on_device(): lax.all_gather(teacher_part, 'dp', axis=0, tiled=True)  15.4 us
    all_gather x1, blocking collectives, on_device(): hidden_full = lax.all_gather(student_part, 'dp', axis=0, tiled=True)  15.2 us
    all_gather x1, blocking collectives, on_device(): lax.all_gather(teacher_hidden, 'vocab', axis=1, tiled=True)  9.98 us
    all_gather x1, blocking collectives, on_device(): lax.all_gather(student_hidden, 'vocab', axis=1, tiled=True)  8.18 us
    unnamed x20, local copies, waits for them, and re-layouts  3.51 us
  transfers between devices with their start and end apart: 3, of which 2 were waited for; matrix products, arithmetic and copies ran while one was open for 2% of the time, Pallas kernels for 0%

commit v1 on v0

v1 whole, which is shorter than its diff:
```python
import jax
import jax.numpy as jnp
from jax import lax
from jax.sharding import PartitionSpec as P


def doubled(value, axis, size, bits):
    me = lax.axis_index(axis)
    for bit in bits:
        pairs = [(i, i ^ (1 << bit)) for i in range(size)]
        other = lax.ppermute(value, axis, pairs)
        upper = (me >> bit) & 1
        value = jnp.where(
            upper == 1,
            jnp.concatenate([other, value], axis=0),
            jnp.concatenate([value, other], axis=0),
        )
    return value


def build(dp, vocab):
    dp_bits = dp.bit_length() - 1
    vocab_bits = vocab.bit_length() - 1

    def on_device(student_hidden, teacher_hidden, student_head, teacher_head):
        rows, share = student_hidden.shape
        teacher_share = teacher_hidden.shape[1]
        tokens = rows * dp
        packed = jnp.concatenate([student_hidden, teacher_hidden], axis=1)[None]
        by_z = doubled(packed, "dp", dp, range(1, dp_bits))
        by_vocab = doubled(by_z[None], "vocab", vocab, range(vocab_bits))
        by_core = doubled(by_vocab[None], "dp", dp, range(1))
        whole = jnp.transpose(by_core, (2, 0, 3, 1, 4))
        student_full = whole[..., :share].reshape(tokens, share * vocab)
        teacher_full = whole[..., share:].reshape(tokens, teacher_share * vocab)

        contract = (((1,), (1,)), ((), ()))
        student_logits = lax.dot_general(
            student_full, student_head, contract, preferred_element_type=jnp.float32
        )
        teacher_logits = lax.dot_general(
            teacher_full, teacher_head, contract, preferred_element_type=jnp.float32
        )
        peak = jnp.max(student_logits, axis=1)
        shifted = jnp.exp(student_logits - peak[:, None])
        total = jnp.sum(shifted, axis=1)
        weighted = jnp.sum(shifted * (student_logits - teacher_logits), axis=1)
        other_peak = jnp.max(teacher_logits, axis=1)
        other_total = jnp.sum(jnp.exp(teacher_logits - other_peak[:, None]), axis=1)
        stats = jnp.stack([peak, total, weighted, other_peak, other_total])
        devices = dp * vocab
        every = lax.all_to_all(
            jnp.broadcast_to(stats[None], (devices,) + stats.shape),
            ("dp", "vocab"), 0, 0, tiled=True,
        )
        top = jnp.max(every[:, 0], axis=0)
        scale = jnp.exp(every[:, 0] - top)
        total_all = jnp.sum(every[:, 1] * scale, axis=0)
        weighted_all = jnp.sum(every[:, 2] * scale, axis=0)
        other_top = jnp.max(every[:, 3], axis=0)
        other_all = jnp.sum(every[:, 4] * jnp.exp(every[:, 3] - other_top), axis=0)
        student_lse = (top + jnp.log(total_all))[:, None]
        teacher_lse = (other_top + jnp.log(other_all))[:, None]
        divergence = (weighted_all / total_all)[:, None] - student_lse + teacher_lse
        log_student = student_logits - student_lse
        probs = jnp.exp(log_student)
        gap = log_student - (teacher_logits - teacher_lse)
        logit_grad = (probs * (gap - divergence)).astype(jnp.bfloat16)

        partial = jnp.dot(
            logit_grad, student_head, preferred_element_type=jnp.float32
        ).astype(jnp.bfloat16)
        by_feature = jnp.transpose(partial.reshape(tokens, vocab, share), (1, 0, 2))
        arrived = lax.all_to_all(by_feature, "vocab", 0, 0, tiled=True)
        summed = jnp.sum(arrived.astype(jnp.float32), axis=0).astype(jnp.bfloat16)
        landed = lax.all_to_all(summed.reshape(dp, rows, share), "dp", 0, 0, tiled=True)
        hidden_grad = jnp.sum(landed.astype(jnp.float32), axis=0).astype(jnp.bfloat16)

        head_grad = lax.dot_general(
            logit_grad, student_full, (((0,), (0,)), ((), ())), preferred_element_type=jnp.float32
        ).astype(jnp.bfloat16)
        return (hidden_grad, head_grad)

    return on_device


def solution(mesh):
    return jax.shard_map(
        build(mesh.shape["dp"], mesh.shape["vocab"]),
        mesh=mesh,
        in_specs=(
            P("dp", "vocab"),
            P("dp", "vocab"),
            P(("dp", "vocab"), None),
            P(("dp", "vocab"), None),
        ),
        out_specs=(P("dp", "vocab"), P(("dp", "vocab"), None)),
        check_vma=False,
    )
```

time: 161 us -> 69.8 us (0.43)
  blocking collectives: 108 us -> 24.8 us
  between operations: 14.9 us -> 0.83 us
  starting transfers between devices: 2.63 us -> 13.4 us
  waiting for transfers between devices: 22.6 us -> 19.4 us
  other arithmetic: 1.91 us -> 3.72 us
    unnamed x2 -> x0, blocking collectives: 59.4 us -> none
    all_gather x4 -> x0, blocking collectives: 48.7 us -> none  [the longest x1 15.4 us: on_device(): lax.all_gather(teacher_part, 'dp', axis=0, tiled=True)]
    all_to_all x0 -> x2, blocking collectives: none -> 24.8 us  [the longest x1 14 us: on_device(): lax.all_to_all(jnp.broadcast_to(stats[None], (devices,) + stats.shape), (...]
    reduce_scatter x1 -> x0, waiting for transfers between devices: 21.8 us -> none  [on_device(): lax.psum_scatter(partial_rows, 'vocab', scatter_dimension=1, tiled=True)]
    ppermute x0 -> x5, waiting for transfers between devices: none -> 14.1 us  [doubled(): other = lax.ppermute(value, axis, pairs)]
    ppermute x0 -> x5, starting transfers between devices: none -> 10.1 us  [doubled(): other = lax.ppermute(value, axis, pairs)]
    all_to_all x0 -> x1, waiting for transfers between devices: none -> 5.28 us  [on_device(): lax.all_to_all(summed.reshape(dp, rows, share), 'dp', 0, 0, tiled=True)]
    all_to_all x0 -> x1, starting transfers between devices: none -> 3.38 us  [on_device(): lax.all_to_all(summed.reshape(dp, rows, share), 'dp', 0, 0, tiled=True)]
  transfers between devices with their start and end apart: 3 -> 6, of which waited for: 2 -> 6; matrix products, arithmetic and copies ran while one was open for 2% -> 3% of each run, Pallas kernels for 0% -> 0%
where the time goes in v1:
time: 69.8 us; the launch traced here: 69.4 us
  blocking collectives  24.8 us (36%)
  waiting for transfers between devices  19.4 us (28%)
  starting transfers between devices  13.4 us (19%)
  matrix products  3.77 us (5%)
  other arithmetic  3.72 us (5%)
  local copies, waits for them, and re-layouts  3.52 us (5%)
  between operations  0.83 us (1%)
    ppermute x5, waiting for transfers between devices, doubled(): other = lax.ppermute(value, axis, pairs)  14.1 us
    all_to_all x1, blocking collectives, on_device(): lax.all_to_all(jnp.broadcast_to(stats[None], (devices,) + stats.shape), (...  14 us
    all_to_all x1, blocking collectives, on_device(): arrived = lax.all_to_all(by_feature, 'vocab', 0, 0, tiled=True)  10.8 us
    ppermute x5, starting transfers between devices, doubled(): other = lax.ppermute(value, axis, pairs)  10.1 us
    all_to_all x1, waiting for transfers between devices, on_device(): lax.all_to_all(summed.reshape(dp, rows, share), 'dp', 0, 0, tiled=True)  5.28 us
    all_to_all x1, starting transfers between devices, on_device(): lax.all_to_all(summed.reshape(dp, rows, share), 'dp', 0, 0, tiled=True)  3.38 us
    dot_general x1, matrix products, on_device(): lax.dot_general(logit_grad, student_full, (((0,), (0,)), ((), ())), prefe...  1.87 us
  transfers between devices with their start and end apart: 6, of which 6 were waited for; matrix products, arithmetic and copies ran while one was open for 3% of the time, Pallas kernels for 0%

profile of v1, /device:TPU:0, one launch (start us, length us, event | category | flops | bytes accessed | tf_op | source)
XLA Modules:
  0.0 69.4 jit_solution(13339447483266674021)
XLA Ops:
  0.6 0.0 copy-start
  0.6 0.9 %maximum_bitcast_fusion = bf16[1,6,2304]{2,1,0:T(8,128)(2,1)S(1)} fusion(bf16[6,1024]{1,0:T(8,128)(2,1)} %param.5, bf16[6,1280]{1,0:T(8,128)(2,1)} %param.4), kind=kLoop, calls=%fused_computation.14 | loop fusion | flops 55296 | bytes 55296 | tf_op jit(solution)/shard_map/broadcast_in_dim | solution.py:29
  1.5 3.1 %collective-permute-start = (bf16[1,6,2304]{2,1,0:T(8,128)(2,1)S(1)}, bf16[1,6,2304]{2,1,0:T(8,128)(2,1)S(1)}, u32[]{:S(2)}, u32[]{:S(2)}) collective-permute-start(bf16[1,6,2304]{2,1,0:T(8,128)(2,1)S(1)} %maximum_bitcast_fusion), channel_id=1, source_target_pairs={{0,8},{4,12},{8,0},{12,4},{16,24},{20,28},{24,16},{28,20},{1,9},{5... | collective-permute-start | bytes 82952 | tf_op jit(solution)/shard_map/ppermute | solution.py:11
  4.6 1.9 %collective-permute-done = bf16[1,6,2304]{2,1,0:T(8,128)(2,1)S(1)} collective-permute-done((bf16[1,6,2304]{2,1,0:T(8,128)(2,1)S(1)}, bf16[1,6,2304]{2,1,0:T(8,128)(2,1)S(1)}, u32[]{:S(2)}, u32[]{:S(2)}) %collective-permute-start) | collective-permute-done | bytes 27680 | tf_op jit(solution)/shard_map/ppermute | solution.py:11
  6.6 3.1 %collective-permute-start.1 = (bf16[2,6,2304]{2,1,0:T(8,128)(2,1)S(1)}, bf16[2,6,2304]{2,1,0:T(8,128)(2,1)S(1)}, u32[]{:S(2)}, u32[]{:S(2)}) collective-permute-start(bf16[2,6,2304]{2,1,0:T(8,128)(2,1)S(1)} %maximum_select_fusion.4), channel_id=1, source_target_pairs={{0,16},{4,20},{8,24},{12,28},{16,0},{20,4},{24,8},{28,12},{1,17},{... | collective-permute-start | bytes 165896 | tf_op jit(solution)/shard_map/ppermute | solution.py:11
  9.7 2.3 %collective-permute-done.1 = bf16[2,6,2304]{2,1,0:T(8,128)(2,1)S(1)} collective-permute-done((bf16[2,6,2304]{2,1,0:T(8,128)(2,1)S(1)}, bf16[2,6,2304]{2,1,0:T(8,128)(2,1)S(1)}, u32[]{:S(2)}, u32[]{:S(2)}) %collective-permute-start.1) | collective-permute-done | bytes 55328 | tf_op jit(solution)/shard_map/ppermute | solution.py:11
  12.0 0.1 maximum_select_fusion.3
  12.1 1.9 %collective-permute-start.2 = (bf16[1,4,6,2304]{3,2,1,0:T(8,128)(2,1)S(1)}, bf16[1,4,6,2304]{3,2,1,0:T(8,128)(2,1)S(1)}, u32[]{:S(2)}, u32[]{:S(2)}) collective-permute-start(bf16[1,4,6,2304]{3,2,1,0:T(8,128)(2,1)S(1)} %maximum_select_fusion.3), channel_id=1, source_target_pairs={{0,1},{1,0},{2,3},{3,2},{4,5},{5,4},{6,7},{7,6},{8,9},{9,8},{10,11... | collective-permute-start | bytes 331784 | tf_op jit(solution)/shard_map/ppermute | solution.py:11
  14.0 3.3 %collective-permute-done.2 = bf16[1,4,6,2304]{3,2,1,0:T(8,128)(2,1)S(1)} collective-permute-done((bf16[1,4,6,2304]{3,2,1,0:T(8,128)(2,1)S(1)}, bf16[1,4,6,2304]{3,2,1,0:T(8,128)(2,1)S(1)}, u32[]{:S(2)}, u32[]{:S(2)}) %collective-permute-start.2) | collective-permute-done | bytes 110624 | tf_op jit(solution)/shard_map/ppermute | solution.py:11
  17.3 0.1 maximum_select_fusion.2
  17.4 1.9 %collective-permute-start.3 = (bf16[2,4,6,2304]{3,2,1,0:T(8,128)(2,1)S(1)}, bf16[2,4,6,2304]{3,2,1,0:T(8,128)(2,1)S(1)}, u32[]{:S(2)}, u32[]{:S(2)}) collective-permute-start(bf16[2,4,6,2304]{3,2,1,0:T(8,128)(2,1)S(1)} %maximum_select_fusion.2), channel_id=1, source_target_pairs={{0,2},{1,3},{2,0},{3,1},{4,6},{5,7},{6,4},{7,5},{8,10},{9,11},{10,... | collective-permute-start | bytes 663560 | tf_op jit(solution)/shard_map/ppermute | solution.py:11
  19.3 0.1 fusion.13
  19.4 4.8 %collective-permute-done.3 = bf16[2,4,6,2304]{3,2,1,0:T(8,128)(2,1)S(1)} collective-permute-done((bf16[2,4,6,2304]{3,2,1,0:T(8,128)(2,1)S(1)}, bf16[2,4,6,2304]{3,2,1,0:T(8,128)(2,1)S(1)}, u32[]{:S(2)}, u32[]{:S(2)}) %collective-permute-start.3) | collective-permute-done | bytes 221216 | tf_op jit(solution)/shard_map/ppermute | solution.py:11
  24.2 0.3 maximum_select_fusion.1
  24.5 0.2 copy.35
  24.6 0.1 collective-permute-start.4
  24.7 1.8 %collective-permute-done.4 = bf16[1,4,4,6,2304]{4,2,3,1,0:T(4,128)(2,1)S(1)} collective-permute-done((bf16[1,4,4,6,2304]{4,2,3,1,0:T(4,128)(2,1)S(1)}, bf16[1,4,4,6,2304]{4,2,3,1,0:T(4,128)(2,1)S(1)}, u32[]{:S(2)}, u32[]{:S(2)}) %collective-permute-start.4) | collective-permute-done | bytes 442400 | tf_op jit(solution)/shard_map/ppermute | solution.py:11
  26.5 0.1 copy.36
  26.6 0.4 fusion
  27.0 0.1 slice.31
  27.1 0.3 copy.39
  27.4 0.0 copy-start.1
  27.4 0.1 copy.49
  27.5 0.4 copy.38
  27.9 0.1 copy.48
  28.0 0.8 %copy-done.1 = bf16[176,4096]{1,0:T(8,128)(2,1)S(1)} copy-done((bf16[176,4096]{1,0:T(8,128)(2,1)S(1)}, bf16[176,4096]{1,0:T(8,128)(2,1)}, u32[]{:S(2)}) %copy-start.1) | copy-done | bytes 1441816
  28.8 0.7 fusion.4
  29.4 0.0 copy-done
  29.4 0.8 %fusion.3 = (f32[48]{0:T(128)S(1)}, f32[48,176]{1,0:T(8,128)S(1)}) fusion(bf16[48,5120]{1,0:T(8,128)(2,1)S(1)} %bitcast.47, bf16[176,5120]{1,0:T(8,128)(2,1)S(1)} %copy-done), kind=kOutput, calls=%fused_computation.23 | convolution fusion | flops 86515920 | bytes 2327744 | tf_op jit(solution)/shard_map/dot_general | solution.py:38
  30.2 0.2 multiply_reduce_fusion
  30.5 0.1 reshape.264
  30.6 14.0 %all_to_all.15 = f32[32,1,240]{2,1,0:T(1,128)S(1)} all-to-all(f32[32,1,240]{2,1,0:T(1,128)S(1)} %reshape.264), channel_id=1, replica_groups=mesh['dp'=8,'vocab'=4] {'dp','vocab'}, dimensions={0} | all-to-all | bytes 61440 | tf_op jit(solution)/shard_map/all_to_all | solution.py:52
  44.6 0.5 broadcast.37
  45.1 0.7 %reduce.4 = f32[32,240]{1,0:T(8,128)S(1)} reduce(f32[32,1,240]{2,1,0:T(1,128)S(1)} %all_to_all.15, f32[]{:T(128)} %broadcast.37), dimensions={1}, to_apply=%all_to_all.9.reduce_sub_computation | reduce | bytes 61444 | tf_op jit(solution)/shard_map/all_to_all | solution.py:52
  45.8 0.1 reshape.265
  45.9 0.1 fusion.2
  46.1 0.1 multiply_convert_fusion
  46.2 0.4 convolution_convert_fusion.1
  46.7 10.8 %all_to_all.16 = bf16[4,48,1280]{2,1,0:T(8,128)(2,1)S(1)} all-to-all(bf16[4,48,1280]{2,1,0:T(8,128)(2,1)S(1)} %bitcast.50), channel_id=1, replica_groups=mesh['dp'=8,'vocab'=4] {'vocab'}, dimensions={0} | all-to-all | bytes 983040 | tf_op jit(solution)/shard_map/all_to_all | solution.py:74
  57.5 0.1 reduce_sum.84
  57.5 0.7 %reshape.263 = bf16[8,6,1280]{2,1,0:T(8,128)(2,1)} reshape(bf16[48,1280]{1,0:T(8,128)(2,1)S(1)} %reduce_sum.84) | data formatting | bytes 245760 | tf_op jit(solution)/shard_map/reshape | solution.py:76
  58.2 3.4 %all-to-all-start.2 = ((bf16[8,6,1280]{2,1,0:T(8,128)(2,1)}), bf16[8,6,1280]{2,1,0:T(8,128)(2,1)S(1)}, u32[]{:S(2)}, u32[]{:S(2)}) async-start(bf16[8,6,1280]{2,1,0:T(8,128)(2,1)} %reshape.263), calls=%async_computation.2 | async-start | bytes 327680 | tf_op jit(solution)/shard_map/all_to_all | solution.py:76
  61.6 1.9 %convolution_convert_fusion = bf16[176,5120]{1,0:T(8,128)(2,1)} fusion(bf16[48,176]{1,0:T(8,128)(2,1)S(1)} %multiply_convert_fusion, bf16[48,5120]{1,0:T(8,128)(2,1)S(1)} %bitcast.48), kind=kOutput, calls=%fused_computation | convolution fusion | flops 87408640 | bytes 2310656 | tf_op jit(solution)/shard_map/dot_general | solution.py:79
  63.5 5.3 %all-to-all-done.2 = bf16[8,6,1280]{2,1,0:T(8,128)(2,1)S(1)} async-done(((bf16[8,6,1280]{2,1,0:T(8,128)(2,1)}), bf16[8,6,1280]{2,1,0:T(8,128)(2,1)S(1)}, u32[]{:S(2)}, u32[]{:S(2)}) %all-to-all-start.2) | async-done | bytes 122912 | tf_op jit(solution)/shard_map/all_to_all | solution.py:76
  68.8 0.6 reduce_sum.85
  (10 shorter events, 0.3 us)
Async XLA Ops:
  0.6 28.8 %copy-start = (bf16[176,5120]{1,0:T(8,128)(2,1)S(1)}, bf16[176,5120]{1,0:T(8,128)(2,1)}, u32[]{:S(2)}) copy-start(bf16[176,5120]{1,0:T(8,128)(2,1)} %param.6) | copy-start | bytes 5406724
  1.5 5.0 %collective-permute-start = (bf16[1,6,2304]{2,1,0:T(8,128)(2,1)S(1)}, bf16[1,6,2304]{2,1,0:T(8,128)(2,1)S(1)}, u32[]{:S(2)}, u32[]{:S(2)}) collective-permute-start(bf16[1,6,2304]{2,1,0:T(8,128)(2,1)S(1)} %maximum_bitcast_fusion), channel_id=1, source_target_pairs={{0,8},{4,12},{8,0},{12,4},{16,24},{20,28},{24,16},{28,20},{1,9},{5... | collective-permute-start | bytes 82952 | tf_op jit(solution)/shard_map/ppermute | solution.py:11
  6.6 5.4 %collective-permute-start.1 = (bf16[2,6,2304]{2,1,0:T(8,128)(2,1)S(1)}, bf16[2,6,2304]{2,1,0:T(8,128)(2,1)S(1)}, u32[]{:S(2)}, u32[]{:S(2)}) collective-permute-start(bf16[2,6,2304]{2,1,0:T(8,128)(2,1)S(1)} %maximum_select_fusion.4), channel_id=1, source_target_pairs={{0,16},{4,20},{8,24},{12,28},{16,0},{20,4},{24,8},{28,12},{1,17},{... | collective-permute-start | bytes 165896 | tf_op jit(solution)/shard_map/ppermute | solution.py:11
  12.1 5.2 %collective-permute-start.2 = (bf16[1,4,6,2304]{3,2,1,0:T(8,128)(2,1)S(1)}, bf16[1,4,6,2304]{3,2,1,0:T(8,128)(2,1)S(1)}, u32[]{:S(2)}, u32[]{:S(2)}) collective-permute-start(bf16[1,4,6,2304]{3,2,1,0:T(8,128)(2,1)S(1)} %maximum_select_fusion.3), channel_id=1, source_target_pairs={{0,1},{1,0},{2,3},{3,2},{4,5},{5,4},{6,7},{7,6},{8,9},{9,8},{10,11... | collective-permute-start | bytes 331784 | tf_op jit(solution)/shard_map/ppermute | solution.py:11
  17.4 6.8 %collective-permute-start.3 = (bf16[2,4,6,2304]{3,2,1,0:T(8,128)(2,1)S(1)}, bf16[2,4,6,2304]{3,2,1,0:T(8,128)(2,1)S(1)}, u32[]{:S(2)}, u32[]{:S(2)}) collective-permute-start(bf16[2,4,6,2304]{3,2,1,0:T(8,128)(2,1)S(1)} %maximum_select_fusion.2), channel_id=1, source_target_pairs={{0,2},{1,3},{2,0},{3,1},{4,6},{5,7},{6,4},{7,5},{8,10},{9,11},{10,... | collective-permute-start | bytes 663560 | tf_op jit(solution)/shard_map/ppermute | solution.py:11
  24.6 1.9 %collective-permute-start.4 = (bf16[1,4,4,6,2304]{4,2,3,1,0:T(4,128)(2,1)S(1)}, bf16[1,4,4,6,2304]{4,2,3,1,0:T(4,128)(2,1)S(1)}, u32[]{:S(2)}, u32[]{:S(2)}) collective-permute-start(bf16[1,4,4,6,2304]{4,2,3,1,0:T(4,128)(2,1)S(1)} %copy.35), channel_id=1, source_target_pairs={{0,4},{4,0},{8,12},{12,8},{16,20},{20,16},{24,28},{28,24},{1,5},{5... | collective-permute-start | bytes 1327112 | tf_op jit(solution)/shard_map/ppermute | solution.py:11
  27.4 1.4 %copy-start.1 = (bf16[176,4096]{1,0:T(8,128)(2,1)S(1)}, bf16[176,4096]{1,0:T(8,128)(2,1)}, u32[]{:S(2)}) copy-start(bf16[176,4096]{1,0:T(8,128)(2,1)} %param.7) | copy-start | bytes 4325380
  58.2 10.5 %all-to-all-start.2 = ((bf16[8,6,1280]{2,1,0:T(8,128)(2,1)}), bf16[8,6,1280]{2,1,0:T(8,128)(2,1)S(1)}, u32[]{:S(2)}, u32[]{:S(2)}) async-start(bf16[8,6,1280]{2,1,0:T(8,128)(2,1)} %reshape.263), calls=%async_computation.2 | async-start | bytes 327680 | tf_op jit(solution)/shard_map/all_to_all | solution.py:76

commit v2 on v1

--- a/solution.py
+++ b/solution.py
@@ -4,35 +4,63 @@
 from jax.sharding import PartitionSpec as P
 
 
-def doubled(value, axis, size, bits):
-    me = lax.axis_index(axis)
-    for bit in bits:
-        pairs = [(i, i ^ (1 << bit)) for i in range(size)]
-        other = lax.ppermute(value, axis, pairs)
-        upper = (me >> bit) & 1
-        value = jnp.where(
-            upper == 1,
-            jnp.concatenate([other, value], axis=0),
-            jnp.concatenate([value, other], axis=0),
-        )
+def grouped(bits):
+    bits = list(bits)
+    return [bits[i : i + 2] for i in range(0, len(bits), 2)]
+
+
+def mask_of(j, bits):
+    return sum(((j >> k) & 1) << bit for k, bit in enumerate(bits))
+
+
+def reorder(parts, index, bits):
+    for k, bit in enumerate(bits):
+        upper = ((index >> bit) & 1) == 1
+        parts = [jnp.where(upper, parts[j ^ (1 << k)], parts[j]) for j in range(len(parts))]
+    return parts
+
+
+def swap(value, axis, size, mask):
+    return lax.ppermute(value, axis, [(i, i ^ mask) for i in range(size)])
+
+
+def gathered(value, axis, size, bits, dim):
+    index = lax.axis_index(axis)
+    for group in grouped(bits):
+        parts = [value] + [
+            swap(value, axis, size, mask_of(j, group)) for j in range(1, 1 << len(group))
+        ]
+        value = jnp.concatenate(reorder(parts, index, group), axis=dim)
     return value
 
 
+def scattered(total, axis, size, bits, dim):
+    index = lax.axis_index(axis)
+    for group in reversed(grouped(bits)):
+        parts = reorder(jnp.split(total, 1 << len(group), axis=dim), index, group)
+        total = parts[0]
+        landed = [
+            swap(parts[j].astype(jnp.bfloat16), axis, size, mask_of(j, group))
+            for j in range(1, 1 << len(group))
+        ]
+        for part in landed:
+            total = total + part.astype(jnp.float32)
+    return total
+
+
 def build(dp, vocab):
-    dp_bits = dp.bit_length() - 1
-    vocab_bits = vocab.bit_length() - 1
+    dp_bits = range(dp.bit_length() - 1)
+    vocab_bits = range(vocab.bit_length() - 1)
+    core, z_bits = dp_bits[:1], dp_bits[1:]
 
     def on_device(student_hidden, teacher_hidden, student_head, teacher_head):
         rows, share = student_hidden.shape
-        teacher_share = teacher_hidden.shape[1]
-        tokens = rows * dp
-        packed = jnp.concatenate([student_hidden, teacher_hidden], axis=1)[None]
-        by_z = doubled(packed, "dp", dp, range(1, dp_bits))
-        by_vocab = doubled(by_z[None], "vocab", vocab, range(vocab_bits))
-        by_core = doubled(by_vocab[None], "dp", dp, range(1))
-        whole = jnp.transpose(by_core, (2, 0, 3, 1, 4))
-        student_full = whole[..., :share].reshape(tokens, share * vocab)
-        teacher_full = whole[..., share:].reshape(tokens, teacher_share * vocab)
+        packed = jnp.concatenate([student_hidden, teacher_hidden], axis=1)
+        by_z = gathered(packed, "dp", dp, z_bits, 0)
+        by_vocab = gathered(by_z[None], "vocab", vocab, vocab_bits, 0)
+        whole = gathered(by_vocab, "dp", dp, core, 1)
+        student_full = jnp.concatenate([whole[i, :, :share] for i in range(vocab)], axis=1)
+        teacher_full = jnp.concatenate([whole[i, :, share:] for i in range(vocab)], axis=1)
 
         contract = (((1,), (1,)), ((), ()))
         student_logits = lax.dot_general(
@@ -67,14 +95,16 @@
         gap = log_student - (teacher_logits - teacher_lse)
         logit_grad = (probs * (gap - divergence)).astype(jnp.bfloat16)
 
-        partial = jnp.dot(
-            logit_grad, student_head, preferred_element_type=jnp.float32
-        ).astype(jnp.bfloat16)
-        by_feature = jnp.transpose(partial.reshape(tokens, vocab, share), (1, 0, 2))
-        arrived = lax.all_to_all(by_feature, "vocab", 0, 0, tiled=True)
-        summed = jnp.sum(arrived.astype(jnp.float32), axis=0).astype(jnp.bfloat16)
-        landed = lax.all_to_all(summed.reshape(dp, rows, share), "dp", 0, 0, tiled=True)
-        hidden_grad = jnp.sum(landed.astype(jnp.float32), axis=0).astype(jnp.bfloat16)
+        index = lax.axis_index("dp")
+        half = logit_grad.shape[0] // 2
+        keep, send = reorder([logit_grad[:half], logit_grad[half:]], index, core)
+        away = jnp.dot(send, student_head, preferred_element_type=jnp.float32).astype(jnp.bfloat16)
+        landed = swap(away, "dp", dp, 1)
+        acc = jnp.dot(keep, student_head, preferred_element_type=jnp.float32)
+        acc = acc + landed.astype(jnp.float32)
+        acc = scattered(acc, "vocab", vocab, vocab_bits, 1)
+        acc = scattered(acc, "dp", dp, z_bits, 0)
+        hidden_grad = acc.astype(jnp.bfloat16)
 
         head_grad = lax.dot_general(
             logit_grad, student_full, (((0,), (0,)), ((), ())), preferred_element_type=jnp.float32

time: 69.8 us -> 53.5 us (0.77)
  blocking collectives: 24.8 us -> 8.99 us
  starting transfers between devices: 13.4 us -> 17.3 us
  waiting for transfers between devices: 19.4 us -> 17.4 us
  other arithmetic: 3.72 us -> 2.33 us
  local copies, waits for them, and re-layouts: 3.52 us -> 2.4 us
    all_to_all x1 -> x0, blocking collectives: 10.8 us -> none  [on_device(): arrived = lax.all_to_all(by_feature, 'vocab', 0, 0, tiled=True)]
    ppermute x5 -> x14, starting transfers between devices: 10.1 us -> 17.3 us  [swap(): return lax.ppermute(value, axis, [(i, i ^ mask) for i in range(size)])]
    all_to_all x1 -> x0, waiting for transfers between devices: 5.28 us -> none  [on_device(): lax.all_to_all(summed.reshape(dp, rows, share), 'dp', 0, 0, tiled=True)]
    all_to_all x1, blocking collectives: 14 us -> 8.99 us  [on_device(): lax.all_to_all(jnp.broadcast_to(stats[None], (devices,) + stats.shape), (...]
    all_to_all x1 -> x0, starting transfers between devices: 3.38 us -> none  [on_device(): lax.all_to_all(summed.reshape(dp, rows, share), 'dp', 0, 0, tiled=True)]
    ppermute x5 -> x14, waiting for transfers between devices: 14.1 us -> 17.4 us  [swap(): return lax.ppermute(value, axis, [(i, i ^ mask) for i in range(size)])]
    broadcast_in_dim x1, other arithmetic: 0.89 us -> 0.06 us  [on_device(): by_vocab = gathered(by_z[None], 'vocab', vocab, vocab_bits, 0)]
    slice x4 -> x0, local copies, waits for them, and re-layouts: 0.79 us -> none  [the longest x2 0.43 us: on_device(): student_full = whole[..., :share].reshape(tokens, share * vocab)]
  transfers between devices with their start and end apart: 6 -> 14, of which waited for: 6 -> 11; matrix products, arithmetic and copies ran while one was open for 3% -> 3% of each run, Pallas kernels for 0% -> 0%
where the time goes in v2:
time: 53.5 us; the launch traced here: 53.3 us
  waiting for transfers between devices  17.4 us (33%)
  starting transfers between devices  17.3 us (32%)
  blocking collectives  8.99 us (17%)
  matrix products  4.04 us (8%)
  local copies, waits for them, and re-layouts  2.4 us (4%)
  other arithmetic  2.33 us (4%)
  between operations  0.81 us (2%)
    ppermute x14, waiting for transfers between devices, swap(): return lax.ppermute(value, axis, [(i, i ^ mask) for i in range(size)])  17.4 us
    ppermute x14, starting transfers between devices, swap(): return lax.ppermute(value, axis, [(i, i ^ mask) for i in range(size)])  17.3 us
    all_to_all x1, blocking collectives, on_device(): lax.all_to_all(jnp.broadcast_to(stats[None], (devices,) + stats.shape), (...  8.99 us
    dot_general x1, matrix products, on_device(): lax.dot_general(logit_grad, student_full, (((0,), (0,)), ((), ())), prefe...  1.87 us
    unnamed x7, local copies, waits for them, and re-layouts  1.08 us
  transfers between devices with their start and end apart: 14, of which 11 were waited for; matrix products, arithmetic and copies ran while one was open for 3% of the time, Pallas kernels for 0%

profile of v2, /device:TPU:0, one launch (start us, length us, event | category | flops | bytes accessed | tf_op | source)
XLA Modules:
  0.0 53.3 jit_solution(10685806295572824678)
XLA Ops:
  0.6 0.0 copy-start
  0.6 0.9 %constant_dynamic-update-slice_fusion.1 = bf16[6,2304]{1,0:T(8,128)(2,1)S(1)} fusion(bf16[6,1280]{1,0:T(8,128)(2,1)} %param.4), kind=kLoop, calls=%fused_computation.98 | loop fusion | bytes 35840
  1.5 0.7 %constant_dynamic-update-slice_fusion = bf16[6,2304]{1,0:T(8,128)(2,1)S(1)} fusion(bf16[6,2304]{1,0:T(8,128)(2,1)S(1)} %constant_dynamic-update-slice_fusion.1, bf16[6,1024]{1,0:T(8,128)(2,1)} %param.5), kind=kLoop, calls=%fused_computation.97 | loop fusion | bytes 28672 | tf_op jit(solution)/shard_map/concatenate | solution.py:58
  2.2 3.0 %collective-permute-start.2 = (bf16[6,2304]{1,0:T(8,128)(2,1)S(1)}, bf16[6,2304]{1,0:T(8,128)(2,1)S(1)}, u32[]{:S(2)}, u32[]{:S(2)}) collective-permute-start(bf16[6,2304]{1,0:T(8,128)(2,1)S(1)} %constant_dynamic-update-slice_fusion), channel_id=1, source_target_pairs={{0,8},{4,12},{8,0},{12,4},{16,24},{20,28},{24,16},{28,20},{1,9},{5... | collective-permute-start | bytes 82952 | tf_op jit(solution)/shard_map/ppermute | solution.py:24
  5.2 2.6 %collective-permute-start.1 = (bf16[6,2304]{1,0:T(8,128)(2,1)S(1)}, bf16[6,2304]{1,0:T(8,128)(2,1)S(1)}, u32[]{:S(2)}, u32[]{:S(2)}) collective-permute-start(bf16[6,2304]{1,0:T(8,128)(2,1)S(1)} %constant_dynamic-update-slice_fusion), channel_id=1, source_target_pairs={{0,16},{4,20},{8,24},{12,28},{16,0},{20,4},{24,8},{28,12},{1,17},{... | collective-permute-start | bytes 82952 | tf_op jit(solution)/shard_map/ppermute | solution.py:24
  7.8 0.0 collective-permute-start
  7.8 0.0 collective-permute-done.2
  7.8 2.9 %collective-permute-done.1 = bf16[6,2304]{1,0:T(8,128)(2,1)S(1)} collective-permute-done((bf16[6,2304]{1,0:T(8,128)(2,1)S(1)}, bf16[6,2304]{1,0:T(8,128)(2,1)S(1)}, u32[]{:S(2)}, u32[]{:S(2)}) %collective-permute-start.1) | collective-permute-done | bytes 27680 | tf_op jit(solution)/shard_map/ppermute | solution.py:24
  10.8 2.8 %collective-permute-done = bf16[6,2304]{1,0:T(8,128)(2,1)S(1)} collective-permute-done((bf16[6,2304]{1,0:T(8,128)(2,1)S(1)}, bf16[6,2304]{1,0:T(8,128)(2,1)S(1)}, u32[]{:S(2)}, u32[]{:S(2)}) %collective-permute-start) | collective-permute-done | bytes 27680 | tf_op jit(solution)/shard_map/ppermute | solution.py:24
  13.6 0.1 maximum_bitcast_fusion
  13.7 1.6 %collective-permute-start.5 = (bf16[1,24,2304]{2,1,0:T(8,128)(2,1)S(1)}, bf16[1,24,2304]{2,1,0:T(8,128)(2,1)S(1)}, u32[]{:S(2)}, u32[]{:S(2)}) collective-permute-start(bf16[1,24,2304]{2,1,0:T(8,128)(2,1)S(1)} %maximum_bitcast_fusion), channel_id=1, source_target_pairs={{0,1},{1,0},{2,3},{3,2},{4,5},{5,4},{6,7},{7,6},{8,9},{9,8},{10,11... | collective-permute-start | bytes 331784 | tf_op jit(solution)/shard_map/ppermute | solution.py:24
  15.2 1.5 %collective-permute-start.4 = (bf16[1,24,2304]{2,1,0:T(8,128)(2,1)S(1)}, bf16[1,24,2304]{2,1,0:T(8,128)(2,1)S(1)}, u32[]{:S(2)}, u32[]{:S(2)}) collective-permute-start(bf16[1,24,2304]{2,1,0:T(8,128)(2,1)S(1)} %maximum_bitcast_fusion), channel_id=1, source_target_pairs={{0,2},{1,3},{2,0},{3,1},{4,6},{5,7},{6,4},{7,5},{8,10},{9,11},{10,... | collective-permute-start | bytes 331784 | tf_op jit(solution)/shard_map/ppermute | solution.py:24
  16.8 0.5 collective-permute-start.3
  17.2 2.1 %collective-permute-done.5 = bf16[1,24,2304]{2,1,0:T(8,128)(2,1)S(1)} collective-permute-done((bf16[1,24,2304]{2,1,0:T(8,128)(2,1)S(1)}, bf16[1,24,2304]{2,1,0:T(8,128)(2,1)S(1)}, u32[]{:S(2)}, u32[]{:S(2)}) %collective-permute-start.5) | collective-permute-done | bytes 110624 | tf_op jit(solution)/shard_map/ppermute | solution.py:24
  19.3 1.2 %collective-permute-done.4 = bf16[1,24,2304]{2,1,0:T(8,128)(2,1)S(1)} collective-permute-done((bf16[1,24,2304]{2,1,0:T(8,128)(2,1)S(1)}, bf16[1,24,2304]{2,1,0:T(8,128)(2,1)S(1)}, u32[]{:S(2)}, u32[]{:S(2)}) %collective-permute-start.4) | collective-permute-done | bytes 110624 | tf_op jit(solution)/shard_map/ppermute | solution.py:24
  20.6 1.8 %collective-permute-done.3 = bf16[1,24,2304]{2,1,0:T(8,128)(2,1)S(1)} collective-permute-done((bf16[1,24,2304]{2,1,0:T(8,128)(2,1)S(1)}, bf16[1,24,2304]{2,1,0:T(8,128)(2,1)S(1)}, u32[]{:S(2)}, u32[]{:S(2)}) %collective-permute-start.3) | collective-permute-done | bytes 110624 | tf_op jit(solution)/shard_map/ppermute | solution.py:24
  22.4 0.1 broadcast_select_fusion.9
  22.6 0.1 pad_maximum_fusion.1
  22.6 0.1 collective-permute-start.6
  22.7 0.0 copy-start.1
  22.7 1.8 %collective-permute-done.6 = bf16[4,24,2304]{2,1,0:T(8,128)(2,1)S(1)} collective-permute-done((bf16[4,24,2304]{2,1,0:T(8,128)(2,1)S(1)}, bf16[4,24,2304]{2,1,0:T(8,128)(2,1)S(1)}, u32[]{:S(2)}, u32[]{:S(2)}) %collective-permute-start.6) | collective-permute-done | bytes 442400 | tf_op jit(solution)/shard_map/ppermute | solution.py:24
  24.5 0.1 broadcast_select_fusion.1
  24.7 0.0 copy-done.1
  24.7 0.7 %fusion.41 = (f32[48]{0:T(128)S(1)}, f32[48,176]{1,0:T(8,128)S(1)}) fusion(bf16[176,4096]{1,0:T(8,128)(2,1)S(1)} %copy-done.1, bf16[48,1024]{1,0:T(8,128)(2,1)S(1)} %get-tuple-element.15, bf16[48,1024]{1,0:T(8,128)(2,1)S(1)} %get-tuple-element.16, bf16[48,1024]{1,0:T(8,128)(2,1)S(1)} %get-tuple-element.14, bf16[48,1024]{1,0:T(8,128)(2,1)S(1)} %get-tuple-element.13), kind=kOutput, calls=%fused_computation.107 | convolution fusion | flops 70787280 | bytes 1868992 | tf_op jit(solution)/shard_map/dot_general | solution.py:69
  25.4 0.0 copy-done
  25.4 0.8 %fusion.40 = (f32[48]{0:T(128)S(1)}, f32[48,176]{1,0:T(8,128)S(1)}) fusion(bf16[176,5120]{1,0:T(8,128)(2,1)S(1)} %copy-done, bf16[48,1280]{1,0:T(8,128)(2,1)S(1)} %get-tuple-element.12, bf16[48,1280]{1,0:T(8,128)(2,1)S(1)} %get-tuple-element.11, bf16[48,1280]{1,0:T(8,128)(2,1)S(1)} %get-tuple-element.10, bf16[48,1280]{1,0:T(8,128)(2,1)S(1)} %get-tuple-element.9), kind=kOutput, calls=%fused_computation.106 | convolution fusion | flops 88482000 | bytes 2327744 | tf_op jit(solution)/shard_map/dot_general | solution.py:66
  26.2 0.2 multiply_reduce_fusion
  26.4 0.1 reshape.36
  26.6 9.0 %all_to_all.5 = f32[32,1,240]{2,1,0:T(1,128)S(1)} all-to-all(f32[32,1,240]{2,1,0:T(1,128)S(1)} %reshape.36), channel_id=1, replica_groups=mesh['dp'=8,'vocab'=4] {'dp','vocab'}, dimensions={0} | all-to-all | bytes 61440 | tf_op jit(solution)/shard_map/all_to_all | solution.py:80
  35.6 0.5 broadcast.5
  36.1 0.7 %reduce.2 = f32[32,240]{1,0:T(8,128)S(1)} reduce(f32[32,1,240]{2,1,0:T(1,128)S(1)} %all_to_all.5, f32[]{:T(128)} %broadcast.5), dimensions={1}, to_apply=%all_to_all.3.reduce_sub_computation | reduce | bytes 61444 | tf_op jit(solution)/shard_map/all_to_all | solution.py:80
  36.8 0.1 reshape.37
  36.9 0.1 fusion.39
  37.1 0.1 multiply_convert_fusion
  37.2 0.3 convolution_convert_fusion.1
  37.5 0.1 collective-permute-start.7
  37.6 1.5 %collective-permute-done.7 = bf16[24,5120]{1,0:T(8,128)(2,1)S(1)} collective-permute-done((bf16[24,5120]{1,0:T(8,128)(2,1)S(1)}, bf16[24,5120]{1,0:T(8,128)(2,1)S(1)}, u32[]{:S(2)}, u32[]{:S(2)}) %collective-permute-start.7) | collective-permute-done | bytes 245792 | tf_op jit(solution)/shard_map/ppermute | solution.py:24
  39.1 0.4 convert_add_fusion
  39.5 0.6 %collective-permute-start.8 = (bf16[24,1280]{1,0:T(8,128)(2,1)S(1)}, bf16[24,1280]{1,0:T(8,128)(2,1)S(1)}, u32[]{:S(2)}, u32[]{:S(2)}) collective-permute-start(bf16[24,1280]{1,0:T(8,128)(2,1)S(1)} %get-tuple-element.19), channel_id=1, source_target_pairs={{0,1},{1,0},{2,3},{3,2},{4,5},{5,4},{6,7},{7,6},{8,9},{9,8},{10,11... | collective-permute-start | bytes 184328 | tf_op jit(solution)/shard_map/ppermute | solution.py:24
  40.0 0.7 %collective-permute-start.9 = (bf16[24,1280]{1,0:T(8,128)(2,1)S(1)}, bf16[24,1280]{1,0:T(8,128)(2,1)S(1)}, u32[]{:S(2)}, u32[]{:S(2)}) collective-permute-start(bf16[24,1280]{1,0:T(8,128)(2,1)S(1)} %get-tuple-element.20), channel_id=1, source_target_pairs={{0,2},{1,3},{2,0},{3,1},{4,6},{5,7},{6,4},{7,5},{8,10},{9,11},{10,... | collective-permute-start | bytes 184328 | tf_op jit(solution)/shard_map/ppermute | solution.py:24
  40.7 2.3 %collective-permute-start.10 = (bf16[24,1280]{1,0:T(8,128)(2,1)S(1)}, bf16[24,1280]{1,0:T(8,128)(2,1)S(1)}, u32[]{:S(2)}, u32[]{:S(2)}) collective-permute-start(bf16[24,1280]{1,0:T(8,128)(2,1)S(1)} %get-tuple-element.21), channel_id=1, source_target_pairs={{0,3},{1,2},{2,1},{3,0},{4,7},{5,6},{6,5},{7,4},{8,11},{9,10},{10,... | collective-permute-start | bytes 184328 | tf_op jit(solution)/shard_map/ppermute | solution.py:24
  43.0 0.9 %collective-permute-done.8 = bf16[24,1280]{1,0:T(8,128)(2,1)S(1)} collective-permute-done((bf16[24,1280]{1,0:T(8,128)(2,1)S(1)}, bf16[24,1280]{1,0:T(8,128)(2,1)S(1)}, u32[]{:S(2)}, u32[]{:S(2)}) %collective-permute-start.8) | collective-permute-done | bytes 61472 | tf_op jit(solution)/shard_map/ppermute | solution.py:24
  43.9 1.0 %collective-permute-done.9 = bf16[24,1280]{1,0:T(8,128)(2,1)S(1)} collective-permute-done((bf16[24,1280]{1,0:T(8,128)(2,1)S(1)}, bf16[24,1280]{1,0:T(8,128)(2,1)S(1)}, u32[]{:S(2)}, u32[]{:S(2)}) %collective-permute-start.9) | collective-permute-done | bytes 61472 | tf_op jit(solution)/shard_map/ppermute | solution.py:24
  44.9 0.9 %collective-permute-done.10 = bf16[24,1280]{1,0:T(8,128)(2,1)S(1)} collective-permute-done((bf16[24,1280]{1,0:T(8,128)(2,1)S(1)}, bf16[24,1280]{1,0:T(8,128)(2,1)S(1)}, u32[]{:S(2)}, u32[]{:S(2)}) %collective-permute-start.10) | collective-permute-done | bytes 61472 | tf_op jit(solution)/shard_map/ppermute | solution.py:24
  45.8 0.1 convert_add_fusion.1
  45.9 0.7 %collective-permute-start.11 = (bf16[6,1280]{1,0:T(8,128)(2,1)S(1)}, bf16[6,1280]{1,0:T(8,128)(2,1)S(1)}, u32[]{:S(2)}, u32[]{:S(2)}) collective-permute-start(bf16[6,1280]{1,0:T(8,128)(2,1)S(1)} %get-tuple-element.35), channel_id=1, source_target_pairs={{0,8},{4,12},{8,0},{12,4},{16,24},{20,28},{24,16},{28,20},{1,9},{5... | collective-permute-start | bytes 46088 | tf_op jit(solution)/shard_map/ppermute | solution.py:24
  46.6 0.5 collective-permute-start.12
  47.0 3.3 %collective-permute-start.13 = (bf16[6,1280]{1,0:T(8,128)(2,1)S(1)}, bf16[6,1280]{1,0:T(8,128)(2,1)S(1)}, u32[]{:S(2)}, u32[]{:S(2)}) collective-permute-start(bf16[6,1280]{1,0:T(8,128)(2,1)S(1)} %get-tuple-element.37), channel_id=1, source_target_pairs={{0,24},{4,28},{8,16},{12,20},{16,8},{20,12},{24,0},{28,4},{1,25},{... | collective-permute-start | bytes 46088 | tf_op jit(solution)/shard_map/ppermute | solution.py:24
  50.4 1.9 %convolution_convert_fusion = bf16[176,5120]{1,0:T(8,128)(2,1)} fusion(bf16[48,176]{1,0:T(8,128)(2,1)S(1)} %multiply_convert_fusion, bf16[48,1280]{1,0:T(8,128)(2,1)S(1)} %get-tuple-element.12, bf16[48,1280]{1,0:T(8,128)(2,1)S(1)} %get-tuple-element.11, bf16[48,1280]{1,0:T(8,128)(2,1)S(1)} %get-tuple-element.10, bf16[48,1280]{1,0:T(8,128)(2,1)S(1)} %get-tuple-element.9), kind=kOutput, calls=%fused_computation | convolution fusion | flops 89374720 | bytes 2310656 | tf_op jit(solution)/shard_map/dot_general | solution.py:109
  52.2 0.0 collective-permute-done.11
  52.2 0.0 collective-permute-done.12
  52.2 0.4 collective-permute-done.13
  52.6 0.6 %add_convert_fusion = bf16[6,1280]{1,0:T(8,128)(2,1)} fusion(bf16[6,1280]{1,0:T(8,128)(2,1)S(1)} %collective-permute-done.13, bf16[6,1280]{1,0:T(8,128)(2,1)S(1)} %collective-permute-done.12, bf16[6,1280]{1,0:T(8,128)(2,1)S(1)} %collective-permute-done.11, pred[]{:T(512)S(6)} %eq.20, f32[24,1280]{1,0:T(8,128)S(1)} %convert_add_fusion.1, pred[]{:T(512)S(6)} %eq.21), kind=kLoop, calls=%fused_computation.68 | loop fusion | flops 76800 | bytes 184322 | tf_op jit(solution)/shard_map/convert_element_type | solution.py:107
  (11 shorter events, 0.3 us)
Async XLA Ops:
  0.6 24.7 %copy-start = (bf16[176,5120]{1,0:T(8,128)(2,1)S(1)}, bf16[176,5120]{1,0:T(8,128)(2,1)}, u32[]{:S(2)}) copy-start(bf16[176,5120]{1,0:T(8,128)(2,1)} %param.6) | copy-start | bytes 5406724
  2.2 5.6 %collective-permute-start.2 = (bf16[6,2304]{1,0:T(8,128)(2,1)S(1)}, bf16[6,2304]{1,0:T(8,128)(2,1)S(1)}, u32[]{:S(2)}, u32[]{:S(2)}) collective-permute-start(bf16[6,2304]{1,0:T(8,128)(2,1)S(1)} %constant_dynamic-update-slice_fusion), channel_id=1, source_target_pairs={{0,8},{4,12},{8,0},{12,4},{16,24},{20,28},{24,16},{28,20},{1,9},{5... | collective-permute-start | bytes 82952 | tf_op jit(solution)/shard_map/ppermute | solution.py:24
  5.2 5.5 %collective-permute-start.1 = (bf16[6,2304]{1,0:T(8,128)(2,1)S(1)}, bf16[6,2304]{1,0:T(8,128)(2,1)S(1)}, u32[]{:S(2)}, u32[]{:S(2)}) collective-permute-start(bf16[6,2304]{1,0:T(8,128)(2,1)S(1)} %constant_dynamic-update-slice_fusion), channel_id=1, source_target_pairs={{0,16},{4,20},{8,24},{12,28},{16,0},{20,4},{24,8},{28,12},{1,17},{... | collective-permute-start | bytes 82952 | tf_op jit(solution)/shard_map/ppermute | solution.py:24
  7.8 5.8 %collective-permute-start = (bf16[6,2304]{1,0:T(8,128)(2,1)S(1)}, bf16[6,2304]{1,0:T(8,128)(2,1)S(1)}, u32[]{:S(2)}, u32[]{:S(2)}) collective-permute-start(bf16[6,2304]{1,0:T(8,128)(2,1)S(1)} %constant_dynamic-update-slice_fusion), channel_id=1, source_target_pairs={{0,24},{4,28},{8,16},{12,20},{16,8},{20,12},{24,0},{28,4},{1,25},{... | collective-permute-start | bytes 82952 | tf_op jit(solution)/shard_map/ppermute | solution.py:24
  13.7 5.7 %collective-permute-start.5 = (bf16[1,24,2304]{2,1,0:T(8,128)(2,1)S(1)}, bf16[1,24,2304]{2,1,0:T(8,128)(2,1)S(1)}, u32[]{:S(2)}, u32[]{:S(2)}) collective-permute-start(bf16[1,24,2304]{2,1,0:T(8,128)(2,1)S(1)} %maximum_bitcast_fusion), channel_id=1, source_target_pairs={{0,1},{1,0},{2,3},{3,2},{4,5},{5,4},{6,7},{7,6},{8,9},{9,8},{10,11... | collective-permute-start | bytes 331784 | tf_op jit(solution)/shard_map/ppermute | solution.py:24
  15.2 5.3 %collective-permute-start.4 = (bf16[1,24,2304]{2,1,0:T(8,128)(2,1)S(1)}, bf16[1,24,2304]{2,1,0:T(8,128)(2,1)S(1)}, u32[]{:S(2)}, u32[]{:S(2)}) collective-permute-start(bf16[1,24,2304]{2,1,0:T(8,128)(2,1)S(1)} %maximum_bitcast_fusion), channel_id=1, source_target_pairs={{0,2},{1,3},{2,0},{3,1},{4,6},{5,7},{6,4},{7,5},{8,10},{9,11},{10,... | collective-permute-start | bytes 331784 | tf_op jit(solution)/shard_map/ppermute | solution.py:24
  16.8 5.6 %collective-permute-start.3 = (bf16[1,24,2304]{2,1,0:T(8,128)(2,1)S(1)}, bf16[1,24,2304]{2,1,0:T(8,128)(2,1)S(1)}, u32[]{:S(2)}, u32[]{:S(2)}) collective-permute-start(bf16[1,24,2304]{2,1,0:T(8,128)(2,1)S(1)} %maximum_bitcast_fusion), channel_id=1, source_target_pairs={{0,3},{1,2},{2,1},{3,0},{4,7},{5,6},{6,5},{7,4},{8,11},{9,10},{10,... | collective-permute-start | bytes 331784 | tf_op jit(solution)/shard_map/ppermute | solution.py:24
  22.6 1.9 %collective-permute-start.6 = (bf16[4,24,2304]{2,1,0:T(8,128)(2,1)S(1)}, bf16[4,24,2304]{2,1,0:T(8,128)(2,1)S(1)}, u32[]{:S(2)}, u32[]{:S(2)}) collective-permute-start(bf16[4,24,2304]{2,1,0:T(8,128)(2,1)S(1)} %pad_maximum_fusion.1), channel_id=1, source_target_pairs={{0,4},{4,0},{8,12},{12,8},{16,20},{20,16},{24,28},{28,24},{1,5},{5... | collective-permute-start | bytes 1327112 | tf_op jit(solution)/shard_map/ppermute | solution.py:24
  22.7 2.0 %copy-start.1 = (bf16[176,4096]{1,0:T(8,128)(2,1)S(1)}, bf16[176,4096]{1,0:T(8,128)(2,1)}, u32[]{:S(2)}) copy-start(bf16[176,4096]{1,0:T(8,128)(2,1)} %param.7) | copy-start | bytes 4325380
  37.5 1.6 %collective-permute-start.7 = (bf16[24,5120]{1,0:T(8,128)(2,1)S(1)}, bf16[24,5120]{1,0:T(8,128)(2,1)S(1)}, u32[]{:S(2)}, u32[]{:S(2)}) collective-permute-start(bf16[24,5120]{1,0:T(8,128)(2,1)S(1)} %convolution_convert_fusion.1), channel_id=1, source_target_pairs={{0,4},{4,0},{8,12},{12,8},{16,20},{20,16},{24,28},{28,24},{1,5},{5... | collective-permute-start | bytes 737288 | tf_op jit(solution)/shard_map/ppermute | solution.py:24
  39.5 4.4 %collective-permute-start.8 = (bf16[24,1280]{1,0:T(8,128)(2,1)S(1)}, bf16[24,1280]{1,0:T(8,128)(2,1)S(1)}, u32[]{:S(2)}, u32[]{:S(2)}) collective-permute-start(bf16[24,1280]{1,0:T(8,128)(2,1)S(1)} %get-tuple-element.19), channel_id=1, source_target_pairs={{0,1},{1,0},{2,3},{3,2},{4,5},{5,4},{6,7},{7,6},{8,9},{9,8},{10,11... | collective-permute-start | bytes 184328 | tf_op jit(solution)/shard_map/ppermute | solution.py:24
  40.0 4.9 %collective-permute-start.9 = (bf16[24,1280]{1,0:T(8,128)(2,1)S(1)}, bf16[24,1280]{1,0:T(8,128)(2,1)S(1)}, u32[]{:S(2)}, u32[]{:S(2)}) collective-permute-start(bf16[24,1280]{1,0:T(8,128)(2,1)S(1)} %get-tuple-element.20), channel_id=1, source_target_pairs={{0,2},{1,3},{2,0},{3,1},{4,6},{5,7},{6,4},{7,5},{8,10},{9,11},{10,... | collective-permute-start | bytes 184328 | tf_op jit(solution)/shard_map/ppermute | solution.py:24
  40.7 5.1 %collective-permute-start.10 = (bf16[24,1280]{1,0:T(8,128)(2,1)S(1)}, bf16[24,1280]{1,0:T(8,128)(2,1)S(1)}, u32[]{:S(2)}, u32[]{:S(2)}) collective-permute-start(bf16[24,1280]{1,0:T(8,128)(2,1)S(1)} %get-tuple-element.21), channel_id=1, source_target_pairs={{0,3},{1,2},{2,1},{3,0},{4,7},{5,6},{6,5},{7,4},{8,11},{9,10},{10,... | collective-permute-start | bytes 184328 | tf_op jit(solution)/shard_map/ppermute | solution.py:24
  45.9 6.3 %collective-permute-start.11 = (bf16[6,1280]{1,0:T(8,128)(2,1)S(1)}, bf16[6,1280]{1,0:T(8,128)(2,1)S(1)}, u32[]{:S(2)}, u32[]{:S(2)}) collective-permute-start(bf16[6,1280]{1,0:T(8,128)(2,1)S(1)} %get-tuple-element.35), channel_id=1, source_target_pairs={{0,8},{4,12},{8,0},{12,4},{16,24},{20,28},{24,16},{28,20},{1,9},{5... | collective-permute-start | bytes 46088 | tf_op jit(solution)/shard_map/ppermute | solution.py:24
  46.6 5.7 %collective-permute-start.12 = (bf16[6,1280]{1,0:T(8,128)(2,1)S(1)}, bf16[6,1280]{1,0:T(8,128)(2,1)S(1)}, u32[]{:S(2)}, u32[]{:S(2)}) collective-permute-start(bf16[6,1280]{1,0:T(8,128)(2,1)S(1)} %get-tuple-element.36), channel_id=1, source_target_pairs={{0,16},{4,20},{8,24},{12,28},{16,0},{20,4},{24,8},{28,12},{1,17},{... | collective-permute-start | bytes 46088 | tf_op jit(solution)/shard_map/ppermute | solution.py:24
  47.0 5.6 %collective-permute-start.13 = (bf16[6,1280]{1,0:T(8,128)(2,1)S(1)}, bf16[6,1280]{1,0:T(8,128)(2,1)S(1)}, u32[]{:S(2)}, u32[]{:S(2)}) collective-permute-start(bf16[6,1280]{1,0:T(8,128)(2,1)S(1)} %get-tuple-element.37), channel_id=1, source_target_pairs={{0,24},{4,28},{8,16},{12,20},{16,8},{20,12},{24,0},{28,4},{1,25},{... | collective-permute-start | bytes 46088 | tf_op jit(solution)/shard_map/ppermute | solution.py:24

commit v3 on v2

--- a/solution.py
+++ b/solution.py
@@ -34,20 +34,6 @@
     return value
 
 
-def scattered(total, axis, size, bits, dim):
-    index = lax.axis_index(axis)
-    for group in reversed(grouped(bits)):
-        parts = reorder(jnp.split(total, 1 << len(group), axis=dim), index, group)
-        total = parts[0]
-        landed = [
-            swap(parts[j].astype(jnp.bfloat16), axis, size, mask_of(j, group))
-            for j in range(1, 1 << len(group))
-        ]
-        for part in landed:
-            total = total + part.astype(jnp.float32)
-    return total
-
-
 def build(dp, vocab):
     dp_bits = range(dp.bit_length() - 1)
     vocab_bits = range(vocab.bit_length() - 1)
@@ -55,9 +41,12 @@
 
     def on_device(student_hidden, teacher_hidden, student_head, teacher_head):
         rows, share = student_hidden.shape
-        packed = jnp.concatenate([student_hidden, teacher_hidden], axis=1)
+        teacher_share = teacher_hidden.shape[1]
+        tokens = rows * dp
+        packed = jnp.concatenate([student_hidden, teacher_hidden], axis=1)[None]
         by_z = gathered(packed, "dp", dp, z_bits, 0)
-        by_vocab = gathered(by_z[None], "vocab", vocab, vocab_bits, 0)
+        by_z = by_z.reshape(1, tokens // 2, share + teacher_share)
+        by_vocab = gathered(by_z, "vocab", vocab, vocab_bits, 0)
         whole = gathered(by_vocab, "dp", dp, core, 1)
         student_full = jnp.concatenate([whole[i, :, :share] for i in range(vocab)], axis=1)
         teacher_full = jnp.concatenate([whole[i, :, share:] for i in range(vocab)], axis=1)
@@ -76,11 +65,12 @@
         other_peak = jnp.max(teacher_logits, axis=1)
         other_total = jnp.sum(jnp.exp(teacher_logits - other_peak[:, None]), axis=1)
         stats = jnp.stack([peak, total, weighted, other_peak, other_total])
+        stats = jnp.pad(stats, ((0, 3), (0, -tokens % 128)))
         devices = dp * vocab
         every = lax.all_to_all(
             jnp.broadcast_to(stats[None], (devices,) + stats.shape),
             ("dp", "vocab"), 0, 0, tiled=True,
-        )
+        )[:, :, :tokens]
         top = jnp.max(every[:, 0], axis=0)
         scale = jnp.exp(every[:, 0] - top)
         total_all = jnp.sum(every[:, 1] * scale, axis=0)
@@ -102,9 +92,16 @@
         landed = swap(away, "dp", dp, 1)
         acc = jnp.dot(keep, student_head, preferred_element_type=jnp.float32)
         acc = acc + landed.astype(jnp.float32)
-        acc = scattered(acc, "vocab", vocab, vocab_bits, 1)
-        acc = scattered(acc, "dp", dp, z_bits, 0)
-        hidden_grad = acc.astype(jnp.bfloat16)
+        zs = dp // 2
+        blocks = acc.astype(jnp.bfloat16).reshape(zs, rows, vocab, share)
+        blocks = jnp.transpose(blocks, (0, 2, 1, 3)).reshape(zs * vocab, rows, share)
+        groups = [
+            [(z * 2 + c) * vocab + v for z in range(zs) for v in range(vocab)] for c in range(2)
+        ]
+        landed = lax.all_to_all(
+            blocks, ("dp", "vocab"), 0, 0, axis_index_groups=groups, tiled=True
+        )
+        hidden_grad = jnp.sum(landed.astype(jnp.float32), axis=0).astype(jnp.bfloat16)
 
         head_grad = lax.dot_general(
             logit_grad, student_full, (((0,), (0,)), ((), ())), preferred_element_type=jnp.float32

time: 53.5 us -> 56.5 us (1.056)
  waiting for transfers between devices: 17.4 us -> 24.2 us
  starting transfers between devices: 17.3 us -> 12.9 us
  local copies, waits for them, and re-layouts: 2.4 us -> 1.08 us
  blocking collectives: 8.99 us -> 10.1 us
  other arithmetic: 2.33 us -> 3.08 us
    all_to_all x0 -> x1, waiting for transfers between devices: none -> 9.98 us  [on_device(): lax.all_to_all(blocks, ('dp', 'vocab'), 0, 0, axis_index_groups=groups, t...]
    ppermute x14 -> x8, starting transfers between devices: 17.3 us -> 9.37 us  [swap(): return lax.ppermute(value, axis, [(i, i ^ mask) for i in range(size)])]
    all_to_all x0 -> x1, starting transfers between devices: none -> 3.54 us  [on_device(): lax.all_to_all(blocks, ('dp', 'vocab'), 0, 0, axis_index_groups=groups, t...]
    ppermute x14 -> x8, waiting for transfers between devices: 17.4 us -> 14.2 us  [swap(): return lax.ppermute(value, axis, [(i, i ^ mask) for i in range(size)])]
    all_to_all x1, blocking collectives: 8.99 us -> 10.1 us  [on_device(): lax.all_to_all(jnp.broadcast_to(stats[None], (devices,) + stats.shape), (...]
    unnamed x7 -> x4, local copies, waits for them, and re-layouts: 1.08 us -> 0.02 us
    reshape x0 -> x3, local copies, waits for them, and re-layouts: none -> 0.96 us  [the longest x1 0.74 us: on_device(): jnp.transpose(blocks, (0, 2, 1, 3)).reshape(zs * vocab, rows, share)]
    broadcast_in_dim x1, other arithmetic: 0.06 us -> 0.89 us  [on_device(): packed = jnp.concatenate([student_hidden, teacher_hidden], axis=1)[None]]
  transfers between devices with their start and end apart: 14 -> 9, of which waited for: 11 -> 8; matrix products, arithmetic and copies ran while one was open for 3% -> 3% of each run, Pallas kernels for 0% -> 0%
where the time goes in v3:
time: 56.5 us; the launch traced here: 56.2 us
  waiting for transfers between devices  24.2 us (43%)
  starting transfers between devices  12.9 us (23%)
  blocking collectives  10.1 us (18%)
  matrix products  4.04 us (7%)
  other arithmetic  3.08 us (5%)
  local copies, waits for them, and re-layouts  1.08 us (2%)
  between operations  0.79 us (1%)
    ppermute x8, waiting for transfers between devices, swap(): return lax.ppermute(value, axis, [(i, i ^ mask) for i in range(size)])  14.2 us
    all_to_all x1, blocking collectives, on_device(): lax.all_to_all(jnp.broadcast_to(stats[None], (devices,) + stats.shape), (...  10.1 us
    all_to_all x1, waiting for transfers between devices, on_device(): lax.all_to_all(blocks, ('dp', 'vocab'), 0, 0, axis_index_groups=groups, t...  9.98 us
    ppermute x8, starting transfers between devices, swap(): return lax.ppermute(value, axis, [(i, i ^ mask) for i in range(size)])  9.37 us
    all_to_all x1, starting transfers between devices, on_device(): lax.all_to_all(blocks, ('dp', 'vocab'), 0, 0, axis_index_groups=groups, t...  3.54 us
    dot_general x1, matrix products, on_device(): lax.dot_general(logit_grad, student_full, (((0,), (0,)), ((), ())), prefe...  1.86 us
  transfers between devices with their start and end apart: 9, of which 8 were waited for; matrix products, arithmetic and copies ran while one was open for 3% of the time, Pallas kernels for 0%

profile of v3, /device:TPU:0, one launch (start us, length us, event | category | flops | bytes accessed | tf_op | source)
XLA Modules:
  0.0 56.2 jit_solution(10435826430392047547)
XLA Ops:
  0.6 0.0 copy-start
  0.6 0.9 %maximum_bitcast_fusion = bf16[1,6,2304]{2,1,0:T(8,128)(2,1)S(1)} fusion(bf16[6,1024]{1,0:T(8,128)(2,1)} %param.5, bf16[6,1280]{1,0:T(8,128)(2,1)} %param.4), kind=kLoop, calls=%fused_computation.60 | loop fusion | flops 55296 | bytes 55296 | tf_op jit(solution)/shard_map/broadcast_in_dim | solution.py:46
  1.5 3.1 %collective-permute-start.2 = (bf16[1,6,2304]{2,1,0:T(8,128)(2,1)S(1)}, bf16[1,6,2304]{2,1,0:T(8,128)(2,1)S(1)}, u32[]{:S(2)}, u32[]{:S(2)}) collective-permute-start(bf16[1,6,2304]{2,1,0:T(8,128)(2,1)S(1)} %maximum_bitcast_fusion), channel_id=1, source_target_pairs={{0,8},{4,12},{8,0},{12,4},{16,24},{20,28},{24,16},{28,20},{1,9},{5... | collective-permute-start | bytes 82952 | tf_op jit(solution)/shard_map/ppermute | solution.py:24
  4.6 2.6 %collective-permute-start.1 = (bf16[1,6,2304]{2,1,0:T(8,128)(2,1)S(1)}, bf16[1,6,2304]{2,1,0:T(8,128)(2,1)S(1)}, u32[]{:S(2)}, u32[]{:S(2)}) collective-permute-start(bf16[1,6,2304]{2,1,0:T(8,128)(2,1)S(1)} %maximum_bitcast_fusion), channel_id=1, source_target_pairs={{0,16},{4,20},{8,24},{12,28},{16,0},{20,4},{24,8},{28,12},{1,17},{... | collective-permute-start | bytes 82952 | tf_op jit(solution)/shard_map/ppermute | solution.py:24
  7.2 0.0 collective-permute-start
  7.2 0.0 collective-permute-done.2
  7.2 2.9 %collective-permute-done.1 = bf16[1,6,2304]{2,1,0:T(8,128)(2,1)S(1)} collective-permute-done((bf16[1,6,2304]{2,1,0:T(8,128)(2,1)S(1)}, bf16[1,6,2304]{2,1,0:T(8,128)(2,1)S(1)}, u32[]{:S(2)}, u32[]{:S(2)}) %collective-permute-start.1) | collective-permute-done | bytes 27680 | tf_op jit(solution)/shard_map/ppermute | solution.py:24
  10.2 2.8 %collective-permute-done = bf16[1,6,2304]{2,1,0:T(8,128)(2,1)S(1)} collective-permute-done((bf16[1,6,2304]{2,1,0:T(8,128)(2,1)S(1)}, bf16[1,6,2304]{2,1,0:T(8,128)(2,1)S(1)}, u32[]{:S(2)}, u32[]{:S(2)}) %collective-permute-start) | collective-permute-done | bytes 27680 | tf_op jit(solution)/shard_map/ppermute | solution.py:24
  13.0 0.8 %broadcast_select_fusion.17 = (bf16[1,6,2304]{2,1,0:T(8,128)(2,1)S(1)}, bf16[1,6,2304]{2,1,0:T(8,128)(2,1)S(1)}, bf16[1,6,2304]{2,1,0:T(8,128)(2,1)S(1)}, bf16[1,6,2304]{2,1,0:T(8,128)(2,1)S(1)}) fusion(pred[]{:T(512)S(6)} %eq.19, bf16[1,6,2304]{2,1,0:T(8,128)(2,1)S(1)} %collective-permute-done, bf16[1,6,2304]{2,1,0:T(8,128)(2,1)S(1)} %collective-permute-done.1, ...), kind=kLoop, calls=%fused_computation.68 | loop fusion | flops 165888 | bytes 221186 | tf_op jit(solution)/shard_map/jit(_where)/select_n | solution.py:19
  13.9 1.6 %collective-permute-start.5 = (bf16[1,24,2304]{2,1,0:T(8,128)(2,1)S(1)}, bf16[1,24,2304]{2,1,0:T(8,128)(2,1)S(1)}, u32[]{:S(2)}, u32[]{:S(2)}) collective-permute-start(bf16[1,24,2304]{2,1,0:T(8,128)(2,1)S(1)} %reshape.45), channel_id=1, source_target_pairs={{0,1},{1,0},{2,3},{3,2},{4,5},{5,4},{6,7},{7,6},{8,9},{9,8},{10,11... | collective-permute-start | bytes 331784 | tf_op jit(solution)/shard_map/ppermute | solution.py:24
  15.4 1.5 %collective-permute-start.4 = (bf16[1,24,2304]{2,1,0:T(8,128)(2,1)S(1)}, bf16[1,24,2304]{2,1,0:T(8,128)(2,1)S(1)}, u32[]{:S(2)}, u32[]{:S(2)}) collective-permute-start(bf16[1,24,2304]{2,1,0:T(8,128)(2,1)S(1)} %reshape.45), channel_id=1, source_target_pairs={{0,2},{1,3},{2,0},{3,1},{4,6},{5,7},{6,4},{7,5},{8,10},{9,11},{10,... | collective-permute-start | bytes 331784 | tf_op jit(solution)/shard_map/ppermute | solution.py:24
  16.9 0.5 collective-permute-start.3
  17.4 2.1 %collective-permute-done.5 = bf16[1,24,2304]{2,1,0:T(8,128)(2,1)S(1)} collective-permute-done((bf16[1,24,2304]{2,1,0:T(8,128)(2,1)S(1)}, bf16[1,24,2304]{2,1,0:T(8,128)(2,1)S(1)}, u32[]{:S(2)}, u32[]{:S(2)}) %collective-permute-start.5) | collective-permute-done | bytes 110624 | tf_op jit(solution)/shard_map/ppermute | solution.py:24
  19.5 1.2 %collective-permute-done.4 = bf16[1,24,2304]{2,1,0:T(8,128)(2,1)S(1)} collective-permute-done((bf16[1,24,2304]{2,1,0:T(8,128)(2,1)S(1)}, bf16[1,24,2304]{2,1,0:T(8,128)(2,1)S(1)}, u32[]{:S(2)}, u32[]{:S(2)}) %collective-permute-start.4) | collective-permute-done | bytes 110624 | tf_op jit(solution)/shard_map/ppermute | solution.py:24
  20.7 1.8 %collective-permute-done.3 = bf16[1,24,2304]{2,1,0:T(8,128)(2,1)S(1)} collective-permute-done((bf16[1,24,2304]{2,1,0:T(8,128)(2,1)S(1)}, bf16[1,24,2304]{2,1,0:T(8,128)(2,1)S(1)}, u32[]{:S(2)}, u32[]{:S(2)}) %collective-permute-start.3) | collective-permute-done | bytes 110624 | tf_op jit(solution)/shard_map/ppermute | solution.py:24
  22.6 0.1 broadcast_select_fusion.9
  22.6 0.1 pad_maximum_fusion.1
  22.7 0.1 collective-permute-start.6
  22.8 0.0 copy-start.1
  22.8 1.8 %collective-permute-done.6 = bf16[4,24,2304]{2,1,0:T(8,128)(2,1)S(1)} collective-permute-done((bf16[4,24,2304]{2,1,0:T(8,128)(2,1)S(1)}, bf16[4,24,2304]{2,1,0:T(8,128)(2,1)S(1)}, u32[]{:S(2)}, u32[]{:S(2)}) %collective-permute-start.6) | collective-permute-done | bytes 442400 | tf_op jit(solution)/shard_map/ppermute | solution.py:24
  24.6 0.1 broadcast_select_fusion.1
  24.7 0.0 copy-done.1
  24.8 0.7 %fusion.41 = (f32[48]{0:T(128)S(1)}, f32[48,176]{1,0:T(8,128)S(1)}) fusion(bf16[176,4096]{1,0:T(8,128)(2,1)S(1)} %copy-done.1, bf16[48,1024]{1,0:T(8,128)(2,1)S(1)} %get-tuple-element.15, bf16[48,1024]{1,0:T(8,128)(2,1)S(1)} %get-tuple-element.16, bf16[48,1024]{1,0:T(8,128)(2,1)S(1)} %get-tuple-element.14, bf16[48,1024]{1,0:T(8,128)(2,1)S(1)} %get-tuple-element.13), kind=kOutput, calls=%fused_computation.90 | convolution fusion | flops 70787280 | bytes 1868992 | tf_op jit(solution)/shard_map/dot_general | solution.py:58
  25.4 0.0 copy-done
  25.4 0.8 %fusion.40 = (f32[48]{0:T(128)S(1)}, f32[48,176]{1,0:T(8,128)S(1)}) fusion(bf16[176,5120]{1,0:T(8,128)(2,1)S(1)} %copy-done, bf16[48,1280]{1,0:T(8,128)(2,1)S(1)} %get-tuple-element.12, bf16[48,1280]{1,0:T(8,128)(2,1)S(1)} %get-tuple-element.11, bf16[48,1280]{1,0:T(8,128)(2,1)S(1)} %get-tuple-element.10, bf16[48,1280]{1,0:T(8,128)(2,1)S(1)} %get-tuple-element.9), kind=kOutput, calls=%fused_computation.89 | convolution fusion | flops 88482000 | bytes 2327744 | tf_op jit(solution)/shard_map/dot_general | solution.py:55
  26.2 0.2 multiply_reduce_fusion
  26.5 10.1 %all_to_all.10 = f32[32,8,128]{2,1,0:T(8,128)S(1)} all-to-all(f32[32,8,128]{2,1,0:T(8,128)S(1)} %broadcast_in_dim.5), channel_id=1, replica_groups=mesh['dp'=8,'vocab'=4] {'dp','vocab'}, dimensions={0} | all-to-all | bytes 262144 | tf_op jit(solution)/shard_map/all_to_all | solution.py:70
  36.6 0.1 fusion.39
  36.8 0.1 multiply_convert_fusion
  36.9 0.3 convolution_convert_fusion.1
  37.2 0.1 collective-permute-start.7
  37.3 1.5 %collective-permute-done.7 = bf16[24,5120]{1,0:T(8,128)(2,1)S(1)} collective-permute-done((bf16[24,5120]{1,0:T(8,128)(2,1)S(1)}, bf16[24,5120]{1,0:T(8,128)(2,1)S(1)}, u32[]{:S(2)}, u32[]{:S(2)}) %collective-permute-start.7) | collective-permute-done | bytes 245792 | tf_op jit(solution)/shard_map/ppermute | solution.py:24
  38.8 0.4 add_convert_fusion
  39.2 0.2 reshape.46
  39.4 0.7 %copy.25 = bf16[4,4,6,1280]{3,2,1,0:T(8,128)(2,1)} copy(bf16[4,4,6,1280]{3,1,2,0:T(4,128)(2,1)S(1)} %bitcast.50) | data formatting | bytes 491520 | tf_op jit(solution)/shard_map/reshape | solution.py:97
  40.1 3.5 %all-to-all-start.1 = ((bf16[16,6,1280]{2,1,0:T(8,128)(2,1)}), bf16[16,6,1280]{2,1,0:T(8,128)(2,1)S(1)}, u32[]{:S(2)}, u32[]{:S(2)}) async-start(bf16[16,6,1280]{2,1,0:T(8,128)(2,1)} %bitcast.20), calls=%async_computation.1 | async-start | bytes 655360 | tf_op jit(solution)/shard_map/all_to_all | solution.py:101
  43.6 1.9 %convolution_convert_fusion = bf16[176,5120]{1,0:T(8,128)(2,1)} fusion(bf16[48,176]{1,0:T(8,128)(2,1)S(1)} %multiply_convert_fusion, bf16[48,1280]{1,0:T(8,128)(2,1)S(1)} %get-tuple-element.12, bf16[48,1280]{1,0:T(8,128)(2,1)S(1)} %get-tuple-element.11, bf16[48,1280]{1,0:T(8,128)(2,1)S(1)} %get-tuple-element.10, bf16[48,1280]{1,0:T(8,128)(2,1)S(1)} %get-tuple-element.9), kind=kOutput, calls=%fused_computation | convolution fusion | flops 89374720 | bytes 2310656 | tf_op jit(solution)/shard_map/dot_general | solution.py:106
  45.5 10.0 %all-to-all-done.1 = bf16[16,6,1280]{2,1,0:T(8,128)(2,1)S(1)} async-done(((bf16[16,6,1280]{2,1,0:T(8,128)(2,1)}), bf16[16,6,1280]{2,1,0:T(8,128)(2,1)S(1)}, u32[]{:S(2)}, u32[]{:S(2)}) %all-to-all-start.1) | async-done | bytes 245792 | tf_op jit(solution)/shard_map/all_to_all | solution.py:101
  55.5 0.7 %reduce_sum.72 = bf16[6,1280]{1,0:T(8,128)(2,1)} reduce(bf16[16,6,1280]{2,1,0:T(8,128)(2,1)S(1)} %all-to-all-done.1, bf16[]{:T(256)} %constant.21.clone.1), dimensions={0}, to_apply=%region_10.11 | reduce | flops 115200 | bytes 261122 | tf_op jit(solution)/shard_map/reduce_sum | solution.py:104
  (11 shorter events, 0.3 us)
Async XLA Ops:
  0.6 24.8 %copy-start = (bf16[176,5120]{1,0:T(8,128)(2,1)S(1)}, bf16[176,5120]{1,0:T(8,128)(2,1)}, u32[]{:S(2)}) copy-start(bf16[176,5120]{1,0:T(8,128)(2,1)} %param.6) | copy-start | bytes 5406724
  1.5 5.7 %collective-permute-start.2 = (bf16[1,6,2304]{2,1,0:T(8,128)(2,1)S(1)}, bf16[1,6,2304]{2,1,0:T(8,128)(2,1)S(1)}, u32[]{:S(2)}, u32[]{:S(2)}) collective-permute-start(bf16[1,6,2304]{2,1,0:T(8,128)(2,1)S(1)} %maximum_bitcast_fusion), channel_id=1, source_target_pairs={{0,8},{4,12},{8,0},{12,4},{16,24},{20,28},{24,16},{28,20},{1,9},{5... | collective-permute-start | bytes 82952 | tf_op jit(solution)/shard_map/ppermute | solution.py:24
  4.6 5.5 %collective-permute-start.1 = (bf16[1,6,2304]{2,1,0:T(8,128)(2,1)S(1)}, bf16[1,6,2304]{2,1,0:T(8,128)(2,1)S(1)}, u32[]{:S(2)}, u32[]{:S(2)}) collective-permute-start(bf16[1,6,2304]{2,1,0:T(8,128)(2,1)S(1)} %maximum_bitcast_fusion), channel_id=1, source_target_pairs={{0,16},{4,20},{8,24},{12,28},{16,0},{20,4},{24,8},{28,12},{1,17},{... | collective-permute-start | bytes 82952 | tf_op jit(solution)/shard_map/ppermute | solution.py:24
  7.2 5.8 %collective-permute-start = (bf16[1,6,2304]{2,1,0:T(8,128)(2,1)S(1)}, bf16[1,6,2304]{2,1,0:T(8,128)(2,1)S(1)}, u32[]{:S(2)}, u32[]{:S(2)}) collective-permute-start(bf16[1,6,2304]{2,1,0:T(8,128)(2,1)S(1)} %maximum_bitcast_fusion), channel_id=1, source_target_pairs={{0,24},{4,28},{8,16},{12,20},{16,8},{20,12},{24,0},{28,4},{1,25},{... | collective-permute-start | bytes 82952 | tf_op jit(solution)/shard_map/ppermute | solution.py:24
  13.9 5.7 %collective-permute-start.5 = (bf16[1,24,2304]{2,1,0:T(8,128)(2,1)S(1)}, bf16[1,24,2304]{2,1,0:T(8,128)(2,1)S(1)}, u32[]{:S(2)}, u32[]{:S(2)}) collective-permute-start(bf16[1,24,2304]{2,1,0:T(8,128)(2,1)S(1)} %reshape.45), channel_id=1, source_target_pairs={{0,1},{1,0},{2,3},{3,2},{4,5},{5,4},{6,7},{7,6},{8,9},{9,8},{10,11... | collective-permute-start | bytes 331784 | tf_op jit(solution)/shard_map/ppermute | solution.py:24
  15.4 5.3 %collective-permute-start.4 = (bf16[1,24,2304]{2,1,0:T(8,128)(2,1)S(1)}, bf16[1,24,2304]{2,1,0:T(8,128)(2,1)S(1)}, u32[]{:S(2)}, u32[]{:S(2)}) collective-permute-start(bf16[1,24,2304]{2,1,0:T(8,128)(2,1)S(1)} %reshape.45), channel_id=1, source_target_pairs={{0,2},{1,3},{2,0},{3,1},{4,6},{5,7},{6,4},{7,5},{8,10},{9,11},{10,... | collective-permute-start | bytes 331784 | tf_op jit(solution)/shard_map/ppermute | solution.py:24
  16.9 5.6 %collective-permute-start.3 = (bf16[1,24,2304]{2,1,0:T(8,128)(2,1)S(1)}, bf16[1,24,2304]{2,1,0:T(8,128)(2,1)S(1)}, u32[]{:S(2)}, u32[]{:S(2)}) collective-permute-start(bf16[1,24,2304]{2,1,0:T(8,128)(2,1)S(1)} %reshape.45), channel_id=1, source_target_pairs={{0,3},{1,2},{2,1},{3,0},{4,7},{5,6},{6,5},{7,4},{8,11},{9,10},{10,... | collective-permute-start | bytes 331784 | tf_op jit(solution)/shard_map/ppermute | solution.py:24
  22.7 1.9 %collective-permute-start.6 = (bf16[4,24,2304]{2,1,0:T(8,128)(2,1)S(1)}, bf16[4,24,2304]{2,1,0:T(8,128)(2,1)S(1)}, u32[]{:S(2)}, u32[]{:S(2)}) collective-permute-start(bf16[4,24,2304]{2,1,0:T(8,128)(2,1)S(1)} %pad_maximum_fusion.1), channel_id=1, source_target_pairs={{0,4},{4,0},{8,12},{12,8},{16,20},{20,16},{24,28},{28,24},{1,5},{5... | collective-permute-start | bytes 1327112 | tf_op jit(solution)/shard_map/ppermute | solution.py:24
  22.8 2.0 %copy-start.1 = (bf16[176,4096]{1,0:T(8,128)(2,1)S(1)}, bf16[176,4096]{1,0:T(8,128)(2,1)}, u32[]{:S(2)}) copy-start(bf16[176,4096]{1,0:T(8,128)(2,1)} %param.7) | copy-start | bytes 4325380
  37.2 1.6 %collective-permute-start.7 = (bf16[24,5120]{1,0:T(8,128)(2,1)S(1)}, bf16[24,5120]{1,0:T(8,128)(2,1)S(1)}, u32[]{:S(2)}, u32[]{:S(2)}) collective-permute-start(bf16[24,5120]{1,0:T(8,128)(2,1)S(1)} %convolution_convert_fusion.1), channel_id=1, source_target_pairs={{0,4},{4,0},{8,12},{12,8},{16,20},{20,16},{24,28},{28,24},{1,5},{5... | collective-permute-start | bytes 737288 | tf_op jit(solution)/shard_map/ppermute | solution.py:24
  40.1 15.4 %all-to-all-start.1 = ((bf16[16,6,1280]{2,1,0:T(8,128)(2,1)}), bf16[16,6,1280]{2,1,0:T(8,128)(2,1)S(1)}, u32[]{:S(2)}, u32[]{:S(2)}) async-start(bf16[16,6,1280]{2,1,0:T(8,128)(2,1)} %bitcast.20), calls=%async_computation.1 | async-start | bytes 655360 | tf_op jit(solution)/shard_map/all_to_all | solution.py:101

commit v4 on v2

--- a/solution.py
+++ b/solution.py
@@ -15,8 +15,8 @@
 
 def reorder(parts, index, bits):
     for k, bit in enumerate(bits):
-        upper = ((index >> bit) & 1) == 1
-        parts = [jnp.where(upper, parts[j ^ (1 << k)], parts[j]) for j in range(len(parts))]
+        lower = ((index >> bit) & 1) == 0
+        parts = [jnp.where(lower, parts[j], parts[j ^ (1 << k)]) for j in range(len(parts))]
     return parts
 
 
@@ -27,9 +27,11 @@
 def gathered(value, axis, size, bits, dim):
     index = lax.axis_index(axis)
     for group in grouped(bits):
-        parts = [value] + [
-            swap(value, axis, size, mask_of(j, group)) for j in range(1, 1 << len(group))
-        ]
+        landed = {
+            j: swap(value, axis, size, mask_of(j, group))
+            for j in reversed(range(1, 1 << len(group)))
+        }
+        parts = [value] + [landed[j] for j in range(1, 1 << len(group))]
         value = jnp.concatenate(reorder(parts, index, group), axis=dim)
     return value
 
@@ -41,7 +43,7 @@
         total = parts[0]
         landed = [
             swap(parts[j].astype(jnp.bfloat16), axis, size, mask_of(j, group))
-            for j in range(1, 1 << len(group))
+            for j in reversed(range(1, 1 << len(group)))
         ]
         for part in landed:
             total = total + part.astype(jnp.float32)
@@ -55,7 +57,14 @@
 
     def on_device(student_hidden, teacher_hidden, student_head, teacher_head):
         rows, share = student_hidden.shape
-        packed = jnp.concatenate([student_hidden, teacher_hidden], axis=1)
+        teacher_share = teacher_hidden.shape[1]
+        tokens = rows * dp
+        lane = lax.broadcasted_iota(jnp.int32, (rows, share + teacher_share), 1)
+        packed = jnp.where(
+            lane < share,
+            jnp.pad(student_hidden, ((0, 0), (0, teacher_share))),
+            jnp.pad(teacher_hidden, ((0, 0), (share, 0))),
+        )
         by_z = gathered(packed, "dp", dp, z_bits, 0)
         by_vocab = gathered(by_z[None], "vocab", vocab, vocab_bits, 0)
         whole = gathered(by_vocab, "dp", dp, core, 1)
@@ -75,21 +84,32 @@
         weighted = jnp.sum(shifted * (student_logits - teacher_logits), axis=1)
         other_peak = jnp.max(teacher_logits, axis=1)
         other_total = jnp.sum(jnp.exp(teacher_logits - other_peak[:, None]), axis=1)
-        stats = jnp.stack([peak, total, weighted, other_peak, other_total])
+        lanes = -(-tokens // 64) * 64
+        stats = jnp.stack([
+            peak + jnp.log(total),
+            weighted / total,
+            other_peak + jnp.log(other_total),
+            jnp.zeros_like(peak),
+        ])
+        stats = jnp.pad(stats, ((0, 0), (0, lanes - tokens))).reshape(2, 2 * lanes)
         devices = dp * vocab
         every = lax.all_to_all(
             jnp.broadcast_to(stats[None], (devices,) + stats.shape),
             ("dp", "vocab"), 0, 0, tiled=True,
         )
-        top = jnp.max(every[:, 0], axis=0)
-        scale = jnp.exp(every[:, 0] - top)
-        total_all = jnp.sum(every[:, 1] * scale, axis=0)
-        weighted_all = jnp.sum(every[:, 2] * scale, axis=0)
-        other_top = jnp.max(every[:, 3], axis=0)
-        other_all = jnp.sum(every[:, 4] * jnp.exp(every[:, 3] - other_top), axis=0)
-        student_lse = (top + jnp.log(total_all))[:, None]
-        teacher_lse = (other_top + jnp.log(other_all))[:, None]
-        divergence = (weighted_all / total_all)[:, None] - student_lse + teacher_lse
+        each_lse = every[:, 0, :tokens]
+        each_mean = every[:, 0, lanes : lanes + tokens]
+        each_other = every[:, 1, :tokens]
+
+        def joined(each):
+            top = jnp.max(each, axis=0)
+            return top + jnp.log(jnp.sum(jnp.exp(each - top), axis=0))
+
+        student_lse = joined(each_lse)
+        teacher_lse = joined(each_other)[:, None]
+        mean = jnp.sum(jnp.exp(each_lse - student_lse) * each_mean, axis=0)[:, None]
+        student_lse = student_lse[:, None]
+        divergence = mean - student_lse + teacher_lse
         log_student = student_logits - student_lse
         probs = jnp.exp(log_student)
         gap = log_student - (teacher_logits - teacher_lse)
@@ -100,15 +120,17 @@
         keep, send = reorder([logit_grad[:half], logit_grad[half:]], index, core)
         away = jnp.dot(send, student_head, preferred_element_type=jnp.float32).astype(jnp.bfloat16)
         landed = swap(away, "dp", dp, 1)
-        acc = jnp.dot(keep, student_head, preferred_element_type=jnp.float32)
-        acc = acc + landed.astype(jnp.float32)
-        acc = scattered(acc, "vocab", vocab, vocab_bits, 1)
-        acc = scattered(acc, "dp", dp, z_bits, 0)
-        hidden_grad = acc.astype(jnp.bfloat16)
-
+        near = lax.optimization_barrier(
+            jnp.dot(keep, student_head, preferred_element_type=jnp.float32)
+        )
+        acc = near + landed.astype(jnp.float32)
         head_grad = lax.dot_general(
             logit_grad, student_full, (((0,), (0,)), ((), ())), preferred_element_type=jnp.float32
         ).astype(jnp.bfloat16)
+        acc = scattered(acc, "vocab", vocab, vocab_bits, 1)
+        acc, head_grad = lax.optimization_barrier((acc, head_grad))
+        acc = scattered(acc, "dp", dp, z_bits, 0)
+        hidden_grad = acc.astype(jnp.bfloat16)
         return (hidden_grad, head_grad)
 
     return on_device

time: 53.5 us -> 50.4 us (0.942)
  waiting for transfers between devices: 17.4 us -> 13.8 us
  local copies, waits for them, and re-layouts: 2.4 us -> 0.29 us
  blocking collectives: 8.99 us -> 11.1 us
    ppermute x14, waiting for transfers between devices: 17.4 us -> 13.8 us  [swap(): return lax.ppermute(value, axis, [(i, i ^ mask) for i in range(size)])]
    all_to_all x1, blocking collectives: 8.99 us -> 11.1 us  [on_device(): lax.all_to_all(jnp.broadcast_to(stats[None], (devices,) + stats.shape), (...]
    unnamed x7 -> x4, local copies, waits for them, and re-layouts: 1.08 us -> 0.01 us
    select_n x3 -> x4, other arithmetic: 0.26 us -> 1.15 us  [the longest x1 0.89 us: on_device(): jnp.where(lane < share, jnp.pad(student_hidden, ((0, 0), (0, teacher_shar...]
    all_to_all x1 -> x0, other arithmetic: 0.72 us -> none  [on_device(): lax.all_to_all(jnp.broadcast_to(stats[None], (devices,) + stats.shape), (...]
    concatenate x1 -> x0, local copies, waits for them, and re-layouts: 0.72 us -> none  [on_device(): packed = jnp.concatenate([student_hidden, teacher_hidden], axis=1)]
  transfers between devices with their start and end apart: 14 -> 14, of which waited for: 11 -> 12; matrix products, arithmetic and copies ran while one was open for 3% -> 5% of each run, Pallas kernels for 0% -> 0%
where the time goes in v4:
time: 50.4 us; the launch traced here: 50.2 us
  starting transfers between devices  17.5 us (35%)
  waiting for transfers between devices  13.8 us (27%)
  blocking collectives  11.1 us (22%)
  matrix products  4.04 us (8%)
  other arithmetic  2.69 us (5%)
  between operations  0.8 us (2%)
    ppermute x14, starting transfers between devices, swap(): return lax.ppermute(value, axis, [(i, i ^ mask) for i in range(size)])  17.5 us
    ppermute x14, waiting for transfers between devices, swap(): return lax.ppermute(value, axis, [(i, i ^ mask) for i in range(size)])  13.8 us
    all_to_all x1, blocking collectives, on_device(): lax.all_to_all(jnp.broadcast_to(stats[None], (devices,) + stats.shape), (...  11.1 us
    dot_general x1, matrix products, on_device(): lax.dot_general(logit_grad, student_full, (((0,), (0,)), ((), ())), prefe...  1.87 us
  transfers between devices with their start and end apart: 14, of which 12 were waited for; matrix products, arithmetic and copies ran while one was open for 5% of the time, Pallas kernels for 0%

profile of v4, /device:TPU:0, one launch (start us, length us, event | category | flops | bytes accessed | tf_op | source)
XLA Modules:
  0.0 50.2 jit_solution(10372946742463589955)
XLA Ops:
  0.6 0.0 copy-start
  0.7 0.9 %pad_select_fusion = bf16[6,2304]{1,0:T(8,128)(2,1)S(1)} fusion(bf16[6,1024]{1,0:T(8,128)(2,1)} %param.5, bf16[6,1280]{1,0:T(8,128)(2,1)} %param.4, pred[2304]{0:T(1024)(128)(4,1)S(1)} %iota_compare_fusion), kind=kLoop, calls=%fused_computation.76 | loop fusion | flops 13824 | bytes 57600 | tf_op jit(solution)/shard_map/jit(_where)/select_n | solution.py:63
  1.6 5.1 %collective-permute-start.2 = (bf16[6,2304]{1,0:T(8,128)(2,1)S(1)}, bf16[6,2304]{1,0:T(8,128)(2,1)S(1)}, u32[]{:S(2)}, u32[]{:S(2)}) collective-permute-start(bf16[6,2304]{1,0:T(8,128)(2,1)S(1)} %pad_select_fusion), channel_id=1, source_target_pairs={{0,24},{4,28},{8,16},{12,20},{16,8},{20,12},{24,0},{28,4},{1,25},{... | collective-permute-start | bytes 82952 | tf_op jit(solution)/shard_map/ppermute | solution.py:24
  6.7 0.0 collective-permute-start.1
  6.7 0.6 %collective-permute-start = (bf16[6,2304]{1,0:T(8,128)(2,1)S(1)}, bf16[6,2304]{1,0:T(8,128)(2,1)S(1)}, u32[]{:S(2)}, u32[]{:S(2)}) collective-permute-start(bf16[6,2304]{1,0:T(8,128)(2,1)S(1)} %pad_select_fusion), channel_id=1, source_target_pairs={{0,8},{4,12},{8,0},{12,4},{16,24},{20,28},{24,16},{28,20},{1,9},{5... | collective-permute-start | bytes 82952 | tf_op jit(solution)/shard_map/ppermute | solution.py:24
  7.3 1.3 %collective-permute-done.2 = bf16[6,2304]{1,0:T(8,128)(2,1)S(1)} collective-permute-done((bf16[6,2304]{1,0:T(8,128)(2,1)S(1)}, bf16[6,2304]{1,0:T(8,128)(2,1)S(1)}, u32[]{:S(2)}, u32[]{:S(2)}) %collective-permute-start.2) | collective-permute-done | bytes 27680 | tf_op jit(solution)/shard_map/ppermute | solution.py:24
  8.6 2.9 %collective-permute-done.1 = bf16[6,2304]{1,0:T(8,128)(2,1)S(1)} collective-permute-done((bf16[6,2304]{1,0:T(8,128)(2,1)S(1)}, bf16[6,2304]{1,0:T(8,128)(2,1)S(1)}, u32[]{:S(2)}, u32[]{:S(2)}) %collective-permute-start.1) | collective-permute-done | bytes 27680 | tf_op jit(solution)/shard_map/ppermute | solution.py:24
  11.5 0.0 collective-permute-done
  11.6 0.1 maximum_bitcast_fusion
  11.6 1.6 %collective-permute-start.4 = (bf16[1,24,2304]{2,1,0:T(8,128)(2,1)S(1)}, bf16[1,24,2304]{2,1,0:T(8,128)(2,1)S(1)}, u32[]{:S(2)}, u32[]{:S(2)}) collective-permute-start(bf16[1,24,2304]{2,1,0:T(8,128)(2,1)S(1)} %maximum_bitcast_fusion), channel_id=1, source_target_pairs={{0,2},{1,3},{2,0},{3,1},{4,6},{5,7},{6,4},{7,5},{8,10},{9,11},{10,... | collective-permute-start | bytes 331784 | tf_op jit(solution)/shard_map/ppermute | solution.py:24
  13.2 1.4 %collective-permute-start.5 = (bf16[1,24,2304]{2,1,0:T(8,128)(2,1)S(1)}, bf16[1,24,2304]{2,1,0:T(8,128)(2,1)S(1)}, u32[]{:S(2)}, u32[]{:S(2)}) collective-permute-start(bf16[1,24,2304]{2,1,0:T(8,128)(2,1)S(1)} %maximum_bitcast_fusion), channel_id=1, source_target_pairs={{0,3},{1,2},{2,1},{3,0},{4,7},{5,6},{6,5},{7,4},{8,11},{9,10},{10,... | collective-permute-start | bytes 331784 | tf_op jit(solution)/shard_map/ppermute | solution.py:24
  14.6 0.5 %collective-permute-start.3 = (bf16[1,24,2304]{2,1,0:T(8,128)(2,1)S(1)}, bf16[1,24,2304]{2,1,0:T(8,128)(2,1)S(1)}, u32[]{:S(2)}, u32[]{:S(2)}) collective-permute-start(bf16[1,24,2304]{2,1,0:T(8,128)(2,1)S(1)} %maximum_bitcast_fusion), channel_id=1, source_target_pairs={{0,1},{1,0},{2,3},{3,2},{4,5},{5,4},{6,7},{7,6},{8,9},{9,8},{10,11... | collective-permute-start | bytes 331784 | tf_op jit(solution)/shard_map/ppermute | solution.py:24
  15.2 2.0 %collective-permute-done.4 = bf16[1,24,2304]{2,1,0:T(8,128)(2,1)S(1)} collective-permute-done((bf16[1,24,2304]{2,1,0:T(8,128)(2,1)S(1)}, bf16[1,24,2304]{2,1,0:T(8,128)(2,1)S(1)}, u32[]{:S(2)}, u32[]{:S(2)}) %collective-permute-start.4) | collective-permute-done | bytes 110624 | tf_op jit(solution)/shard_map/ppermute | solution.py:24
  17.2 1.7 %collective-permute-done.5 = bf16[1,24,2304]{2,1,0:T(8,128)(2,1)S(1)} collective-permute-done((bf16[1,24,2304]{2,1,0:T(8,128)(2,1)S(1)}, bf16[1,24,2304]{2,1,0:T(8,128)(2,1)S(1)}, u32[]{:S(2)}, u32[]{:S(2)}) %collective-permute-start.5) | collective-permute-done | bytes 110624 | tf_op jit(solution)/shard_map/ppermute | solution.py:24
  18.9 0.5 %collective-permute-done.3 = bf16[1,24,2304]{2,1,0:T(8,128)(2,1)S(1)} collective-permute-done((bf16[1,24,2304]{2,1,0:T(8,128)(2,1)S(1)}, bf16[1,24,2304]{2,1,0:T(8,128)(2,1)S(1)}, u32[]{:S(2)}, u32[]{:S(2)}) %collective-permute-start.3) | collective-permute-done | bytes 110624 | tf_op jit(solution)/shard_map/ppermute | solution.py:24
  19.4 0.1 broadcast_select_fusion.9
  19.5 0.1 pad_maximum_fusion.1
  19.6 0.1 collective-permute-start.6
  19.7 0.1 pad.18.clone
  19.8 0.0 copy-start.1
  19.8 1.7 %collective-permute-done.6 = bf16[4,24,2304]{2,1,0:T(8,128)(2,1)S(1)} collective-permute-done((bf16[4,24,2304]{2,1,0:T(8,128)(2,1)S(1)}, bf16[4,24,2304]{2,1,0:T(8,128)(2,1)S(1)}, u32[]{:S(2)}, u32[]{:S(2)}) %collective-permute-start.6) | collective-permute-done | bytes 442400 | tf_op jit(solution)/shard_map/ppermute | solution.py:24
  21.5 0.1 broadcast_select_fusion.1
  21.7 0.0 copy-done.1
  21.7 0.7 %fusion.38 = (f32[48]{0:T(128)S(1)}, f32[48,176]{1,0:T(8,128)S(1)}) fusion(bf16[176,4096]{1,0:T(8,128)(2,1)S(1)} %copy-done.1, bf16[48,1024]{1,0:T(8,128)(2,1)S(1)} %get-tuple-element.17, bf16[48,1024]{1,0:T(8,128)(2,1)S(1)} %get-tuple-element.18, bf16[48,1024]{1,0:T(8,128)(2,1)S(1)} %get-tuple-element.16, bf16[48,1024]{1,0:T(8,128)(2,1)S(1)} %get-tuple-element.15), kind=kOutput, calls=%fused_computation.109 | convolution fusion | flops 70787280 | bytes 1868992 | tf_op jit(solution)/shard_map/dot_general | solution.py:78
  22.3 0.0 copy-done
  22.4 0.8 %fusion.39 = (f32[48]{0:T(128)S(1)}, f32[48,176]{1,0:T(8,128)S(1)}) fusion(bf16[176,5120]{1,0:T(8,128)(2,1)S(1)} %copy-done, bf16[48,1280]{1,0:T(8,128)(2,1)S(1)} %get-tuple-element.14, bf16[48,1280]{1,0:T(8,128)(2,1)S(1)} %get-tuple-element.13, bf16[48,1280]{1,0:T(8,128)(2,1)S(1)} %get-tuple-element.12, bf16[48,1280]{1,0:T(8,128)(2,1)S(1)} %get-tuple-element.11), kind=kOutput, calls=%fused_computation.110 | convolution fusion | flops 88482000 | bytes 2327744 | tf_op jit(solution)/shard_map/dot_general | solution.py:75
  23.1 0.2 fusion.24
  23.4 0.1 maximum_maximum_fusion
  23.5 0.1 broadcast_in_dim.7
  23.6 11.1 %all_to_all.5 = f32[32,2,128]{2,1,0:T(2,128)S(1)} all-to-all(f32[32,2,128]{2,1,0:T(2,128)S(1)} %broadcast_in_dim.8), channel_id=1, replica_groups=mesh['dp'=8,'vocab'=4] {'dp','vocab'}, dimensions={0} | all-to-all | bytes 65536 | tf_op jit(solution)/shard_map/all_to_all | solution.py:96
  34.6 0.1 fusion.37
  34.9 0.1 multiply_convert_fusion
  35.0 0.3 convolution_convert_fusion.1
  35.4 0.1 collective-permute-start.7
  35.4 0.4 fusion.26
  35.8 1.1 %collective-permute-done.7 = bf16[24,5120]{1,0:T(8,128)(2,1)S(1)} collective-permute-done((bf16[24,5120]{1,0:T(8,128)(2,1)S(1)}, bf16[24,5120]{1,0:T(8,128)(2,1)S(1)}, u32[]{:S(2)}, u32[]{:S(2)}) %collective-permute-start.7) | collective-permute-done | bytes 245792 | tf_op jit(solution)/shard_map/ppermute | solution.py:24
  37.0 0.7 %collective-permute-start.8 = (bf16[24,1280]{1,0:T(8,128)(2,1)S(1)}, bf16[24,1280]{1,0:T(8,128)(2,1)S(1)}, u32[]{:S(2)}, u32[]{:S(2)}) collective-permute-start(bf16[24,1280]{1,0:T(8,128)(2,1)S(1)} %get-tuple-element.21), channel_id=1, source_target_pairs={{0,3},{1,2},{2,1},{3,0},{4,7},{5,6},{6,5},{7,4},{8,11},{9,10},{10,... | collective-permute-start | bytes 184328 | tf_op jit(solution)/shard_map/ppermute | solution.py:24
  37.7 1.3 %collective-permute-start.9 = (bf16[24,1280]{1,0:T(8,128)(2,1)S(1)}, bf16[24,1280]{1,0:T(8,128)(2,1)S(1)}, u32[]{:S(2)}, u32[]{:S(2)}) collective-permute-start(bf16[24,1280]{1,0:T(8,128)(2,1)S(1)} %get-tuple-element.22), channel_id=1, source_target_pairs={{0,2},{1,3},{2,0},{3,1},{4,6},{5,7},{6,4},{7,5},{8,10},{9,11},{10,... | collective-permute-start | bytes 184328 | tf_op jit(solution)/shard_map/ppermute | solution.py:24
  39.0 1.5 %collective-permute-start.10 = (bf16[24,1280]{1,0:T(8,128)(2,1)S(1)}, bf16[24,1280]{1,0:T(8,128)(2,1)S(1)}, u32[]{:S(2)}, u32[]{:S(2)}) collective-permute-start(bf16[24,1280]{1,0:T(8,128)(2,1)S(1)} %get-tuple-element.23), channel_id=1, source_target_pairs={{0,1},{1,0},{2,3},{3,2},{4,5},{5,4},{6,7},{7,6},{8,9},{9,8},{10,11... | collective-permute-start | bytes 184328 | tf_op jit(solution)/shard_map/ppermute | solution.py:24
  40.6 1.9 %convolution_convert_fusion = bf16[176,5120]{1,0:T(8,128)(2,1)} fusion(bf16[48,176]{1,0:T(8,128)(2,1)S(1)} %multiply_convert_fusion, bf16[48,1280]{1,0:T(8,128)(2,1)S(1)} %get-tuple-element.14, bf16[48,1280]{1,0:T(8,128)(2,1)S(1)} %get-tuple-element.13, bf16[48,1280]{1,0:T(8,128)(2,1)S(1)} %get-tuple-element.12, bf16[48,1280]{1,0:T(8,128)(2,1)S(1)} %get-tuple-element.11), kind=kOutput, calls=%fused_computation | convolution fusion | flops 89374720 | bytes 2310656 | tf_op jit(solution)/shard_map/dot_general | solution.py:127
  42.4 0.3 collective-permute-done.8
  42.7 0.1 collective-permute-done.9
  42.8 0.5 collective-permute-done.10
  43.3 0.1 convert_add_fusion.1
  43.3 0.7 %collective-permute-start.11 = (bf16[6,1280]{1,0:T(8,128)(2,1)S(1)}, bf16[6,1280]{1,0:T(8,128)(2,1)S(1)}, u32[]{:S(2)}, u32[]{:S(2)}) collective-permute-start(bf16[6,1280]{1,0:T(8,128)(2,1)S(1)} %get-tuple-element.32), channel_id=1, source_target_pairs={{0,24},{4,28},{8,16},{12,20},{16,8},{20,12},{24,0},{28,4},{1,25},{... | collective-permute-start | bytes 46088 | tf_op jit(solution)/shard_map/ppermute | solution.py:24
  44.0 1.4 %collective-permute-start.12 = (bf16[6,1280]{1,0:T(8,128)(2,1)S(1)}, bf16[6,1280]{1,0:T(8,128)(2,1)S(1)}, u32[]{:S(2)}, u32[]{:S(2)}) collective-permute-start(bf16[6,1280]{1,0:T(8,128)(2,1)S(1)} %get-tuple-element.33), channel_id=1, source_target_pairs={{0,16},{4,20},{8,24},{12,28},{16,0},{20,4},{24,8},{28,12},{1,17},{... | collective-permute-start | bytes 46088 | tf_op jit(solution)/shard_map/ppermute | solution.py:24
  45.5 2.3 %collective-permute-start.13 = (bf16[6,1280]{1,0:T(8,128)(2,1)S(1)}, bf16[6,1280]{1,0:T(8,128)(2,1)S(1)}, u32[]{:S(2)}, u32[]{:S(2)}) collective-permute-start(bf16[6,1280]{1,0:T(8,128)(2,1)S(1)} %get-tuple-element.34), channel_id=1, source_target_pairs={{0,8},{4,12},{8,0},{12,4},{16,24},{20,28},{24,16},{28,20},{1,9},{5... | collective-permute-start | bytes 46088 | tf_op jit(solution)/shard_map/ppermute | solution.py:24
  47.8 1.2 %collective-permute-done.11 = bf16[6,1280]{1,0:T(8,128)(2,1)S(1)} collective-permute-done((bf16[6,1280]{1,0:T(8,128)(2,1)S(1)}, bf16[6,1280]{1,0:T(8,128)(2,1)S(1)}, u32[]{:S(2)}, u32[]{:S(2)}) %collective-permute-start.11) | collective-permute-done | bytes 15392 | tf_op jit(solution)/shard_map/ppermute | solution.py:24
  49.0 0.0 collective-permute-done.12
  49.0 0.6 %collective-permute-done.13 = bf16[6,1280]{1,0:T(8,128)(2,1)S(1)} collective-permute-done((bf16[6,1280]{1,0:T(8,128)(2,1)S(1)}, bf16[6,1280]{1,0:T(8,128)(2,1)S(1)}, u32[]{:S(2)}, u32[]{:S(2)}) %collective-permute-start.13) | collective-permute-done | bytes 15392 | tf_op jit(solution)/shard_map/ppermute | solution.py:24
  49.6 0.6 %add_convert_fusion = bf16[6,1280]{1,0:T(8,128)(2,1)} fusion(bf16[6,1280]{1,0:T(8,128)(2,1)S(1)} %collective-permute-done.13, bf16[6,1280]{1,0:T(8,128)(2,1)S(1)} %collective-permute-done.12, bf16[6,1280]{1,0:T(8,128)(2,1)S(1)} %collective-permute-done.11, pred[]{:T(512)S(6)} %eq.20, f32[24,1280]{1,0:T(8,128)S(1)} %convert_add_fusion.1, pred[]{:T(512)S(6)} %eq.21), kind=kLoop, calls=%fused_computation.68 | loop fusion | flops 76800 | bytes 184322 | tf_op jit(solution)/shard_map/convert_element_type | solution.py:133
  (17 shorter events, 0.4 us)
Async XLA Ops:
  0.6 21.7 %copy-start = (bf16[176,5120]{1,0:T(8,128)(2,1)S(1)}, bf16[176,5120]{1,0:T(8,128)(2,1)}, u32[]{:S(2)}) copy-start(bf16[176,5120]{1,0:T(8,128)(2,1)} %param.6) | copy-start | bytes 5406724
  1.6 7.1 %collective-permute-start.2 = (bf16[6,2304]{1,0:T(8,128)(2,1)S(1)}, bf16[6,2304]{1,0:T(8,128)(2,1)S(1)}, u32[]{:S(2)}, u32[]{:S(2)}) collective-permute-start(bf16[6,2304]{1,0:T(8,128)(2,1)S(1)} %pad_select_fusion), channel_id=1, source_target_pairs={{0,24},{4,28},{8,16},{12,20},{16,8},{20,12},{24,0},{28,4},{1,25},{... | collective-permute-start | bytes 82952 | tf_op jit(solution)/shard_map/ppermute | solution.py:24
  6.7 4.9 %collective-permute-start.1 = (bf16[6,2304]{1,0:T(8,128)(2,1)S(1)}, bf16[6,2304]{1,0:T(8,128)(2,1)S(1)}, u32[]{:S(2)}, u32[]{:S(2)}) collective-permute-start(bf16[6,2304]{1,0:T(8,128)(2,1)S(1)} %pad_select_fusion), channel_id=1, source_target_pairs={{0,16},{4,20},{8,24},{12,28},{16,0},{20,4},{24,8},{28,12},{1,17},{... | collective-permute-start | bytes 82952 | tf_op jit(solution)/shard_map/ppermute | solution.py:24
  6.7 4.9 %collective-permute-start = (bf16[6,2304]{1,0:T(8,128)(2,1)S(1)}, bf16[6,2304]{1,0:T(8,128)(2,1)S(1)}, u32[]{:S(2)}, u32[]{:S(2)}) collective-permute-start(bf16[6,2304]{1,0:T(8,128)(2,1)S(1)} %pad_select_fusion), channel_id=1, source_target_pairs={{0,8},{4,12},{8,0},{12,4},{16,24},{20,28},{24,16},{28,20},{1,9},{5... | collective-permute-start | bytes 82952 | tf_op jit(solution)/shard_map/ppermute | solution.py:24
  11.6 5.6 %collective-permute-start.4 = (bf16[1,24,2304]{2,1,0:T(8,128)(2,1)S(1)}, bf16[1,24,2304]{2,1,0:T(8,128)(2,1)S(1)}, u32[]{:S(2)}, u32[]{:S(2)}) collective-permute-start(bf16[1,24,2304]{2,1,0:T(8,128)(2,1)S(1)} %maximum_bitcast_fusion), channel_id=1, source_target_pairs={{0,2},{1,3},{2,0},{3,1},{4,6},{5,7},{6,4},{7,5},{8,10},{9,11},{10,... | collective-permute-start | bytes 331784 | tf_op jit(solution)/shard_map/ppermute | solution.py:24
  13.2 5.6 %collective-permute-start.5 = (bf16[1,24,2304]{2,1,0:T(8,128)(2,1)S(1)}, bf16[1,24,2304]{2,1,0:T(8,128)(2,1)S(1)}, u32[]{:S(2)}, u32[]{:S(2)}) collective-permute-start(bf16[1,24,2304]{2,1,0:T(8,128)(2,1)S(1)} %maximum_bitcast_fusion), channel_id=1, source_target_pairs={{0,3},{1,2},{2,1},{3,0},{4,7},{5,6},{6,5},{7,4},{8,11},{9,10},{10,... | collective-permute-start | bytes 331784 | tf_op jit(solution)/shard_map/ppermute | solution.py:24
  14.6 4.7 %collective-permute-start.3 = (bf16[1,24,2304]{2,1,0:T(8,128)(2,1)S(1)}, bf16[1,24,2304]{2,1,0:T(8,128)(2,1)S(1)}, u32[]{:S(2)}, u32[]{:S(2)}) collective-permute-start(bf16[1,24,2304]{2,1,0:T(8,128)(2,1)S(1)} %maximum_bitcast_fusion), channel_id=1, source_target_pairs={{0,1},{1,0},{2,3},{3,2},{4,5},{5,4},{6,7},{7,6},{8,9},{9,8},{10,11... | collective-permute-start | bytes 331784 | tf_op jit(solution)/shard_map/ppermute | solution.py:24
  19.6 1.9 %collective-permute-start.6 = (bf16[4,24,2304]{2,1,0:T(8,128)(2,1)S(1)}, bf16[4,24,2304]{2,1,0:T(8,128)(2,1)S(1)}, u32[]{:S(2)}, u32[]{:S(2)}) collective-permute-start(bf16[4,24,2304]{2,1,0:T(8,128)(2,1)S(1)} %pad_maximum_fusion.1), channel_id=1, source_target_pairs={{0,4},{4,0},{8,12},{12,8},{16,20},{20,16},{24,28},{28,24},{1,5},{5... | collective-permute-start | bytes 1327112 | tf_op jit(solution)/shard_map/ppermute | solution.py:24
  19.8 1.9 %copy-start.1 = (bf16[176,4096]{1,0:T(8,128)(2,1)S(1)}, bf16[176,4096]{1,0:T(8,128)(2,1)}, u32[]{:S(2)}) copy-start(bf16[176,4096]{1,0:T(8,128)(2,1)} %param.7) | copy-start | bytes 4325380
  35.4 1.6 %collective-permute-start.7 = (bf16[24,5120]{1,0:T(8,128)(2,1)S(1)}, bf16[24,5120]{1,0:T(8,128)(2,1)S(1)}, u32[]{:S(2)}, u32[]{:S(2)}) collective-permute-start(bf16[24,5120]{1,0:T(8,128)(2,1)S(1)} %convolution_convert_fusion.1), channel_id=1, source_target_pairs={{0,4},{4,0},{8,12},{12,8},{16,20},{20,16},{24,28},{28,24},{1,5},{5... | collective-permute-start | bytes 737288 | tf_op jit(solution)/shard_map/ppermute | solution.py:24
  37.0 5.7 %collective-permute-start.8 = (bf16[24,1280]{1,0:T(8,128)(2,1)S(1)}, bf16[24,1280]{1,0:T(8,128)(2,1)S(1)}, u32[]{:S(2)}, u32[]{:S(2)}) collective-permute-start(bf16[24,1280]{1,0:T(8,128)(2,1)S(1)} %get-tuple-element.21), channel_id=1, source_target_pairs={{0,3},{1,2},{2,1},{3,0},{4,7},{5,6},{6,5},{7,4},{8,11},{9,10},{10,... | collective-permute-start | bytes 184328 | tf_op jit(solution)/shard_map/ppermute | solution.py:24
  37.7 5.1 %collective-permute-start.9 = (bf16[24,1280]{1,0:T(8,128)(2,1)S(1)}, bf16[24,1280]{1,0:T(8,128)(2,1)S(1)}, u32[]{:S(2)}, u32[]{:S(2)}) collective-permute-start(bf16[24,1280]{1,0:T(8,128)(2,1)S(1)} %get-tuple-element.22), channel_id=1, source_target_pairs={{0,2},{1,3},{2,0},{3,1},{4,6},{5,7},{6,4},{7,5},{8,10},{9,11},{10,... | collective-permute-start | bytes 184328 | tf_op jit(solution)/shard_map/ppermute | solution.py:24
  39.0 4.2 %collective-permute-start.10 = (bf16[24,1280]{1,0:T(8,128)(2,1)S(1)}, bf16[24,1280]{1,0:T(8,128)(2,1)S(1)}, u32[]{:S(2)}, u32[]{:S(2)}) collective-permute-start(bf16[24,1280]{1,0:T(8,128)(2,1)S(1)} %get-tuple-element.23), channel_id=1, source_target_pairs={{0,1},{1,0},{2,3},{3,2},{4,5},{5,4},{6,7},{7,6},{8,9},{9,8},{10,11... | collective-permute-start | bytes 184328 | tf_op jit(solution)/shard_map/ppermute | solution.py:24
  43.3 5.6 %collective-permute-start.11 = (bf16[6,1280]{1,0:T(8,128)(2,1)S(1)}, bf16[6,1280]{1,0:T(8,128)(2,1)S(1)}, u32[]{:S(2)}, u32[]{:S(2)}) collective-permute-start(bf16[6,1280]{1,0:T(8,128)(2,1)S(1)} %get-tuple-element.32), channel_id=1, source_target_pairs={{0,24},{4,28},{8,16},{12,20},{16,8},{20,12},{24,0},{28,4},{1,25},{... | collective-permute-start | bytes 46088 | tf_op jit(solution)/shard_map/ppermute | solution.py:24
  44.0 5.0 %collective-permute-start.12 = (bf16[6,1280]{1,0:T(8,128)(2,1)S(1)}, bf16[6,1280]{1,0:T(8,128)(2,1)S(1)}, u32[]{:S(2)}, u32[]{:S(2)}) collective-permute-start(bf16[6,1280]{1,0:T(8,128)(2,1)S(1)} %get-tuple-element.33), channel_id=1, source_target_pairs={{0,16},{4,20},{8,24},{12,28},{16,0},{20,4},{24,8},{28,12},{1,17},{... | collective-permute-start | bytes 46088 | tf_op jit(solution)/shard_map/ppermute | solution.py:24
  45.5 4.1 %collective-permute-start.13 = (bf16[6,1280]{1,0:T(8,128)(2,1)S(1)}, bf16[6,1280]{1,0:T(8,128)(2,1)S(1)}, u32[]{:S(2)}, u32[]{:S(2)}) collective-permute-start(bf16[6,1280]{1,0:T(8,128)(2,1)S(1)} %get-tuple-element.34), channel_id=1, source_target_pairs={{0,8},{4,12},{8,0},{12,4},{16,24},{20,28},{24,16},{28,20},{1,9},{5... | collective-permute-start | bytes 46088 | tf_op jit(solution)/shard_map/ppermute | solution.py:24

commit v5 on v4

--- a/solution.py
+++ b/solution.py
@@ -67,9 +67,13 @@
         )
         by_z = gathered(packed, "dp", dp, z_bits, 0)
         by_vocab = gathered(by_z[None], "vocab", vocab, vocab_bits, 0)
-        whole = gathered(by_vocab, "dp", dp, core, 1)
-        student_full = jnp.concatenate([whole[i, :, :share] for i in range(vocab)], axis=1)
-        teacher_full = jnp.concatenate([whole[i, :, share:] for i in range(vocab)], axis=1)
+        index = lax.axis_index("dp")
+        teacher_half = jnp.concatenate([by_vocab[i, :, share:] for i in range(vocab)], axis=1)
+        student_half = jnp.concatenate([by_vocab[i, :, :share] for i in range(vocab)], axis=1)
+        teacher_full, student_full = [
+            jnp.concatenate(reorder([rows_of_half, swap(rows_of_half, "dp", dp, 1)], index, core))
+            for rows_of_half in (teacher_half, student_half)
+        ]
 
         contract = (((1,), (1,)), ((), ()))
         student_logits = lax.dot_general(
@@ -115,7 +119,6 @@
         gap = log_student - (teacher_logits - teacher_lse)
         logit_grad = (probs * (gap - divergence)).astype(jnp.bfloat16)
 
-        index = lax.axis_index("dp")
         half = logit_grad.shape[0] // 2
         keep, send = reorder([logit_grad[:half], logit_grad[half:]], index, core)
         away = jnp.dot(send, student_head, preferred_element_type=jnp.float32).astype(jnp.bfloat16)

time: 50.4 us -> 51.2 us (1.016)
  other arithmetic: 2.69 us -> 3.66 us
  waiting for transfers between devices: 13.8 us -> 13 us
    select_n x3 -> x4, other arithmetic: 0.26 us -> 1.33 us  [reorder(): jnp.where(lower, parts[j], parts[j ^ 1 << k])]
    ppermute x14 -> x15, waiting for transfers between devices: 13.8 us -> 13 us  [swap(): return lax.ppermute(value, axis, [(i, i ^ mask) for i in range(size)])]
    ppermute x14 -> x15, starting transfers between devices: 17.5 us -> 18 us  [swap(): return lax.ppermute(value, axis, [(i, i ^ mask) for i in range(size)])]
  transfers between devices with their start and end apart: 14 -> 15, of which waited for: 12 -> 12; matrix products, arithmetic and copies ran while one was open for 5% -> 6% of each run, Pallas kernels for 0% -> 0%
where the time goes in v5:
time: 51.2 us; the launch traced here: 51 us
  starting transfers between devices  18 us (35%)
  waiting for transfers between devices  13 us (25%)
  blocking collectives  11.1 us (22%)
  matrix products  4.03 us (8%)
  other arithmetic  3.66 us (7%)
  between operations  0.83 us (2%)
    ppermute x15, starting transfers between devices, swap(): return lax.ppermute(value, axis, [(i, i ^ mask) for i in range(size)])  18 us
    ppermute x15, waiting for transfers between devices, swap(): return lax.ppermute(value, axis, [(i, i ^ mask) for i in range(size)])  13 us
    all_to_all x1, blocking collectives, on_device(): lax.all_to_all(jnp.broadcast_to(stats[None], (devices,) + stats.shape), (...  11.1 us
    dot_general x1, matrix products, on_device(): lax.dot_general(logit_grad, student_full, (((0,), (0,)), ((), ())), prefe...  1.86 us
    select_n x4, other arithmetic, reorder(): jnp.where(lower, parts[j], parts[j ^ 1 << k])  1.33 us
  transfers between devices with their start and end apart: 15, of which 12 were waited for; matrix products, arithmetic and copies ran while one was open for 6% of the time, Pallas kernels for 0%

profile of v5, /device:TPU:0, one launch (start us, length us, event | category | flops | bytes accessed | tf_op | source)
XLA Modules:
  0.0 51.0 jit_solution(10431782772717344670)
XLA Ops:
  0.6 0.0 copy-start
  0.7 0.9 %pad_select_fusion = bf16[6,2304]{1,0:T(8,128)(2,1)S(1)} fusion(bf16[6,1024]{1,0:T(8,128)(2,1)} %param.5, bf16[6,1280]{1,0:T(8,128)(2,1)} %param.4, pred[2304]{0:T(1024)(128)(4,1)S(1)} %iota_compare_fusion), kind=kLoop, calls=%fused_computation.53 | loop fusion | flops 13824 | bytes 57600 | tf_op jit(solution)/shard_map/jit(_where)/select_n | solution.py:63
  1.6 5.1 %collective-permute-start.2 = (bf16[6,2304]{1,0:T(8,128)(2,1)S(1)}, bf16[6,2304]{1,0:T(8,128)(2,1)S(1)}, u32[]{:S(2)}, u32[]{:S(2)}) collective-permute-start(bf16[6,2304]{1,0:T(8,128)(2,1)S(1)} %pad_select_fusion), channel_id=1, source_target_pairs={{0,24},{4,28},{8,16},{12,20},{16,8},{20,12},{24,0},{28,4},{1,25},{... | collective-permute-start | bytes 82952 | tf_op jit(solution)/shard_map/ppermute | solution.py:24
  6.7 0.0 collective-permute-start.1
  6.7 0.6 %collective-permute-start = (bf16[6,2304]{1,0:T(8,128)(2,1)S(1)}, bf16[6,2304]{1,0:T(8,128)(2,1)S(1)}, u32[]{:S(2)}, u32[]{:S(2)}) collective-permute-start(bf16[6,2304]{1,0:T(8,128)(2,1)S(1)} %pad_select_fusion), channel_id=1, source_target_pairs={{0,8},{4,12},{8,0},{12,4},{16,24},{20,28},{24,16},{28,20},{1,9},{5... | collective-permute-start | bytes 82952 | tf_op jit(solution)/shard_map/ppermute | solution.py:24
  7.3 1.3 %collective-permute-done.2 = bf16[6,2304]{1,0:T(8,128)(2,1)S(1)} collective-permute-done((bf16[6,2304]{1,0:T(8,128)(2,1)S(1)}, bf16[6,2304]{1,0:T(8,128)(2,1)S(1)}, u32[]{:S(2)}, u32[]{:S(2)}) %collective-permute-start.2) | collective-permute-done | bytes 27680 | tf_op jit(solution)/shard_map/ppermute | solution.py:24
  8.6 2.9 %collective-permute-done.1 = bf16[6,2304]{1,0:T(8,128)(2,1)S(1)} collective-permute-done((bf16[6,2304]{1,0:T(8,128)(2,1)S(1)}, bf16[6,2304]{1,0:T(8,128)(2,1)S(1)}, u32[]{:S(2)}, u32[]{:S(2)}) %collective-permute-start.1) | collective-permute-done | bytes 27680 | tf_op jit(solution)/shard_map/ppermute | solution.py:24
  11.5 0.0 collective-permute-done
  11.6 0.1 maximum_bitcast_fusion
  11.6 0.0 copy-start.1
  11.6 1.6 %collective-permute-start.4 = (bf16[1,24,2304]{2,1,0:T(8,128)(2,1)S(1)}, bf16[1,24,2304]{2,1,0:T(8,128)(2,1)}, u32[]{:S(2)}, u32[]{:S(2)}) collective-permute-start(bf16[1,24,2304]{2,1,0:T(8,128)(2,1)S(1)} %maximum_bitcast_fusion), channel_id=1, source_target_pairs={{0,2},{1,3},{2,0},{3,1},{4,6},{5,7},{6,4},{7,5},{8,10},{9,11},{10,... | collective-permute-start | bytes 331784 | tf_op jit(solution)/shard_map/ppermute | solution.py:24
  13.2 1.4 %collective-permute-start.5 = (bf16[1,24,2304]{2,1,0:T(8,128)(2,1)S(1)}, bf16[1,24,2304]{2,1,0:T(8,128)(2,1)}, u32[]{:S(2)}, u32[]{:S(2)}) collective-permute-start(bf16[1,24,2304]{2,1,0:T(8,128)(2,1)S(1)} %maximum_bitcast_fusion), channel_id=1, source_target_pairs={{0,3},{1,2},{2,1},{3,0},{4,7},{5,6},{6,5},{7,4},{8,11},{9,10},{10,... | collective-permute-start | bytes 331784 | tf_op jit(solution)/shard_map/ppermute | solution.py:24
  14.7 0.5 %collective-permute-start.3 = (bf16[1,24,2304]{2,1,0:T(8,128)(2,1)S(1)}, bf16[1,24,2304]{2,1,0:T(8,128)(2,1)}, u32[]{:S(2)}, u32[]{:S(2)}) collective-permute-start(bf16[1,24,2304]{2,1,0:T(8,128)(2,1)S(1)} %maximum_bitcast_fusion), channel_id=1, source_target_pairs={{0,1},{1,0},{2,3},{3,2},{4,5},{5,4},{6,7},{7,6},{8,9},{9,8},{10,11... | collective-permute-start | bytes 331784 | tf_op jit(solution)/shard_map/ppermute | solution.py:24
  15.2 0.1 pad.18.clone
  15.3 2.0 %collective-permute-done.4 = bf16[1,24,2304]{2,1,0:T(8,128)(2,1)} collective-permute-done((bf16[1,24,2304]{2,1,0:T(8,128)(2,1)S(1)}, bf16[1,24,2304]{2,1,0:T(8,128)(2,1)}, u32[]{:S(2)}, u32[]{:S(2)}) %collective-permute-start.4) | collective-permute-done | bytes 110624 | tf_op jit(solution)/shard_map/ppermute | solution.py:24
  17.3 1.7 %collective-permute-done.5 = bf16[1,24,2304]{2,1,0:T(8,128)(2,1)} collective-permute-done((bf16[1,24,2304]{2,1,0:T(8,128)(2,1)S(1)}, bf16[1,24,2304]{2,1,0:T(8,128)(2,1)}, u32[]{:S(2)}, u32[]{:S(2)}) %collective-permute-start.5) | collective-permute-done | bytes 110624 | tf_op jit(solution)/shard_map/ppermute | solution.py:24
  19.0 0.5 %collective-permute-done.3 = bf16[1,24,2304]{2,1,0:T(8,128)(2,1)} collective-permute-done((bf16[1,24,2304]{2,1,0:T(8,128)(2,1)S(1)}, bf16[1,24,2304]{2,1,0:T(8,128)(2,1)}, u32[]{:S(2)}, u32[]{:S(2)}) %collective-permute-start.3) | collective-permute-done | bytes 110624 | tf_op jit(solution)/shard_map/ppermute | solution.py:24
  19.5 1.2 %broadcast_select_fusion.11 = (bf16[1,24,2304]{2,1,0:T(8,128)(2,1)S(1)}, bf16[1,24,2304]{2,1,0:T(8,128)(2,1)S(1)}, bf16[1,24,2304]{2,1,0:T(8,128)(2,1)S(1)}, bf16[1,24,2304]{2,1,0:T(8,128)(2,1)S(1)}) fusion(pred[]{:T(512)S(6)} %eq.23, bf16[1,24,2304]{2,1,0:T(8,128)(2,1)} %collective-permute-done.3, pred[]{:T(512)S(6)} %eq.24, ...), kind=kLoop, calls=%fused_computation.31 | loop fusion | flops 884736 | bytes 884738 | tf_op jit(solution)/shard_map/jit(_where)/select_n | solution.py:19
  20.8 0.1 collective-permute-start.7
  20.9 0.6 %collective-permute-start.6 = (bf16[24,5120]{1,0:T(8,128)(2,1)S(1)}, bf16[24,5120]{1,0:T(8,128)(2,1)S(1)}, u32[]{:S(2)}, u32[]{:S(2)}) collective-permute-start(bf16[24,5120]{1,0:T(8,128)(2,1)S(1)} %pad_maximum_fusion.3), channel_id=1, source_target_pairs={{0,4},{4,0},{8,12},{12,8},{16,20},{20,16},{24,28},{28,24},{1,5},{5... | collective-permute-start | bytes 737288 | tf_op jit(solution)/shard_map/ppermute | solution.py:24
  21.4 0.8 %collective-permute-done.7 = bf16[24,4096]{1,0:T(8,128)(2,1)S(1)} collective-permute-done((bf16[24,4096]{1,0:T(8,128)(2,1)S(1)}, bf16[24,4096]{1,0:T(8,128)(2,1)S(1)}, u32[]{:S(2)}, u32[]{:S(2)}) %collective-permute-start.7) | collective-permute-done | bytes 196640 | tf_op jit(solution)/shard_map/ppermute | solution.py:24
  22.3 0.1 broadcast_select_fusion.3
  22.3 0.0 copy-done.1
  22.3 0.7 %fusion.19 = (f32[48]{0:T(128)S(1)}, f32[48,176]{1,0:T(8,128)S(1)}) fusion(bf16[176,4096]{1,0:T(8,128)(2,1)S(1)} %copy-done.1, bf16[24,4096]{1,0:T(8,128)(2,1)S(1)} %get-tuple-element.21, bf16[24,4096]{1,0:T(8,128)(2,1)S(1)} %get-tuple-element.20), kind=kOutput, calls=%fused_computation.86 | convolution fusion | flops 70000848 | bytes 1868992 | tf_op jit(solution)/shard_map/dot_general | solution.py:82
  23.0 0.0 collective-permute-done.6
  23.0 0.1 broadcast_select_fusion.1
  23.1 0.0 copy-done
  23.1 0.8 %fusion.20 = (f32[48]{0:T(128)S(1)}, f32[48,176]{1,0:T(8,128)S(1)}) fusion(bf16[176,5120]{1,0:T(8,128)(2,1)S(1)} %copy-done, bf16[24,5120]{1,0:T(8,128)(2,1)S(1)} %get-tuple-element.15, bf16[24,5120]{1,0:T(8,128)(2,1)S(1)} %get-tuple-element.14), kind=kOutput, calls=%fused_computation.87 | convolution fusion | flops 87498960 | bytes 2327744 | tf_op jit(solution)/shard_map/dot_general | solution.py:79
  23.9 0.2 fusion.5
  24.2 0.1 maximum_maximum_fusion
  24.3 0.1 broadcast_in_dim.7
  24.4 11.1 %all_to_all.5 = f32[32,2,128]{2,1,0:T(2,128)S(1)} all-to-all(f32[32,2,128]{2,1,0:T(2,128)S(1)} %broadcast_in_dim.8), channel_id=1, replica_groups=mesh['dp'=8,'vocab'=4] {'dp','vocab'}, dimensions={0} | all-to-all | bytes 65536 | tf_op jit(solution)/shard_map/all_to_all | solution.py:100
  35.4 0.1 fusion.18
  35.7 0.1 multiply_convert_fusion
  35.8 0.3 convolution_convert_fusion.1
  36.2 0.1 collective-permute-start.8
  36.2 0.3 fusion.7
  36.6 1.1 %collective-permute-done.8 = bf16[24,5120]{1,0:T(8,128)(2,1)S(1)} collective-permute-done((bf16[24,5120]{1,0:T(8,128)(2,1)S(1)}, bf16[24,5120]{1,0:T(8,128)(2,1)S(1)}, u32[]{:S(2)}, u32[]{:S(2)}) %collective-permute-start.8) | collective-permute-done | bytes 245792 | tf_op jit(solution)/shard_map/ppermute | solution.py:24
  37.8 0.7 %collective-permute-start.9 = (bf16[24,1280]{1,0:T(8,128)(2,1)S(1)}, bf16[24,1280]{1,0:T(8,128)(2,1)S(1)}, u32[]{:S(2)}, u32[]{:S(2)}) collective-permute-start(bf16[24,1280]{1,0:T(8,128)(2,1)S(1)} %get-tuple-element.11), channel_id=1, source_target_pairs={{0,3},{1,2},{2,1},{3,0},{4,7},{5,6},{6,5},{7,4},{8,11},{9,10},{10,... | collective-permute-start | bytes 184328 | tf_op jit(solution)/shard_map/ppermute | solution.py:24
  38.5 1.3 %collective-permute-start.10 = (bf16[24,1280]{1,0:T(8,128)(2,1)S(1)}, bf16[24,1280]{1,0:T(8,128)(2,1)S(1)}, u32[]{:S(2)}, u32[]{:S(2)}) collective-permute-start(bf16[24,1280]{1,0:T(8,128)(2,1)S(1)} %get-tuple-element.12), channel_id=1, source_target_pairs={{0,2},{1,3},{2,0},{3,1},{4,6},{5,7},{6,4},{7,5},{8,10},{9,11},{10,... | collective-permute-start | bytes 184328 | tf_op jit(solution)/shard_map/ppermute | solution.py:24
  39.8 1.5 %collective-permute-start.11 = (bf16[24,1280]{1,0:T(8,128)(2,1)S(1)}, bf16[24,1280]{1,0:T(8,128)(2,1)S(1)}, u32[]{:S(2)}, u32[]{:S(2)}) collective-permute-start(bf16[24,1280]{1,0:T(8,128)(2,1)S(1)} %get-tuple-element.13), channel_id=1, source_target_pairs={{0,1},{1,0},{2,3},{3,2},{4,5},{5,4},{6,7},{7,6},{8,9},{9,8},{10,11... | collective-permute-start | bytes 184328 | tf_op jit(solution)/shard_map/ppermute | solution.py:24
  41.4 1.9 %convolution_convert_fusion = bf16[176,5120]{1,0:T(8,128)(2,1)} fusion(bf16[48,176]{1,0:T(8,128)(2,1)S(1)} %multiply_convert_fusion, bf16[24,5120]{1,0:T(8,128)(2,1)S(1)} %get-tuple-element.15, bf16[24,5120]{1,0:T(8,128)(2,1)S(1)} %get-tuple-element.14), kind=kOutput, calls=%fused_computation | convolution fusion | flops 88391680 | bytes 2310656 | tf_op jit(solution)/shard_map/dot_general | solution.py:130
  43.2 0.3 collective-permute-done.9
  43.5 0.1 collective-permute-done.10
  43.6 0.5 collective-permute-done.11
  44.1 0.7 %collective-permute-start.12 = (bf16[6,1280]{1,0:T(8,128)(2,1)S(1)}, bf16[6,1280]{1,0:T(8,128)(2,1)S(1)}, u32[]{:S(2)}, u32[]{:S(2)}) collective-permute-start(bf16[6,1280]{1,0:T(8,128)(2,1)S(1)} %get-tuple-element.26), channel_id=1, source_target_pairs={{0,24},{4,28},{8,16},{12,20},{16,8},{20,12},{24,0},{28,4},{1,25},{... | collective-permute-start | bytes 46088 | tf_op jit(solution)/shard_map/ppermute | solution.py:24
  44.8 1.4 %collective-permute-start.13 = (bf16[6,1280]{1,0:T(8,128)(2,1)S(1)}, bf16[6,1280]{1,0:T(8,128)(2,1)S(1)}, u32[]{:S(2)}, u32[]{:S(2)}) collective-permute-start(bf16[6,1280]{1,0:T(8,128)(2,1)S(1)} %get-tuple-element.27), channel_id=1, source_target_pairs={{0,16},{4,20},{8,24},{12,28},{16,0},{20,4},{24,8},{28,12},{1,17},{... | collective-permute-start | bytes 46088 | tf_op jit(solution)/shard_map/ppermute | solution.py:24
  46.2 2.3 %collective-permute-start.14 = (bf16[6,1280]{1,0:T(8,128)(2,1)S(1)}, bf16[6,1280]{1,0:T(8,128)(2,1)S(1)}, u32[]{:S(2)}, u32[]{:S(2)}) collective-permute-start(bf16[6,1280]{1,0:T(8,128)(2,1)S(1)} %get-tuple-element.28), channel_id=1, source_target_pairs={{0,8},{4,12},{8,0},{12,4},{16,24},{20,28},{24,16},{28,20},{1,9},{5... | collective-permute-start | bytes 46088 | tf_op jit(solution)/shard_map/ppermute | solution.py:24
  48.6 1.2 %collective-permute-done.12 = bf16[6,1280]{1,0:T(8,128)(2,1)S(1)} collective-permute-done((bf16[6,1280]{1,0:T(8,128)(2,1)S(1)}, bf16[6,1280]{1,0:T(8,128)(2,1)S(1)}, u32[]{:S(2)}, u32[]{:S(2)}) %collective-permute-start.12) | collective-permute-done | bytes 15392 | tf_op jit(solution)/shard_map/ppermute | solution.py:24
  49.8 0.0 collective-permute-done.13
  49.8 0.6 %collective-permute-done.14 = bf16[6,1280]{1,0:T(8,128)(2,1)S(1)} collective-permute-done((bf16[6,1280]{1,0:T(8,128)(2,1)S(1)}, bf16[6,1280]{1,0:T(8,128)(2,1)S(1)}, u32[]{:S(2)}, u32[]{:S(2)}) %collective-permute-start.14) | collective-permute-done | bytes 15392 | tf_op jit(solution)/shard_map/ppermute | solution.py:24
  50.3 0.6 %add_convert_fusion = bf16[6,1280]{1,0:T(8,128)(2,1)} fusion(bf16[6,1280]{1,0:T(8,128)(2,1)S(1)} %collective-permute-done.14, bf16[6,1280]{1,0:T(8,128)(2,1)S(1)} %collective-permute-done.13, bf16[6,1280]{1,0:T(8,128)(2,1)S(1)} %collective-permute-done.12, pred[]{:T(512)S(6)} %eq.10, f32[24,1280]{1,0:T(8,128)S(1)} %convert_add_fusion.1, pred[]{:T(512)S(6)} %eq.22), kind=kLoop, calls=%fused_computation.45 | loop fusion | flops 76800 | bytes 184322 | tf_op jit(solution)/shard_map/convert_element_type | solution.py:136
  (23 shorter events, 0.4 us)
Async XLA Ops:
  0.6 22.5 %copy-start = (bf16[176,5120]{1,0:T(8,128)(2,1)S(1)}, bf16[176,5120]{1,0:T(8,128)(2,1)}, u32[]{:S(2)}) copy-start(bf16[176,5120]{1,0:T(8,128)(2,1)} %param.6) | copy-start | bytes 5406724
  1.6 7.1 %collective-permute-start.2 = (bf16[6,2304]{1,0:T(8,128)(2,1)S(1)}, bf16[6,2304]{1,0:T(8,128)(2,1)S(1)}, u32[]{:S(2)}, u32[]{:S(2)}) collective-permute-start(bf16[6,2304]{1,0:T(8,128)(2,1)S(1)} %pad_select_fusion), channel_id=1, source_target_pairs={{0,24},{4,28},{8,16},{12,20},{16,8},{20,12},{24,0},{28,4},{1,25},{... | collective-permute-start | bytes 82952 | tf_op jit(solution)/shard_map/ppermute | solution.py:24
  6.7 4.9 %collective-permute-start.1 = (bf16[6,2304]{1,0:T(8,128)(2,1)S(1)}, bf16[6,2304]{1,0:T(8,128)(2,1)S(1)}, u32[]{:S(2)}, u32[]{:S(2)}) collective-permute-start(bf16[6,2304]{1,0:T(8,128)(2,1)S(1)} %pad_select_fusion), channel_id=1, source_target_pairs={{0,16},{4,20},{8,24},{12,28},{16,0},{20,4},{24,8},{28,12},{1,17},{... | collective-permute-start | bytes 82952 | tf_op jit(solution)/shard_map/ppermute | solution.py:24
  6.7 4.9 %collective-permute-start = (bf16[6,2304]{1,0:T(8,128)(2,1)S(1)}, bf16[6,2304]{1,0:T(8,128)(2,1)S(1)}, u32[]{:S(2)}, u32[]{:S(2)}) collective-permute-start(bf16[6,2304]{1,0:T(8,128)(2,1)S(1)} %pad_select_fusion), channel_id=1, source_target_pairs={{0,8},{4,12},{8,0},{12,4},{16,24},{20,28},{24,16},{28,20},{1,9},{5... | collective-permute-start | bytes 82952 | tf_op jit(solution)/shard_map/ppermute | solution.py:24
  11.6 10.7 %copy-start.1 = (bf16[176,4096]{1,0:T(8,128)(2,1)S(1)}, bf16[176,4096]{1,0:T(8,128)(2,1)}, u32[]{:S(2)}) copy-start(bf16[176,4096]{1,0:T(8,128)(2,1)} %param.7) | copy-start | bytes 4325380
  11.6 5.7 %collective-permute-start.4 = (bf16[1,24,2304]{2,1,0:T(8,128)(2,1)S(1)}, bf16[1,24,2304]{2,1,0:T(8,128)(2,1)}, u32[]{:S(2)}, u32[]{:S(2)}) collective-permute-start(bf16[1,24,2304]{2,1,0:T(8,128)(2,1)S(1)} %maximum_bitcast_fusion), channel_id=1, source_target_pairs={{0,2},{1,3},{2,0},{3,1},{4,6},{5,7},{6,4},{7,5},{8,10},{9,11},{10,... | collective-permute-start | bytes 331784 | tf_op jit(solution)/shard_map/ppermute | solution.py:24
  13.2 5.8 %collective-permute-start.5 = (bf16[1,24,2304]{2,1,0:T(8,128)(2,1)S(1)}, bf16[1,24,2304]{2,1,0:T(8,128)(2,1)}, u32[]{:S(2)}, u32[]{:S(2)}) collective-permute-start(bf16[1,24,2304]{2,1,0:T(8,128)(2,1)S(1)} %maximum_bitcast_fusion), channel_id=1, source_target_pairs={{0,3},{1,2},{2,1},{3,0},{4,7},{5,6},{6,5},{7,4},{8,11},{9,10},{10,... | collective-permute-start | bytes 331784 | tf_op jit(solution)/shard_map/ppermute | solution.py:24
  14.7 4.9 %collective-permute-start.3 = (bf16[1,24,2304]{2,1,0:T(8,128)(2,1)S(1)}, bf16[1,24,2304]{2,1,0:T(8,128)(2,1)}, u32[]{:S(2)}, u32[]{:S(2)}) collective-permute-start(bf16[1,24,2304]{2,1,0:T(8,128)(2,1)S(1)} %maximum_bitcast_fusion), channel_id=1, source_target_pairs={{0,1},{1,0},{2,3},{3,2},{4,5},{5,4},{6,7},{7,6},{8,9},{9,8},{10,11... | collective-permute-start | bytes 331784 | tf_op jit(solution)/shard_map/ppermute | solution.py:24
  20.8 1.5 %collective-permute-start.7 = (bf16[24,4096]{1,0:T(8,128)(2,1)S(1)}, bf16[24,4096]{1,0:T(8,128)(2,1)S(1)}, u32[]{:S(2)}, u32[]{:S(2)}) collective-permute-start(bf16[24,4096]{1,0:T(8,128)(2,1)S(1)} %pad_maximum_fusion.4), channel_id=1, source_target_pairs={{0,4},{4,0},{8,12},{12,8},{16,20},{20,16},{24,28},{28,24},{1,5},{5... | collective-permute-start | bytes 589832 | tf_op jit(solution)/shard_map/ppermute | solution.py:24
  20.9 2.2 %collective-permute-start.6 = (bf16[24,5120]{1,0:T(8,128)(2,1)S(1)}, bf16[24,5120]{1,0:T(8,128)(2,1)S(1)}, u32[]{:S(2)}, u32[]{:S(2)}) collective-permute-start(bf16[24,5120]{1,0:T(8,128)(2,1)S(1)} %pad_maximum_fusion.3), channel_id=1, source_target_pairs={{0,4},{4,0},{8,12},{12,8},{16,20},{20,16},{24,28},{28,24},{1,5},{5... | collective-permute-start | bytes 737288 | tf_op jit(solution)/shard_map/ppermute | solution.py:24
  36.2 1.6 %collective-permute-start.8 = (bf16[24,5120]{1,0:T(8,128)(2,1)S(1)}, bf16[24,5120]{1,0:T(8,128)(2,1)S(1)}, u32[]{:S(2)}, u32[]{:S(2)}) collective-permute-start(bf16[24,5120]{1,0:T(8,128)(2,1)S(1)} %convolution_convert_fusion.1), channel_id=1, source_target_pairs={{0,4},{4,0},{8,12},{12,8},{16,20},{20,16},{24,28},{28,24},{1,5},{5... | collective-permute-start | bytes 737288 | tf_op jit(solution)/shard_map/ppermute | solution.py:24
  37.8 5.7 %collective-permute-start.9 = (bf16[24,1280]{1,0:T(8,128)(2,1)S(1)}, bf16[24,1280]{1,0:T(8,128)(2,1)S(1)}, u32[]{:S(2)}, u32[]{:S(2)}) collective-permute-start(bf16[24,1280]{1,0:T(8,128)(2,1)S(1)} %get-tuple-element.11), channel_id=1, source_target_pairs={{0,3},{1,2},{2,1},{3,0},{4,7},{5,6},{6,5},{7,4},{8,11},{9,10},{10,... | collective-permute-start | bytes 184328 | tf_op jit(solution)/shard_map/ppermute | solution.py:24
  38.5 5.1 %collective-permute-start.10 = (bf16[24,1280]{1,0:T(8,128)(2,1)S(1)}, bf16[24,1280]{1,0:T(8,128)(2,1)S(1)}, u32[]{:S(2)}, u32[]{:S(2)}) collective-permute-start(bf16[24,1280]{1,0:T(8,128)(2,1)S(1)} %get-tuple-element.12), channel_id=1, source_target_pairs={{0,2},{1,3},{2,0},{3,1},{4,6},{5,7},{6,4},{7,5},{8,10},{9,11},{10,... | collective-permute-start | bytes 184328 | tf_op jit(solution)/shard_map/ppermute | solution.py:24
  39.8 4.2 %collective-permute-start.11 = (bf16[24,1280]{1,0:T(8,128)(2,1)S(1)}, bf16[24,1280]{1,0:T(8,128)(2,1)S(1)}, u32[]{:S(2)}, u32[]{:S(2)}) collective-permute-start(bf16[24,1280]{1,0:T(8,128)(2,1)S(1)} %get-tuple-element.13), channel_id=1, source_target_pairs={{0,1},{1,0},{2,3},{3,2},{4,5},{5,4},{6,7},{7,6},{8,9},{9,8},{10,11... | collective-permute-start | bytes 184328 | tf_op jit(solution)/shard_map/ppermute | solution.py:24
  44.1 5.6 %collective-permute-start.12 = (bf16[6,1280]{1,0:T(8,128)(2,1)S(1)}, bf16[6,1280]{1,0:T(8,128)(2,1)S(1)}, u32[]{:S(2)}, u32[]{:S(2)}) collective-permute-start(bf16[6,1280]{1,0:T(8,128)(2,1)S(1)} %get-tuple-element.26), channel_id=1, source_target_pairs={{0,24},{4,28},{8,16},{12,20},{16,8},{20,12},{24,0},{28,4},{1,25},{... | collective-permute-start | bytes 46088 | tf_op jit(solution)/shard_map/ppermute | solution.py:24
  44.8 5.0 %collective-permute-start.13 = (bf16[6,1280]{1,0:T(8,128)(2,1)S(1)}, bf16[6,1280]{1,0:T(8,128)(2,1)S(1)}, u32[]{:S(2)}, u32[]{:S(2)}) collective-permute-start(bf16[6,1280]{1,0:T(8,128)(2,1)S(1)} %get-tuple-element.27), channel_id=1, source_target_pairs={{0,16},{4,20},{8,24},{12,28},{16,0},{20,4},{24,8},{28,12},{1,17},{... | collective-permute-start | bytes 46088 | tf_op jit(solution)/shard_map/ppermute | solution.py:24
  46.2 4.1 %collective-permute-start.14 = (bf16[6,1280]{1,0:T(8,128)(2,1)S(1)}, bf16[6,1280]{1,0:T(8,128)(2,1)S(1)}, u32[]{:S(2)}, u32[]{:S(2)}) collective-permute-start(bf16[6,1280]{1,0:T(8,128)(2,1)S(1)} %get-tuple-element.28), channel_id=1, source_target_pairs={{0,8},{4,12},{8,0},{12,4},{16,24},{20,28},{24,16},{28,20},{1,9},{5... | collective-permute-start | bytes 46088 | tf_op jit(solution)/shard_map/ppermute | solution.py:24

commit v6 on v4

--- a/solution.py
+++ b/solution.py
@@ -31,7 +31,8 @@
             j: swap(value, axis, size, mask_of(j, group))
             for j in reversed(range(1, 1 << len(group)))
         }
-        parts = [value] + [landed[j] for j in range(1, 1 << len(group))]
+        parts = lax.optimization_barrier([landed[j] for j in range(1, 1 << len(group))])
+        parts = [value] + list(parts)
         value = jnp.concatenate(reorder(parts, index, group), axis=dim)
     return value
 
@@ -86,10 +87,10 @@
         other_total = jnp.sum(jnp.exp(teacher_logits - other_peak[:, None]), axis=1)
         lanes = -(-tokens // 64) * 64
         stats = jnp.stack([
-            peak + jnp.log(total),
+            peak,
+            total,
             weighted / total,
             other_peak + jnp.log(other_total),
-            jnp.zeros_like(peak),
         ])
         stats = jnp.pad(stats, ((0, 0), (0, lanes - tokens))).reshape(2, 2 * lanes)
         devices = dp * vocab
@@ -97,18 +98,18 @@
             jnp.broadcast_to(stats[None], (devices,) + stats.shape),
             ("dp", "vocab"), 0, 0, tiled=True,
         )
-        each_lse = every[:, 0, :tokens]
-        each_mean = every[:, 0, lanes : lanes + tokens]
-        each_other = every[:, 1, :tokens]
-
-        def joined(each):
-            top = jnp.max(each, axis=0)
-            return top + jnp.log(jnp.sum(jnp.exp(each - top), axis=0))
-
-        student_lse = joined(each_lse)
-        teacher_lse = joined(each_other)[:, None]
-        mean = jnp.sum(jnp.exp(each_lse - student_lse) * each_mean, axis=0)[:, None]
-        student_lse = student_lse[:, None]
+        each_peak = every[:, 0, :tokens]
+        each_total = every[:, 0, lanes : lanes + tokens]
+        each_mean = every[:, 1, :tokens]
+        each_other = every[:, 1, lanes : lanes + tokens]
+        top = jnp.max(each_peak, axis=0)
+        each_total = each_total * jnp.exp(each_peak - top)
+        total_all = jnp.sum(each_total, axis=0)
+        mean = (jnp.sum(each_total * each_mean, axis=0) / total_all)[:, None]
+        student_lse = (top + jnp.log(total_all))[:, None]
+        other_top = jnp.max(each_other, axis=0)
+        other_all = jnp.sum(jnp.exp(each_other - other_top), axis=0)
+        teacher_lse = (other_top + jnp.log(other_all))[:, None]
         divergence = mean - student_lse + teacher_lse
         log_student = student_logits - student_lse
         probs = jnp.exp(log_student)

time: 50.4 us -> 49.6 us (0.984)
  blocking collectives: 11.1 us -> 10.4 us
    all_to_all x1, blocking collectives: 11.1 us -> 10.4 us  [on_device(): lax.all_to_all(jnp.broadcast_to(stats[None], (devices,) + stats.shape), (...]
  transfers between devices with their start and end apart: 14 -> 14, of which waited for: 12 -> 12; matrix products, arithmetic and copies ran while one was open for 5% -> 4% of each run, Pallas kernels for 0% -> 0%
where the time goes in v6:
time: 49.6 us; the launch traced here: 49.5 us
  starting transfers between devices  17.5 us (35%)
  waiting for transfers between devices  13.9 us (28%)
  blocking collectives  10.4 us (21%)
  matrix products  4.04 us (8%)
  other arithmetic  2.57 us (5%)
  between operations  0.81 us (2%)
    ppermute x14, starting transfers between devices, swap(): return lax.ppermute(value, axis, [(i, i ^ mask) for i in range(size)])  17.5 us
    ppermute x14, waiting for transfers between devices, swap(): return lax.ppermute(value, axis, [(i, i ^ mask) for i in range(size)])  13.9 us
    all_to_all x1, blocking collectives, on_device(): lax.all_to_all(jnp.broadcast_to(stats[None], (devices,) + stats.shape), (...  10.4 us
    dot_general x1, matrix products, on_device(): lax.dot_general(logit_grad, student_full, (((0,), (0,)), ((), ())), prefe...  1.87 us
  transfers between devices with their start and end apart: 14, of which 12 were waited for; matrix products, arithmetic and copies ran while one was open for 4% of the time, Pallas kernels for 0%

profile of v6, /device:TPU:0, one launch (start us, length us, event | category | flops | bytes accessed | tf_op | source)
XLA Modules:
  0.0 49.5 jit_solution(984798203805693148)
XLA Ops:
  0.6 0.0 copy-start
  0.7 0.9 %pad_select_fusion = bf16[6,2304]{1,0:T(8,128)(2,1)S(1)} fusion(bf16[6,1024]{1,0:T(8,128)(2,1)} %param.5, bf16[6,1280]{1,0:T(8,128)(2,1)} %param.4, pred[2304]{0:T(1024)(128)(4,1)S(1)} %iota_compare_fusion), kind=kLoop, calls=%fused_computation.76 | loop fusion | flops 13824 | bytes 57600 | tf_op jit(solution)/shard_map/jit(_where)/select_n | solution.py:64
  1.6 5.1 %collective-permute-start.2 = (bf16[6,2304]{1,0:T(8,128)(2,1)S(1)}, bf16[6,2304]{1,0:T(8,128)(2,1)S(1)}, u32[]{:S(2)}, u32[]{:S(2)}) collective-permute-start(bf16[6,2304]{1,0:T(8,128)(2,1)S(1)} %pad_select_fusion), channel_id=1, source_target_pairs={{0,24},{4,28},{8,16},{12,20},{16,8},{20,12},{24,0},{28,4},{1,25},{... | collective-permute-start | bytes 82952 | tf_op jit(solution)/shard_map/ppermute | solution.py:24
  6.7 0.0 collective-permute-start.1
  6.7 0.6 %collective-permute-start = (bf16[6,2304]{1,0:T(8,128)(2,1)S(1)}, bf16[6,2304]{1,0:T(8,128)(2,1)S(1)}, u32[]{:S(2)}, u32[]{:S(2)}) collective-permute-start(bf16[6,2304]{1,0:T(8,128)(2,1)S(1)} %pad_select_fusion), channel_id=1, source_target_pairs={{0,8},{4,12},{8,0},{12,4},{16,24},{20,28},{24,16},{28,20},{1,9},{5... | collective-permute-start | bytes 82952 | tf_op jit(solution)/shard_map/ppermute | solution.py:24
  7.3 1.3 %collective-permute-done.2 = bf16[6,2304]{1,0:T(8,128)(2,1)S(1)} collective-permute-done((bf16[6,2304]{1,0:T(8,128)(2,1)S(1)}, bf16[6,2304]{1,0:T(8,128)(2,1)S(1)}, u32[]{:S(2)}, u32[]{:S(2)}) %collective-permute-start.2) | collective-permute-done | bytes 27680 | tf_op jit(solution)/shard_map/ppermute | solution.py:24
  8.6 2.9 %collective-permute-done.1 = bf16[6,2304]{1,0:T(8,128)(2,1)S(1)} collective-permute-done((bf16[6,2304]{1,0:T(8,128)(2,1)S(1)}, bf16[6,2304]{1,0:T(8,128)(2,1)S(1)}, u32[]{:S(2)}, u32[]{:S(2)}) %collective-permute-start.1) | collective-permute-done | bytes 27680 | tf_op jit(solution)/shard_map/ppermute | solution.py:24
  11.5 0.0 collective-permute-done
  11.6 0.1 maximum_bitcast_fusion
  11.6 2.5 %collective-permute-start.5 = (bf16[1,24,2304]{2,1,0:T(8,128)(2,1)S(1)}, bf16[1,24,2304]{2,1,0:T(8,128)(2,1)S(1)}, u32[]{:S(2)}, u32[]{:S(2)}) collective-permute-start(bf16[1,24,2304]{2,1,0:T(8,128)(2,1)S(1)} %maximum_bitcast_fusion), channel_id=1, source_target_pairs={{0,3},{1,2},{2,1},{3,0},{4,7},{5,6},{6,5},{7,4},{8,11},{9,10},{10,... | collective-permute-start | bytes 331784 | tf_op jit(solution)/shard_map/ppermute | solution.py:24
  14.1 0.5 %collective-permute-start.4 = (bf16[1,24,2304]{2,1,0:T(8,128)(2,1)S(1)}, bf16[1,24,2304]{2,1,0:T(8,128)(2,1)S(1)}, u32[]{:S(2)}, u32[]{:S(2)}) collective-permute-start(bf16[1,24,2304]{2,1,0:T(8,128)(2,1)S(1)} %maximum_bitcast_fusion), channel_id=1, source_target_pairs={{0,2},{1,3},{2,0},{3,1},{4,6},{5,7},{6,4},{7,5},{8,10},{9,11},{10,... | collective-permute-start | bytes 331784 | tf_op jit(solution)/shard_map/ppermute | solution.py:24
  14.6 0.5 %collective-permute-start.3 = (bf16[1,24,2304]{2,1,0:T(8,128)(2,1)S(1)}, bf16[1,24,2304]{2,1,0:T(8,128)(2,1)S(1)}, u32[]{:S(2)}, u32[]{:S(2)}) collective-permute-start(bf16[1,24,2304]{2,1,0:T(8,128)(2,1)S(1)} %maximum_bitcast_fusion), channel_id=1, source_target_pairs={{0,1},{1,0},{2,3},{3,2},{4,5},{5,4},{6,7},{7,6},{8,9},{9,8},{10,11... | collective-permute-start | bytes 331784 | tf_op jit(solution)/shard_map/ppermute | solution.py:24
  15.2 3.3 %collective-permute-done.5 = bf16[1,24,2304]{2,1,0:T(8,128)(2,1)S(1)} collective-permute-done((bf16[1,24,2304]{2,1,0:T(8,128)(2,1)S(1)}, bf16[1,24,2304]{2,1,0:T(8,128)(2,1)S(1)}, u32[]{:S(2)}, u32[]{:S(2)}) %collective-permute-start.5) | collective-permute-done | bytes 110624 | tf_op jit(solution)/shard_map/ppermute | solution.py:24
  18.5 0.8 %collective-permute-done.4 = bf16[1,24,2304]{2,1,0:T(8,128)(2,1)S(1)} collective-permute-done((bf16[1,24,2304]{2,1,0:T(8,128)(2,1)S(1)}, bf16[1,24,2304]{2,1,0:T(8,128)(2,1)S(1)}, u32[]{:S(2)}, u32[]{:S(2)}) %collective-permute-start.4) | collective-permute-done | bytes 110624 | tf_op jit(solution)/shard_map/ppermute | solution.py:24
  19.3 0.1 collective-permute-done.3
  19.4 0.1 broadcast_select_fusion.9
  19.5 0.1 pad_maximum_fusion.1
  19.6 0.1 collective-permute-start.6
  19.7 0.0 copy-start.1
  19.7 1.8 %collective-permute-done.6 = bf16[4,24,2304]{2,1,0:T(8,128)(2,1)S(1)} collective-permute-done((bf16[4,24,2304]{2,1,0:T(8,128)(2,1)S(1)}, bf16[4,24,2304]{2,1,0:T(8,128)(2,1)S(1)}, u32[]{:S(2)}, u32[]{:S(2)}) %collective-permute-start.6) | collective-permute-done | bytes 442400 | tf_op jit(solution)/shard_map/ppermute | solution.py:24
  21.5 0.1 broadcast_select_fusion.1
  21.7 0.0 copy-done.1
  21.7 0.7 %fusion.39 = (f32[48]{0:T(128)S(1)}, f32[48,176]{1,0:T(8,128)S(1)}) fusion(bf16[176,4096]{1,0:T(8,128)(2,1)S(1)} %copy-done.1, bf16[48,1024]{1,0:T(8,128)(2,1)S(1)} %get-tuple-element.31, bf16[48,1024]{1,0:T(8,128)(2,1)S(1)} %get-tuple-element.32, bf16[48,1024]{1,0:T(8,128)(2,1)S(1)} %get-tuple-element.30, bf16[48,1024]{1,0:T(8,128)(2,1)S(1)} %get-tuple-element.29), kind=kOutput, calls=%fused_computation.112 | convolution fusion | flops 70787280 | bytes 1868992 | tf_op jit(solution)/shard_map/dot_general | solution.py:79
  22.3 0.0 copy-done
  22.4 0.8 %fusion.40 = (f32[48]{0:T(128)S(1)}, f32[48,176]{1,0:T(8,128)S(1)}) fusion(bf16[176,5120]{1,0:T(8,128)(2,1)S(1)} %copy-done, bf16[48,1280]{1,0:T(8,128)(2,1)S(1)} %get-tuple-element.28, bf16[48,1280]{1,0:T(8,128)(2,1)S(1)} %get-tuple-element.27, bf16[48,1280]{1,0:T(8,128)(2,1)S(1)} %get-tuple-element.26, bf16[48,1280]{1,0:T(8,128)(2,1)S(1)} %get-tuple-element.25), kind=kOutput, calls=%fused_computation.113 | convolution fusion | flops 88482000 | bytes 2327744 | tf_op jit(solution)/shard_map/dot_general | solution.py:76
  23.1 0.2 fusion.24
  23.4 0.1 broadcast_in_dim.7
  23.5 10.4 %all_to_all.5 = f32[32,2,128]{2,1,0:T(2,128)S(1)} all-to-all(f32[32,2,128]{2,1,0:T(2,128)S(1)} %broadcast_in_dim.8), channel_id=1, replica_groups=mesh['dp'=8,'vocab'=4] {'dp','vocab'}, dimensions={0} | all-to-all | bytes 65536 | tf_op jit(solution)/shard_map/all_to_all | solution.py:97
  34.0 0.1 fusion.38
  34.2 0.1 multiply_convert_fusion
  34.3 0.3 convolution_convert_fusion.1
  34.6 0.1 collective-permute-start.7
  34.7 0.4 fusion.26
  35.1 1.1 %collective-permute-done.7 = bf16[24,5120]{1,0:T(8,128)(2,1)S(1)} collective-permute-done((bf16[24,5120]{1,0:T(8,128)(2,1)S(1)}, bf16[24,5120]{1,0:T(8,128)(2,1)S(1)}, u32[]{:S(2)}, u32[]{:S(2)}) %collective-permute-start.7) | collective-permute-done | bytes 245792 | tf_op jit(solution)/shard_map/ppermute | solution.py:24
  36.3 0.7 %collective-permute-start.8 = (bf16[24,1280]{1,0:T(8,128)(2,1)S(1)}, bf16[24,1280]{1,0:T(8,128)(2,1)S(1)}, u32[]{:S(2)}, u32[]{:S(2)}) collective-permute-start(bf16[24,1280]{1,0:T(8,128)(2,1)S(1)} %get-tuple-element.35), channel_id=1, source_target_pairs={{0,3},{1,2},{2,1},{3,0},{4,7},{5,6},{6,5},{7,4},{8,11},{9,10},{10,... | collective-permute-start | bytes 184328 | tf_op jit(solution)/shard_map/ppermute | solution.py:24
  37.0 1.3 %collective-permute-start.9 = (bf16[24,1280]{1,0:T(8,128)(2,1)S(1)}, bf16[24,1280]{1,0:T(8,128)(2,1)S(1)}, u32[]{:S(2)}, u32[]{:S(2)}) collective-permute-start(bf16[24,1280]{1,0:T(8,128)(2,1)S(1)} %get-tuple-element.36), channel_id=1, source_target_pairs={{0,2},{1,3},{2,0},{3,1},{4,6},{5,7},{6,4},{7,5},{8,10},{9,11},{10,... | collective-permute-start | bytes 184328 | tf_op jit(solution)/shard_map/ppermute | solution.py:24
  38.3 1.5 %collective-permute-start.10 = (bf16[24,1280]{1,0:T(8,128)(2,1)S(1)}, bf16[24,1280]{1,0:T(8,128)(2,1)S(1)}, u32[]{:S(2)}, u32[]{:S(2)}) collective-permute-start(bf16[24,1280]{1,0:T(8,128)(2,1)S(1)} %get-tuple-element.37), channel_id=1, source_target_pairs={{0,1},{1,0},{2,3},{3,2},{4,5},{5,4},{6,7},{7,6},{8,9},{9,8},{10,11... | collective-permute-start | bytes 184328 | tf_op jit(solution)/shard_map/ppermute | solution.py:24
  39.9 1.9 %convolution_convert_fusion = bf16[176,5120]{1,0:T(8,128)(2,1)} fusion(bf16[48,176]{1,0:T(8,128)(2,1)S(1)} %multiply_convert_fusion, bf16[48,1280]{1,0:T(8,128)(2,1)S(1)} %get-tuple-element.28, bf16[48,1280]{1,0:T(8,128)(2,1)S(1)} %get-tuple-element.27, bf16[48,1280]{1,0:T(8,128)(2,1)S(1)} %get-tuple-element.26, bf16[48,1280]{1,0:T(8,128)(2,1)S(1)} %get-tuple-element.25), kind=kOutput, calls=%fused_computation | convolution fusion | flops 89374720 | bytes 2310656 | tf_op jit(solution)/shard_map/dot_general | solution.py:128
  41.7 0.3 collective-permute-done.8
  42.0 0.1 collective-permute-done.9
  42.1 0.5 collective-permute-done.10
  42.5 0.1 convert_add_fusion.1
  42.6 0.7 %collective-permute-start.11 = (bf16[6,1280]{1,0:T(8,128)(2,1)S(1)}, bf16[6,1280]{1,0:T(8,128)(2,1)S(1)}, u32[]{:S(2)}, u32[]{:S(2)}) collective-permute-start(bf16[6,1280]{1,0:T(8,128)(2,1)S(1)} %get-tuple-element.46), channel_id=1, source_target_pairs={{0,24},{4,28},{8,16},{12,20},{16,8},{20,12},{24,0},{28,4},{1,25},{... | collective-permute-start | bytes 46088 | tf_op jit(solution)/shard_map/ppermute | solution.py:24
  43.3 1.4 %collective-permute-start.12 = (bf16[6,1280]{1,0:T(8,128)(2,1)S(1)}, bf16[6,1280]{1,0:T(8,128)(2,1)S(1)}, u32[]{:S(2)}, u32[]{:S(2)}) collective-permute-start(bf16[6,1280]{1,0:T(8,128)(2,1)S(1)} %get-tuple-element.47), channel_id=1, source_target_pairs={{0,16},{4,20},{8,24},{12,28},{16,0},{20,4},{24,8},{28,12},{1,17},{... | collective-permute-start | bytes 46088 | tf_op jit(solution)/shard_map/ppermute | solution.py:24
  44.7 2.3 %collective-permute-start.13 = (bf16[6,1280]{1,0:T(8,128)(2,1)S(1)}, bf16[6,1280]{1,0:T(8,128)(2,1)S(1)}, u32[]{:S(2)}, u32[]{:S(2)}) collective-permute-start(bf16[6,1280]{1,0:T(8,128)(2,1)S(1)} %get-tuple-element.48), channel_id=1, source_target_pairs={{0,8},{4,12},{8,0},{12,4},{16,24},{20,28},{24,16},{28,20},{1,9},{5... | collective-permute-start | bytes 46088 | tf_op jit(solution)/shard_map/ppermute | solution.py:24
  47.1 1.2 %collective-permute-done.11 = bf16[6,1280]{1,0:T(8,128)(2,1)S(1)} collective-permute-done((bf16[6,1280]{1,0:T(8,128)(2,1)S(1)}, bf16[6,1280]{1,0:T(8,128)(2,1)S(1)}, u32[]{:S(2)}, u32[]{:S(2)}) %collective-permute-start.11) | collective-permute-done | bytes 15392 | tf_op jit(solution)/shard_map/ppermute | solution.py:24
  48.3 0.0 collective-permute-done.12
  48.3 0.6 %collective-permute-done.13 = bf16[6,1280]{1,0:T(8,128)(2,1)S(1)} collective-permute-done((bf16[6,1280]{1,0:T(8,128)(2,1)S(1)}, bf16[6,1280]{1,0:T(8,128)(2,1)S(1)}, u32[]{:S(2)}, u32[]{:S(2)}) %collective-permute-start.13) | collective-permute-done | bytes 15392 | tf_op jit(solution)/shard_map/ppermute | solution.py:24
  48.8 0.6 %add_convert_fusion = bf16[6,1280]{1,0:T(8,128)(2,1)} fusion(bf16[6,1280]{1,0:T(8,128)(2,1)S(1)} %collective-permute-done.13, bf16[6,1280]{1,0:T(8,128)(2,1)S(1)} %collective-permute-done.12, bf16[6,1280]{1,0:T(8,128)(2,1)S(1)} %collective-permute-done.11, pred[]{:T(512)S(6)} %eq.20, f32[24,1280]{1,0:T(8,128)S(1)} %convert_add_fusion.1, pred[]{:T(512)S(6)} %eq.21), kind=kLoop, calls=%fused_computation.68 | loop fusion | flops 76800 | bytes 184322 | tf_op jit(solution)/shard_map/convert_element_type | solution.py:134
  (15 shorter events, 0.3 us)
Async XLA Ops:
  0.6 21.7 %copy-start = (bf16[176,5120]{1,0:T(8,128)(2,1)S(1)}, bf16[176,5120]{1,0:T(8,128)(2,1)}, u32[]{:S(2)}) copy-start(bf16[176,5120]{1,0:T(8,128)(2,1)} %param.6) | copy-start | bytes 5406724
  1.6 7.1 %collective-permute-start.2 = (bf16[6,2304]{1,0:T(8,128)(2,1)S(1)}, bf16[6,2304]{1,0:T(8,128)(2,1)S(1)}, u32[]{:S(2)}, u32[]{:S(2)}) collective-permute-start(bf16[6,2304]{1,0:T(8,128)(2,1)S(1)} %pad_select_fusion), channel_id=1, source_target_pairs={{0,24},{4,28},{8,16},{12,20},{16,8},{20,12},{24,0},{28,4},{1,25},{... | collective-permute-start | bytes 82952 | tf_op jit(solution)/shard_map/ppermute | solution.py:24
  6.7 4.9 %collective-permute-start.1 = (bf16[6,2304]{1,0:T(8,128)(2,1)S(1)}, bf16[6,2304]{1,0:T(8,128)(2,1)S(1)}, u32[]{:S(2)}, u32[]{:S(2)}) collective-permute-start(bf16[6,2304]{1,0:T(8,128)(2,1)S(1)} %pad_select_fusion), channel_id=1, source_target_pairs={{0,16},{4,20},{8,24},{12,28},{16,0},{20,4},{24,8},{28,12},{1,17},{... | collective-permute-start | bytes 82952 | tf_op jit(solution)/shard_map/ppermute | solution.py:24
  6.7 4.9 %collective-permute-start = (bf16[6,2304]{1,0:T(8,128)(2,1)S(1)}, bf16[6,2304]{1,0:T(8,128)(2,1)S(1)}, u32[]{:S(2)}, u32[]{:S(2)}) collective-permute-start(bf16[6,2304]{1,0:T(8,128)(2,1)S(1)} %pad_select_fusion), channel_id=1, source_target_pairs={{0,8},{4,12},{8,0},{12,4},{16,24},{20,28},{24,16},{28,20},{1,9},{5... | collective-permute-start | bytes 82952 | tf_op jit(solution)/shard_map/ppermute | solution.py:24
  11.6 6.9 %collective-permute-start.5 = (bf16[1,24,2304]{2,1,0:T(8,128)(2,1)S(1)}, bf16[1,24,2304]{2,1,0:T(8,128)(2,1)S(1)}, u32[]{:S(2)}, u32[]{:S(2)}) collective-permute-start(bf16[1,24,2304]{2,1,0:T(8,128)(2,1)S(1)} %maximum_bitcast_fusion), channel_id=1, source_target_pairs={{0,3},{1,2},{2,1},{3,0},{4,7},{5,6},{6,5},{7,4},{8,11},{9,10},{10,... | collective-permute-start | bytes 331784 | tf_op jit(solution)/shard_map/ppermute | solution.py:24
  14.1 5.2 %collective-permute-start.4 = (bf16[1,24,2304]{2,1,0:T(8,128)(2,1)S(1)}, bf16[1,24,2304]{2,1,0:T(8,128)(2,1)S(1)}, u32[]{:S(2)}, u32[]{:S(2)}) collective-permute-start(bf16[1,24,2304]{2,1,0:T(8,128)(2,1)S(1)} %maximum_bitcast_fusion), channel_id=1, source_target_pairs={{0,2},{1,3},{2,0},{3,1},{4,6},{5,7},{6,4},{7,5},{8,10},{9,11},{10,... | collective-permute-start | bytes 331784 | tf_op jit(solution)/shard_map/ppermute | solution.py:24
  14.6 4.7 %collective-permute-start.3 = (bf16[1,24,2304]{2,1,0:T(8,128)(2,1)S(1)}, bf16[1,24,2304]{2,1,0:T(8,128)(2,1)S(1)}, u32[]{:S(2)}, u32[]{:S(2)}) collective-permute-start(bf16[1,24,2304]{2,1,0:T(8,128)(2,1)S(1)} %maximum_bitcast_fusion), channel_id=1, source_target_pairs={{0,1},{1,0},{2,3},{3,2},{4,5},{5,4},{6,7},{7,6},{8,9},{9,8},{10,11... | collective-permute-start | bytes 331784 | tf_op jit(solution)/shard_map/ppermute | solution.py:24
  19.6 1.9 %collective-permute-start.6 = (bf16[4,24,2304]{2,1,0:T(8,128)(2,1)S(1)}, bf16[4,24,2304]{2,1,0:T(8,128)(2,1)S(1)}, u32[]{:S(2)}, u32[]{:S(2)}) collective-permute-start(bf16[4,24,2304]{2,1,0:T(8,128)(2,1)S(1)} %pad_maximum_fusion.1), channel_id=1, source_target_pairs={{0,4},{4,0},{8,12},{12,8},{16,20},{20,16},{24,28},{28,24},{1,5},{5... | collective-permute-start | bytes 1327112 | tf_op jit(solution)/shard_map/ppermute | solution.py:24
  19.7 2.0 %copy-start.1 = (bf16[176,4096]{1,0:T(8,128)(2,1)S(1)}, bf16[176,4096]{1,0:T(8,128)(2,1)}, u32[]{:S(2)}) copy-start(bf16[176,4096]{1,0:T(8,128)(2,1)} %param.7) | copy-start | bytes 4325380
  34.6 1.6 %collective-permute-start.7 = (bf16[24,5120]{1,0:T(8,128)(2,1)S(1)}, bf16[24,5120]{1,0:T(8,128)(2,1)S(1)}, u32[]{:S(2)}, u32[]{:S(2)}) collective-permute-start(bf16[24,5120]{1,0:T(8,128)(2,1)S(1)} %convolution_convert_fusion.1), channel_id=1, source_target_pairs={{0,4},{4,0},{8,12},{12,8},{16,20},{20,16},{24,28},{28,24},{1,5},{5... | collective-permute-start | bytes 737288 | tf_op jit(solution)/shard_map/ppermute | solution.py:24
  36.3 5.7 %collective-permute-start.8 = (bf16[24,1280]{1,0:T(8,128)(2,1)S(1)}, bf16[24,1280]{1,0:T(8,128)(2,1)S(1)}, u32[]{:S(2)}, u32[]{:S(2)}) collective-permute-start(bf16[24,1280]{1,0:T(8,128)(2,1)S(1)} %get-tuple-element.35), channel_id=1, source_target_pairs={{0,3},{1,2},{2,1},{3,0},{4,7},{5,6},{6,5},{7,4},{8,11},{9,10},{10,... | collective-permute-start | bytes 184328 | tf_op jit(solution)/shard_map/ppermute | solution.py:24
  37.0 5.1 %collective-permute-start.9 = (bf16[24,1280]{1,0:T(8,128)(2,1)S(1)}, bf16[24,1280]{1,0:T(8,128)(2,1)S(1)}, u32[]{:S(2)}, u32[]{:S(2)}) collective-permute-start(bf16[24,1280]{1,0:T(8,128)(2,1)S(1)} %get-tuple-element.36), channel_id=1, source_target_pairs={{0,2},{1,3},{2,0},{3,1},{4,6},{5,7},{6,4},{7,5},{8,10},{9,11},{10,... | collective-permute-start | bytes 184328 | tf_op jit(solution)/shard_map/ppermute | solution.py:24
  38.3 4.2 %collective-permute-start.10 = (bf16[24,1280]{1,0:T(8,128)(2,1)S(1)}, bf16[24,1280]{1,0:T(8,128)(2,1)S(1)}, u32[]{:S(2)}, u32[]{:S(2)}) collective-permute-start(bf16[24,1280]{1,0:T(8,128)(2,1)S(1)} %get-tuple-element.37), channel_id=1, source_target_pairs={{0,1},{1,0},{2,3},{3,2},{4,5},{5,4},{6,7},{7,6},{8,9},{9,8},{10,11... | collective-permute-start | bytes 184328 | tf_op jit(solution)/shard_map/ppermute | solution.py:24
  42.6 5.6 %collective-permute-start.11 = (bf16[6,1280]{1,0:T(8,128)(2,1)S(1)}, bf16[6,1280]{1,0:T(8,128)(2,1)S(1)}, u32[]{:S(2)}, u32[]{:S(2)}) collective-permute-start(bf16[6,1280]{1,0:T(8,128)(2,1)S(1)} %get-tuple-element.46), channel_id=1, source_target_pairs={{0,24},{4,28},{8,16},{12,20},{16,8},{20,12},{24,0},{28,4},{1,25},{... | collective-permute-start | bytes 46088 | tf_op jit(solution)/shard_map/ppermute | solution.py:24
  43.3 5.0 %collective-permute-start.12 = (bf16[6,1280]{1,0:T(8,128)(2,1)S(1)}, bf16[6,1280]{1,0:T(8,128)(2,1)S(1)}, u32[]{:S(2)}, u32[]{:S(2)}) collective-permute-start(bf16[6,1280]{1,0:T(8,128)(2,1)S(1)} %get-tuple-element.47), channel_id=1, source_target_pairs={{0,16},{4,20},{8,24},{12,28},{16,0},{20,4},{24,8},{28,12},{1,17},{... | collective-permute-start | bytes 46088 | tf_op jit(solution)/shard_map/ppermute | solution.py:24
  44.7 4.1 %collective-permute-start.13 = (bf16[6,1280]{1,0:T(8,128)(2,1)S(1)}, bf16[6,1280]{1,0:T(8,128)(2,1)S(1)}, u32[]{:S(2)}, u32[]{:S(2)}) collective-permute-start(bf16[6,1280]{1,0:T(8,128)(2,1)S(1)} %get-tuple-element.48), channel_id=1, source_target_pairs={{0,8},{4,12},{8,0},{12,4},{16,24},{20,28},{24,16},{28,20},{1,9},{5... | collective-permute-start | bytes 46088 | tf_op jit(solution)/shard_map/ppermute | solution.py:24

commit v7 on v6

--- a/solution.py
+++ b/solution.py
@@ -37,14 +37,14 @@
     return value
 
 
-def scattered(total, axis, size, bits, dim):
+def scattered(total, axis, size, bits, dim, farthest_first=True):
     index = lax.axis_index(axis)
     for group in reversed(grouped(bits)):
         parts = reorder(jnp.split(total, 1 << len(group), axis=dim), index, group)
         total = parts[0]
         landed = [
             swap(parts[j].astype(jnp.bfloat16), axis, size, mask_of(j, group))
-            for j in reversed(range(1, 1 << len(group)))
+            for j in sorted(range(1, 1 << len(group)), reverse=farthest_first)
         ]
         for part in landed:
             total = total + part.astype(jnp.float32)
@@ -130,7 +130,7 @@
         ).astype(jnp.bfloat16)
         acc = scattered(acc, "vocab", vocab, vocab_bits, 1)
         acc, head_grad = lax.optimization_barrier((acc, head_grad))
-        acc = scattered(acc, "dp", dp, z_bits, 0)
+        acc = scattered(acc, "dp", dp, z_bits, 0, farthest_first=False)
         hidden_grad = acc.astype(jnp.bfloat16)
         return (hidden_grad, head_grad)
 

time: 49.6 us -> 50.3 us (1.014)
  waiting for transfers between devices: 13.9 us -> 14.5 us
    ppermute x14, waiting for transfers between devices: 13.9 us -> 14.5 us  [swap(): return lax.ppermute(value, axis, [(i, i ^ mask) for i in range(size)])]
where the time goes in v7:
time: 50.3 us; the launch traced here: 50.1 us
  starting transfers between devices  17.5 us (35%)
  waiting for transfers between devices  14.5 us (29%)
  blocking collectives  10.4 us (21%)
  matrix products  4.04 us (8%)
  other arithmetic  2.57 us (5%)
  between operations  0.81 us (2%)
    ppermute x14, starting transfers between devices, swap(): return lax.ppermute(value, axis, [(i, i ^ mask) for i in range(size)])  17.5 us
    ppermute x14, waiting for transfers between devices, swap(): return lax.ppermute(value, axis, [(i, i ^ mask) for i in range(size)])  14.5 us
    all_to_all x1, blocking collectives, on_device(): lax.all_to_all(jnp.broadcast_to(stats[None], (devices,) + stats.shape), (...  10.4 us
    dot_general x1, matrix products, on_device(): lax.dot_general(logit_grad, student_full, (((0,), (0,)), ((), ())), prefe...  1.87 us
  transfers between devices with their start and end apart: 14, of which 12 were waited for; matrix products, arithmetic and copies ran while one was open for 4% of the time, Pallas kernels for 0%

profile of v7, /device:TPU:0, one launch (start us, length us, event | category | flops | bytes accessed | tf_op | source)
XLA Modules:
  0.0 50.1 jit_solution(7672510789167926907)
XLA Ops:
  0.6 0.0 copy-start
  0.7 0.9 %pad_select_fusion = bf16[6,2304]{1,0:T(8,128)(2,1)S(1)} fusion(bf16[6,1024]{1,0:T(8,128)(2,1)} %param.5, bf16[6,1280]{1,0:T(8,128)(2,1)} %param.4, pred[2304]{0:T(1024)(128)(4,1)S(1)} %iota_compare_fusion), kind=kLoop, calls=%fused_computation.76 | loop fusion | flops 13824 | bytes 57600 | tf_op jit(solution)/shard_map/jit(_where)/select_n | solution.py:64
  1.6 5.1 %collective-permute-start.2 = (bf16[6,2304]{1,0:T(8,128)(2,1)S(1)}, bf16[6,2304]{1,0:T(8,128)(2,1)S(1)}, u32[]{:S(2)}, u32[]{:S(2)}) collective-permute-start(bf16[6,2304]{1,0:T(8,128)(2,1)S(1)} %pad_select_fusion), channel_id=1, source_target_pairs={{0,24},{4,28},{8,16},{12,20},{16,8},{20,12},{24,0},{28,4},{1,25},{... | collective-permute-start | bytes 82952 | tf_op jit(solution)/shard_map/ppermute | solution.py:24
  6.7 0.0 collective-permute-start.1
  6.7 0.6 %collective-permute-start = (bf16[6,2304]{1,0:T(8,128)(2,1)S(1)}, bf16[6,2304]{1,0:T(8,128)(2,1)S(1)}, u32[]{:S(2)}, u32[]{:S(2)}) collective-permute-start(bf16[6,2304]{1,0:T(8,128)(2,1)S(1)} %pad_select_fusion), channel_id=1, source_target_pairs={{0,8},{4,12},{8,0},{12,4},{16,24},{20,28},{24,16},{28,20},{1,9},{5... | collective-permute-start | bytes 82952 | tf_op jit(solution)/shard_map/ppermute | solution.py:24
  7.3 1.3 %collective-permute-done.2 = bf16[6,2304]{1,0:T(8,128)(2,1)S(1)} collective-permute-done((bf16[6,2304]{1,0:T(8,128)(2,1)S(1)}, bf16[6,2304]{1,0:T(8,128)(2,1)S(1)}, u32[]{:S(2)}, u32[]{:S(2)}) %collective-permute-start.2) | collective-permute-done | bytes 27680 | tf_op jit(solution)/shard_map/ppermute | solution.py:24
  8.6 2.9 %collective-permute-done.1 = bf16[6,2304]{1,0:T(8,128)(2,1)S(1)} collective-permute-done((bf16[6,2304]{1,0:T(8,128)(2,1)S(1)}, bf16[6,2304]{1,0:T(8,128)(2,1)S(1)}, u32[]{:S(2)}, u32[]{:S(2)}) %collective-permute-start.1) | collective-permute-done | bytes 27680 | tf_op jit(solution)/shard_map/ppermute | solution.py:24
  11.5 0.0 collective-permute-done
  11.6 0.1 maximum_bitcast_fusion
  11.6 2.5 %collective-permute-start.5 = (bf16[1,24,2304]{2,1,0:T(8,128)(2,1)S(1)}, bf16[1,24,2304]{2,1,0:T(8,128)(2,1)S(1)}, u32[]{:S(2)}, u32[]{:S(2)}) collective-permute-start(bf16[1,24,2304]{2,1,0:T(8,128)(2,1)S(1)} %maximum_bitcast_fusion), channel_id=1, source_target_pairs={{0,3},{1,2},{2,1},{3,0},{4,7},{5,6},{6,5},{7,4},{8,11},{9,10},{10,... | collective-permute-start | bytes 331784 | tf_op jit(solution)/shard_map/ppermute | solution.py:24
  14.1 0.5 %collective-permute-start.4 = (bf16[1,24,2304]{2,1,0:T(8,128)(2,1)S(1)}, bf16[1,24,2304]{2,1,0:T(8,128)(2,1)S(1)}, u32[]{:S(2)}, u32[]{:S(2)}) collective-permute-start(bf16[1,24,2304]{2,1,0:T(8,128)(2,1)S(1)} %maximum_bitcast_fusion), channel_id=1, source_target_pairs={{0,2},{1,3},{2,0},{3,1},{4,6},{5,7},{6,4},{7,5},{8,10},{9,11},{10,... | collective-permute-start | bytes 331784 | tf_op jit(solution)/shard_map/ppermute | solution.py:24
  14.6 0.5 %collective-permute-start.3 = (bf16[1,24,2304]{2,1,0:T(8,128)(2,1)S(1)}, bf16[1,24,2304]{2,1,0:T(8,128)(2,1)S(1)}, u32[]{:S(2)}, u32[]{:S(2)}) collective-permute-start(bf16[1,24,2304]{2,1,0:T(8,128)(2,1)S(1)} %maximum_bitcast_fusion), channel_id=1, source_target_pairs={{0,1},{1,0},{2,3},{3,2},{4,5},{5,4},{6,7},{7,6},{8,9},{9,8},{10,11... | collective-permute-start | bytes 331784 | tf_op jit(solution)/shard_map/ppermute | solution.py:24
  15.2 3.3 %collective-permute-done.5 = bf16[1,24,2304]{2,1,0:T(8,128)(2,1)S(1)} collective-permute-done((bf16[1,24,2304]{2,1,0:T(8,128)(2,1)S(1)}, bf16[1,24,2304]{2,1,0:T(8,128)(2,1)S(1)}, u32[]{:S(2)}, u32[]{:S(2)}) %collective-permute-start.5) | collective-permute-done | bytes 110624 | tf_op jit(solution)/shard_map/ppermute | solution.py:24
  18.5 0.8 %collective-permute-done.4 = bf16[1,24,2304]{2,1,0:T(8,128)(2,1)S(1)} collective-permute-done((bf16[1,24,2304]{2,1,0:T(8,128)(2,1)S(1)}, bf16[1,24,2304]{2,1,0:T(8,128)(2,1)S(1)}, u32[]{:S(2)}, u32[]{:S(2)}) %collective-permute-start.4) | collective-permute-done | bytes 110624 | tf_op jit(solution)/shard_map/ppermute | solution.py:24
  19.3 0.1 collective-permute-done.3
  19.4 0.1 broadcast_select_fusion.9
  19.5 0.1 pad_maximum_fusion.1
  19.6 0.1 collective-permute-start.6
  19.7 0.0 copy-start.1
  19.7 1.8 %collective-permute-done.6 = bf16[4,24,2304]{2,1,0:T(8,128)(2,1)S(1)} collective-permute-done((bf16[4,24,2304]{2,1,0:T(8,128)(2,1)S(1)}, bf16[4,24,2304]{2,1,0:T(8,128)(2,1)S(1)}, u32[]{:S(2)}, u32[]{:S(2)}) %collective-permute-start.6) | collective-permute-done | bytes 442400 | tf_op jit(solution)/shard_map/ppermute | solution.py:24
  21.5 0.1 broadcast_select_fusion.1
  21.7 0.0 copy-done.1
  21.7 0.7 %fusion.39 = (f32[48]{0:T(128)S(1)}, f32[48,176]{1,0:T(8,128)S(1)}) fusion(bf16[176,4096]{1,0:T(8,128)(2,1)S(1)} %copy-done.1, bf16[48,1024]{1,0:T(8,128)(2,1)S(1)} %get-tuple-element.31, bf16[48,1024]{1,0:T(8,128)(2,1)S(1)} %get-tuple-element.32, bf16[48,1024]{1,0:T(8,128)(2,1)S(1)} %get-tuple-element.30, bf16[48,1024]{1,0:T(8,128)(2,1)S(1)} %get-tuple-element.29), kind=kOutput, calls=%fused_computation.112 | convolution fusion | flops 70787280 | bytes 1868992 | tf_op jit(solution)/shard_map/dot_general | solution.py:79
  22.3 0.0 copy-done
  22.4 0.8 %fusion.40 = (f32[48]{0:T(128)S(1)}, f32[48,176]{1,0:T(8,128)S(1)}) fusion(bf16[176,5120]{1,0:T(8,128)(2,1)S(1)} %copy-done, bf16[48,1280]{1,0:T(8,128)(2,1)S(1)} %get-tuple-element.28, bf16[48,1280]{1,0:T(8,128)(2,1)S(1)} %get-tuple-element.27, bf16[48,1280]{1,0:T(8,128)(2,1)S(1)} %get-tuple-element.26, bf16[48,1280]{1,0:T(8,128)(2,1)S(1)} %get-tuple-element.25), kind=kOutput, calls=%fused_computation.113 | convolution fusion | flops 88482000 | bytes 2327744 | tf_op jit(solution)/shard_map/dot_general | solution.py:76
  23.1 0.2 fusion.24
  23.4 0.1 broadcast_in_dim.7
  23.5 10.4 %all_to_all.5 = f32[32,2,128]{2,1,0:T(2,128)S(1)} all-to-all(f32[32,2,128]{2,1,0:T(2,128)S(1)} %broadcast_in_dim.8), channel_id=1, replica_groups=mesh['dp'=8,'vocab'=4] {'dp','vocab'}, dimensions={0} | all-to-all | bytes 65536 | tf_op jit(solution)/shard_map/all_to_all | solution.py:97
  34.0 0.1 fusion.38
  34.2 0.1 multiply_convert_fusion
  34.3 0.3 convolution_convert_fusion.1
  34.6 0.1 collective-permute-start.7
  34.7 0.4 fusion.26
  35.1 1.1 %collective-permute-done.7 = bf16[24,5120]{1,0:T(8,128)(2,1)S(1)} collective-permute-done((bf16[24,5120]{1,0:T(8,128)(2,1)S(1)}, bf16[24,5120]{1,0:T(8,128)(2,1)S(1)}, u32[]{:S(2)}, u32[]{:S(2)}) %collective-permute-start.7) | collective-permute-done | bytes 245792 | tf_op jit(solution)/shard_map/ppermute | solution.py:24
  36.3 0.7 %collective-permute-start.8 = (bf16[24,1280]{1,0:T(8,128)(2,1)S(1)}, bf16[24,1280]{1,0:T(8,128)(2,1)S(1)}, u32[]{:S(2)}, u32[]{:S(2)}) collective-permute-start(bf16[24,1280]{1,0:T(8,128)(2,1)S(1)} %get-tuple-element.35), channel_id=1, source_target_pairs={{0,3},{1,2},{2,1},{3,0},{4,7},{5,6},{6,5},{7,4},{8,11},{9,10},{10,... | collective-permute-start | bytes 184328 | tf_op jit(solution)/shard_map/ppermute | solution.py:24
  37.0 1.3 %collective-permute-start.9 = (bf16[24,1280]{1,0:T(8,128)(2,1)S(1)}, bf16[24,1280]{1,0:T(8,128)(2,1)S(1)}, u32[]{:S(2)}, u32[]{:S(2)}) collective-permute-start(bf16[24,1280]{1,0:T(8,128)(2,1)S(1)} %get-tuple-element.36), channel_id=1, source_target_pairs={{0,2},{1,3},{2,0},{3,1},{4,6},{5,7},{6,4},{7,5},{8,10},{9,11},{10,... | collective-permute-start | bytes 184328 | tf_op jit(solution)/shard_map/ppermute | solution.py:24
  38.3 1.5 %collective-permute-start.10 = (bf16[24,1280]{1,0:T(8,128)(2,1)S(1)}, bf16[24,1280]{1,0:T(8,128)(2,1)S(1)}, u32[]{:S(2)}, u32[]{:S(2)}) collective-permute-start(bf16[24,1280]{1,0:T(8,128)(2,1)S(1)} %get-tuple-element.37), channel_id=1, source_target_pairs={{0,1},{1,0},{2,3},{3,2},{4,5},{5,4},{6,7},{7,6},{8,9},{9,8},{10,11... | collective-permute-start | bytes 184328 | tf_op jit(solution)/shard_map/ppermute | solution.py:24
  39.9 1.9 %convolution_convert_fusion = bf16[176,5120]{1,0:T(8,128)(2,1)} fusion(bf16[48,176]{1,0:T(8,128)(2,1)S(1)} %multiply_convert_fusion, bf16[48,1280]{1,0:T(8,128)(2,1)S(1)} %get-tuple-element.28, bf16[48,1280]{1,0:T(8,128)(2,1)S(1)} %get-tuple-element.27, bf16[48,1280]{1,0:T(8,128)(2,1)S(1)} %get-tuple-element.26, bf16[48,1280]{1,0:T(8,128)(2,1)S(1)} %get-tuple-element.25), kind=kOutput, calls=%fused_computation | convolution fusion | flops 89374720 | bytes 2310656 | tf_op jit(solution)/shard_map/dot_general | solution.py:128
  41.7 0.3 collective-permute-done.8
  42.0 0.1 collective-permute-done.9
  42.1 0.5 collective-permute-done.10
  42.5 0.1 convert_add_fusion.1
  42.6 0.7 %collective-permute-start.11 = (bf16[6,1280]{1,0:T(8,128)(2,1)S(1)}, bf16[6,1280]{1,0:T(8,128)(2,1)S(1)}, u32[]{:S(2)}, u32[]{:S(2)}) collective-permute-start(bf16[6,1280]{1,0:T(8,128)(2,1)S(1)} %get-tuple-element.46), channel_id=1, source_target_pairs={{0,8},{4,12},{8,0},{12,4},{16,24},{20,28},{24,16},{28,20},{1,9},{5... | collective-permute-start | bytes 46088 | tf_op jit(solution)/shard_map/ppermute | solution.py:24
  43.3 0.6 %collective-permute-start.12 = (bf16[6,1280]{1,0:T(8,128)(2,1)S(1)}, bf16[6,1280]{1,0:T(8,128)(2,1)S(1)}, u32[]{:S(2)}, u32[]{:S(2)}) collective-permute-start(bf16[6,1280]{1,0:T(8,128)(2,1)S(1)} %get-tuple-element.47), channel_id=1, source_target_pairs={{0,16},{4,20},{8,24},{12,28},{16,0},{20,4},{24,8},{28,12},{1,17},{... | collective-permute-start | bytes 46088 | tf_op jit(solution)/shard_map/ppermute | solution.py:24
  43.9 3.2 %collective-permute-start.13 = (bf16[6,1280]{1,0:T(8,128)(2,1)S(1)}, bf16[6,1280]{1,0:T(8,128)(2,1)S(1)}, u32[]{:S(2)}, u32[]{:S(2)}) collective-permute-start(bf16[6,1280]{1,0:T(8,128)(2,1)S(1)} %get-tuple-element.48), channel_id=1, source_target_pairs={{0,24},{4,28},{8,16},{12,20},{16,8},{20,12},{24,0},{28,4},{1,25},{... | collective-permute-start | bytes 46088 | tf_op jit(solution)/shard_map/ppermute | solution.py:24
  47.1 0.0 collective-permute-done.11
  47.1 0.9 %collective-permute-done.12 = bf16[6,1280]{1,0:T(8,128)(2,1)S(1)} collective-permute-done((bf16[6,1280]{1,0:T(8,128)(2,1)S(1)}, bf16[6,1280]{1,0:T(8,128)(2,1)S(1)}, u32[]{:S(2)}, u32[]{:S(2)}) %collective-permute-start.12) | collective-permute-done | bytes 15392 | tf_op jit(solution)/shard_map/ppermute | solution.py:24
  48.0 1.5 %collective-permute-done.13 = bf16[6,1280]{1,0:T(8,128)(2,1)S(1)} collective-permute-done((bf16[6,1280]{1,0:T(8,128)(2,1)S(1)}, bf16[6,1280]{1,0:T(8,128)(2,1)S(1)}, u32[]{:S(2)}, u32[]{:S(2)}) %collective-permute-start.13) | collective-permute-done | bytes 15392 | tf_op jit(solution)/shard_map/ppermute | solution.py:24
  49.5 0.6 %add_convert_fusion = bf16[6,1280]{1,0:T(8,128)(2,1)} fusion(bf16[6,1280]{1,0:T(8,128)(2,1)S(1)} %collective-permute-done.13, bf16[6,1280]{1,0:T(8,128)(2,1)S(1)} %collective-permute-done.12, bf16[6,1280]{1,0:T(8,128)(2,1)S(1)} %collective-permute-done.11, pred[]{:T(512)S(6)} %eq.20, f32[24,1280]{1,0:T(8,128)S(1)} %convert_add_fusion.1, pred[]{:T(512)S(6)} %eq.21), kind=kLoop, calls=%fused_computation.68 | loop fusion | flops 76800 | bytes 184322 | tf_op jit(solution)/shard_map/convert_element_type | solution.py:134
  (15 shorter events, 0.3 us)
Async XLA Ops:
  0.6 21.7 %copy-start = (bf16[176,5120]{1,0:T(8,128)(2,1)S(1)}, bf16[176,5120]{1,0:T(8,128)(2,1)}, u32[]{:S(2)}) copy-start(bf16[176,5120]{1,0:T(8,128)(2,1)} %param.6) | copy-start | bytes 5406724
  1.6 7.1 %collective-permute-start.2 = (bf16[6,2304]{1,0:T(8,128)(2,1)S(1)}, bf16[6,2304]{1,0:T(8,128)(2,1)S(1)}, u32[]{:S(2)}, u32[]{:S(2)}) collective-permute-start(bf16[6,2304]{1,0:T(8,128)(2,1)S(1)} %pad_select_fusion), channel_id=1, source_target_pairs={{0,24},{4,28},{8,16},{12,20},{16,8},{20,12},{24,0},{28,4},{1,25},{... | collective-permute-start | bytes 82952 | tf_op jit(solution)/shard_map/ppermute | solution.py:24
  6.7 4.9 %collective-permute-start.1 = (bf16[6,2304]{1,0:T(8,128)(2,1)S(1)}, bf16[6,2304]{1,0:T(8,128)(2,1)S(1)}, u32[]{:S(2)}, u32[]{:S(2)}) collective-permute-start(bf16[6,2304]{1,0:T(8,128)(2,1)S(1)} %pad_select_fusion), channel_id=1, source_target_pairs={{0,16},{4,20},{8,24},{12,28},{16,0},{20,4},{24,8},{28,12},{1,17},{... | collective-permute-start | bytes 82952 | tf_op jit(solution)/shard_map/ppermute | solution.py:24
  6.7 4.9 %collective-permute-start = (bf16[6,2304]{1,0:T(8,128)(2,1)S(1)}, bf16[6,2304]{1,0:T(8,128)(2,1)S(1)}, u32[]{:S(2)}, u32[]{:S(2)}) collective-permute-start(bf16[6,2304]{1,0:T(8,128)(2,1)S(1)} %pad_select_fusion), channel_id=1, source_target_pairs={{0,8},{4,12},{8,0},{12,4},{16,24},{20,28},{24,16},{28,20},{1,9},{5... | collective-permute-start | bytes 82952 | tf_op jit(solution)/shard_map/ppermute | solution.py:24
  11.6 6.9 %collective-permute-start.5 = (bf16[1,24,2304]{2,1,0:T(8,128)(2,1)S(1)}, bf16[1,24,2304]{2,1,0:T(8,128)(2,1)S(1)}, u32[]{:S(2)}, u32[]{:S(2)}) collective-permute-start(bf16[1,24,2304]{2,1,0:T(8,128)(2,1)S(1)} %maximum_bitcast_fusion), channel_id=1, source_target_pairs={{0,3},{1,2},{2,1},{3,0},{4,7},{5,6},{6,5},{7,4},{8,11},{9,10},{10,... | collective-permute-start | bytes 331784 | tf_op jit(solution)/shard_map/ppermute | solution.py:24
  14.1 5.2 %collective-permute-start.4 = (bf16[1,24,2304]{2,1,0:T(8,128)(2,1)S(1)}, bf16[1,24,2304]{2,1,0:T(8,128)(2,1)S(1)}, u32[]{:S(2)}, u32[]{:S(2)}) collective-permute-start(bf16[1,24,2304]{2,1,0:T(8,128)(2,1)S(1)} %maximum_bitcast_fusion), channel_id=1, source_target_pairs={{0,2},{1,3},{2,0},{3,1},{4,6},{5,7},{6,4},{7,5},{8,10},{9,11},{10,... | collective-permute-start | bytes 331784 | tf_op jit(solution)/shard_map/ppermute | solution.py:24
  14.6 4.7 %collective-permute-start.3 = (bf16[1,24,2304]{2,1,0:T(8,128)(2,1)S(1)}, bf16[1,24,2304]{2,1,0:T(8,128)(2,1)S(1)}, u32[]{:S(2)}, u32[]{:S(2)}) collective-permute-start(bf16[1,24,2304]{2,1,0:T(8,128)(2,1)S(1)} %maximum_bitcast_fusion), channel_id=1, source_target_pairs={{0,1},{1,0},{2,3},{3,2},{4,5},{5,4},{6,7},{7,6},{8,9},{9,8},{10,11... | collective-permute-start | bytes 331784 | tf_op jit(solution)/shard_map/ppermute | solution.py:24
  19.6 1.9 %collective-permute-start.6 = (bf16[4,24,2304]{2,1,0:T(8,128)(2,1)S(1)}, bf16[4,24,2304]{2,1,0:T(8,128)(2,1)S(1)}, u32[]{:S(2)}, u32[]{:S(2)}) collective-permute-start(bf16[4,24,2304]{2,1,0:T(8,128)(2,1)S(1)} %pad_maximum_fusion.1), channel_id=1, source_target_pairs={{0,4},{4,0},{8,12},{12,8},{16,20},{20,16},{24,28},{28,24},{1,5},{5... | collective-permute-start | bytes 1327112 | tf_op jit(solution)/shard_map/ppermute | solution.py:24
  19.7 2.0 %copy-start.1 = (bf16[176,4096]{1,0:T(8,128)(2,1)S(1)}, bf16[176,4096]{1,0:T(8,128)(2,1)}, u32[]{:S(2)}) copy-start(bf16[176,4096]{1,0:T(8,128)(2,1)} %param.7) | copy-start | bytes 4325380
  34.6 1.6 %collective-permute-start.7 = (bf16[24,5120]{1,0:T(8,128)(2,1)S(1)}, bf16[24,5120]{1,0:T(8,128)(2,1)S(1)}, u32[]{:S(2)}, u32[]{:S(2)}) collective-permute-start(bf16[24,5120]{1,0:T(8,128)(2,1)S(1)} %convolution_convert_fusion.1), channel_id=1, source_target_pairs={{0,4},{4,0},{8,12},{12,8},{16,20},{20,16},{24,28},{28,24},{1,5},{5... | collective-permute-start | bytes 737288 | tf_op jit(solution)/shard_map/ppermute | solution.py:24
  36.3 5.7 %collective-permute-start.8 = (bf16[24,1280]{1,0:T(8,128)(2,1)S(1)}, bf16[24,1280]{1,0:T(8,128)(2,1)S(1)}, u32[]{:S(2)}, u32[]{:S(2)}) collective-permute-start(bf16[24,1280]{1,0:T(8,128)(2,1)S(1)} %get-tuple-element.35), channel_id=1, source_target_pairs={{0,3},{1,2},{2,1},{3,0},{4,7},{5,6},{6,5},{7,4},{8,11},{9,10},{10,... | collective-permute-start | bytes 184328 | tf_op jit(solution)/shard_map/ppermute | solution.py:24
  37.0 5.1 %collective-permute-start.9 = (bf16[24,1280]{1,0:T(8,128)(2,1)S(1)}, bf16[24,1280]{1,0:T(8,128)(2,1)S(1)}, u32[]{:S(2)}, u32[]{:S(2)}) collective-permute-start(bf16[24,1280]{1,0:T(8,128)(2,1)S(1)} %get-tuple-element.36), channel_id=1, source_target_pairs={{0,2},{1,3},{2,0},{3,1},{4,6},{5,7},{6,4},{7,5},{8,10},{9,11},{10,... | collective-permute-start | bytes 184328 | tf_op jit(solution)/shard_map/ppermute | solution.py:24
  38.3 4.2 %collective-permute-start.10 = (bf16[24,1280]{1,0:T(8,128)(2,1)S(1)}, bf16[24,1280]{1,0:T(8,128)(2,1)S(1)}, u32[]{:S(2)}, u32[]{:S(2)}) collective-permute-start(bf16[24,1280]{1,0:T(8,128)(2,1)S(1)} %get-tuple-element.37), channel_id=1, source_target_pairs={{0,1},{1,0},{2,3},{3,2},{4,5},{5,4},{6,7},{7,6},{8,9},{9,8},{10,11... | collective-permute-start | bytes 184328 | tf_op jit(solution)/shard_map/ppermute | solution.py:24
  42.6 4.5 %collective-permute-start.11 = (bf16[6,1280]{1,0:T(8,128)(2,1)S(1)}, bf16[6,1280]{1,0:T(8,128)(2,1)S(1)}, u32[]{:S(2)}, u32[]{:S(2)}) collective-permute-start(bf16[6,1280]{1,0:T(8,128)(2,1)S(1)} %get-tuple-element.46), channel_id=1, source_target_pairs={{0,8},{4,12},{8,0},{12,4},{16,24},{20,28},{24,16},{28,20},{1,9},{5... | collective-permute-start | bytes 46088 | tf_op jit(solution)/shard_map/ppermute | solution.py:24
  43.3 4.7 %collective-permute-start.12 = (bf16[6,1280]{1,0:T(8,128)(2,1)S(1)}, bf16[6,1280]{1,0:T(8,128)(2,1)S(1)}, u32[]{:S(2)}, u32[]{:S(2)}) collective-permute-start(bf16[6,1280]{1,0:T(8,128)(2,1)S(1)} %get-tuple-element.47), channel_id=1, source_target_pairs={{0,16},{4,20},{8,24},{12,28},{16,0},{20,4},{24,8},{28,12},{1,17},{... | collective-permute-start | bytes 46088 | tf_op jit(solution)/shard_map/ppermute | solution.py:24
  43.9 5.6 %collective-permute-start.13 = (bf16[6,1280]{1,0:T(8,128)(2,1)S(1)}, bf16[6,1280]{1,0:T(8,128)(2,1)S(1)}, u32[]{:S(2)}, u32[]{:S(2)}) collective-permute-start(bf16[6,1280]{1,0:T(8,128)(2,1)S(1)} %get-tuple-element.48), channel_id=1, source_target_pairs={{0,24},{4,28},{8,16},{12,20},{16,8},{20,12},{24,0},{28,4},{1,25},{... | collective-permute-start | bytes 46088 | tf_op jit(solution)/shard_map/ppermute | solution.py:24

commit v8 on v6

--- a/solution.py
+++ b/solution.py
@@ -24,15 +24,14 @@
     return lax.ppermute(value, axis, [(i, i ^ mask) for i in range(size)])
 
 
-def gathered(value, axis, size, bits, dim):
+def gathered(value, axis, size, bits, dim, first=3):
     index = lax.axis_index(axis)
     for group in grouped(bits):
-        landed = {
-            j: swap(value, axis, size, mask_of(j, group))
-            for j in reversed(range(1, 1 << len(group)))
-        }
-        parts = lax.optimization_barrier([landed[j] for j in range(1, 1 << len(group))])
-        parts = [value] + list(parts)
+        order = sorted(range(1, 1 << len(group)), key=lambda j: (j != first, -j))
+        landed = [swap(value, axis, size, mask_of(j, group)) for j in order]
+        landed = dict(zip(reversed(order), lax.optimization_barrier(landed[::-1])))
+        parts = [landed[j] for j in sorted(order)]
+        parts = [value] + parts
         value = jnp.concatenate(reorder(parts, index, group), axis=dim)
     return value
 
@@ -66,7 +65,7 @@
             jnp.pad(student_hidden, ((0, 0), (0, teacher_share))),
             jnp.pad(teacher_hidden, ((0, 0), (share, 0))),
         )
-        by_z = gathered(packed, "dp", dp, z_bits, 0)
+        by_z = gathered(packed, "dp", dp, z_bits, 0, first=2)
         by_vocab = gathered(by_z[None], "vocab", vocab, vocab_bits, 0)
         whole = gathered(by_vocab, "dp", dp, core, 1)
         student_full = jnp.concatenate([whole[i, :, :share] for i in range(vocab)], axis=1)

time: 49.6 us -> 49.5 us (level)
  no operation moved by 1% of the time
where the time goes in v8:
time: 49.5 us; the launch traced here: 49.4 us
  starting transfers between devices  17.4 us (35%)
  waiting for transfers between devices  13.9 us (28%)
  blocking collectives  10.4 us (21%)
  matrix products  4.04 us (8%)
  other arithmetic  2.57 us (5%)
  between operations  0.81 us (2%)
    ppermute x14, starting transfers between devices, swap(): return lax.ppermute(value, axis, [(i, i ^ mask) for i in range(size)])  17.4 us
    ppermute x14, waiting for transfers between devices, swap(): return lax.ppermute(value, axis, [(i, i ^ mask) for i in range(size)])  13.9 us
    all_to_all x1, blocking collectives, on_device(): lax.all_to_all(jnp.broadcast_to(stats[None], (devices,) + stats.shape), (...  10.4 us
    dot_general x1, matrix products, on_device(): lax.dot_general(logit_grad, student_full, (((0,), (0,)), ((), ())), prefe...  1.87 us
  transfers between devices with their start and end apart: 14, of which 12 were waited for; matrix products, arithmetic and copies ran while one was open for 4% of the time, Pallas kernels for 0%

profile of v8, /device:TPU:0, one launch (start us, length us, event | category | flops | bytes accessed | tf_op | source)
XLA Modules:
  0.0 49.4 jit_solution(9027598778590830216)
XLA Ops:
  0.6 0.0 copy-start
  0.7 0.9 %pad_select_fusion = bf16[6,2304]{1,0:T(8,128)(2,1)S(1)} fusion(bf16[6,1024]{1,0:T(8,128)(2,1)} %param.5, bf16[6,1280]{1,0:T(8,128)(2,1)} %param.4, pred[2304]{0:T(1024)(128)(4,1)S(1)} %iota_compare_fusion), kind=kLoop, calls=%fused_computation.76 | loop fusion | flops 13824 | bytes 57600 | tf_op jit(solution)/shard_map/jit(_where)/select_n | solution.py:63
  1.6 4.1 %collective-permute-start.2 = (bf16[6,2304]{1,0:T(8,128)(2,1)S(1)}, bf16[6,2304]{1,0:T(8,128)(2,1)S(1)}, u32[]{:S(2)}, u32[]{:S(2)}) collective-permute-start(bf16[6,2304]{1,0:T(8,128)(2,1)S(1)} %pad_select_fusion), channel_id=1, source_target_pairs={{0,16},{4,20},{8,24},{12,28},{16,0},{20,4},{24,8},{28,12},{1,17},{... | collective-permute-start | bytes 82952 | tf_op jit(solution)/shard_map/ppermute | solution.py:24
  5.7 1.3 %collective-permute-start.1 = (bf16[6,2304]{1,0:T(8,128)(2,1)S(1)}, bf16[6,2304]{1,0:T(8,128)(2,1)S(1)}, u32[]{:S(2)}, u32[]{:S(2)}) collective-permute-start(bf16[6,2304]{1,0:T(8,128)(2,1)S(1)} %pad_select_fusion), channel_id=1, source_target_pairs={{0,24},{4,28},{8,16},{12,20},{16,8},{20,12},{24,0},{28,4},{1,25},{... | collective-permute-start | bytes 82952 | tf_op jit(solution)/shard_map/ppermute | solution.py:24
  7.0 0.2 collective-permute-start
  7.2 0.8 %collective-permute-done.2 = bf16[6,2304]{1,0:T(8,128)(2,1)S(1)} collective-permute-done((bf16[6,2304]{1,0:T(8,128)(2,1)S(1)}, bf16[6,2304]{1,0:T(8,128)(2,1)S(1)}, u32[]{:S(2)}, u32[]{:S(2)}) %collective-permute-start.2) | collective-permute-done | bytes 27680 | tf_op jit(solution)/shard_map/ppermute | solution.py:24
  8.0 3.4 %collective-permute-done.1 = bf16[6,2304]{1,0:T(8,128)(2,1)S(1)} collective-permute-done((bf16[6,2304]{1,0:T(8,128)(2,1)S(1)}, bf16[6,2304]{1,0:T(8,128)(2,1)S(1)}, u32[]{:S(2)}, u32[]{:S(2)}) %collective-permute-start.1) | collective-permute-done | bytes 27680 | tf_op jit(solution)/shard_map/ppermute | solution.py:24
  11.4 0.0 collective-permute-done
  11.4 0.1 maximum_bitcast_fusion
  11.5 2.5 %collective-permute-start.5 = (bf16[1,24,2304]{2,1,0:T(8,128)(2,1)S(1)}, bf16[1,24,2304]{2,1,0:T(8,128)(2,1)S(1)}, u32[]{:S(2)}, u32[]{:S(2)}) collective-permute-start(bf16[1,24,2304]{2,1,0:T(8,128)(2,1)S(1)} %maximum_bitcast_fusion), channel_id=1, source_target_pairs={{0,3},{1,2},{2,1},{3,0},{4,7},{5,6},{6,5},{7,4},{8,11},{9,10},{10,... | collective-permute-start | bytes 331784 | tf_op jit(solution)/shard_map/ppermute | solution.py:24
  14.0 0.5 %collective-permute-start.4 = (bf16[1,24,2304]{2,1,0:T(8,128)(2,1)S(1)}, bf16[1,24,2304]{2,1,0:T(8,128)(2,1)S(1)}, u32[]{:S(2)}, u32[]{:S(2)}) collective-permute-start(bf16[1,24,2304]{2,1,0:T(8,128)(2,1)S(1)} %maximum_bitcast_fusion), channel_id=1, source_target_pairs={{0,2},{1,3},{2,0},{3,1},{4,6},{5,7},{6,4},{7,5},{8,10},{9,11},{10,... | collective-permute-start | bytes 331784 | tf_op jit(solution)/shard_map/ppermute | solution.py:24
  14.5 0.5 %collective-permute-start.3 = (bf16[1,24,2304]{2,1,0:T(8,128)(2,1)S(1)}, bf16[1,24,2304]{2,1,0:T(8,128)(2,1)S(1)}, u32[]{:S(2)}, u32[]{:S(2)}) collective-permute-start(bf16[1,24,2304]{2,1,0:T(8,128)(2,1)S(1)} %maximum_bitcast_fusion), channel_id=1, source_target_pairs={{0,1},{1,0},{2,3},{3,2},{4,5},{5,4},{6,7},{7,6},{8,9},{9,8},{10,11... | collective-permute-start | bytes 331784 | tf_op jit(solution)/shard_map/ppermute | solution.py:24
  15.1 3.3 %collective-permute-done.5 = bf16[1,24,2304]{2,1,0:T(8,128)(2,1)S(1)} collective-permute-done((bf16[1,24,2304]{2,1,0:T(8,128)(2,1)S(1)}, bf16[1,24,2304]{2,1,0:T(8,128)(2,1)S(1)}, u32[]{:S(2)}, u32[]{:S(2)}) %collective-permute-start.5) | collective-permute-done | bytes 110624 | tf_op jit(solution)/shard_map/ppermute | solution.py:24
  18.4 0.8 %collective-permute-done.4 = bf16[1,24,2304]{2,1,0:T(8,128)(2,1)S(1)} collective-permute-done((bf16[1,24,2304]{2,1,0:T(8,128)(2,1)S(1)}, bf16[1,24,2304]{2,1,0:T(8,128)(2,1)S(1)}, u32[]{:S(2)}, u32[]{:S(2)}) %collective-permute-start.4) | collective-permute-done | bytes 110624 | tf_op jit(solution)/shard_map/ppermute | solution.py:24
  19.2 0.1 collective-permute-done.3
  19.3 0.1 broadcast_select_fusion.9
  19.4 0.1 pad_maximum_fusion.1
  19.5 0.1 collective-permute-start.6
  19.6 0.0 copy-start.1
  19.6 1.8 %collective-permute-done.6 = bf16[4,24,2304]{2,1,0:T(8,128)(2,1)S(1)} collective-permute-done((bf16[4,24,2304]{2,1,0:T(8,128)(2,1)S(1)}, bf16[4,24,2304]{2,1,0:T(8,128)(2,1)S(1)}, u32[]{:S(2)}, u32[]{:S(2)}) %collective-permute-start.6) | collective-permute-done | bytes 442400 | tf_op jit(solution)/shard_map/ppermute | solution.py:24
  21.4 0.1 broadcast_select_fusion.1
  21.5 0.0 copy-done.1
  21.5 0.7 %fusion.39 = (f32[48]{0:T(128)S(1)}, f32[48,176]{1,0:T(8,128)S(1)}) fusion(bf16[176,4096]{1,0:T(8,128)(2,1)S(1)} %copy-done.1, bf16[48,1024]{1,0:T(8,128)(2,1)S(1)} %get-tuple-element.31, bf16[48,1024]{1,0:T(8,128)(2,1)S(1)} %get-tuple-element.32, bf16[48,1024]{1,0:T(8,128)(2,1)S(1)} %get-tuple-element.30, bf16[48,1024]{1,0:T(8,128)(2,1)S(1)} %get-tuple-element.29), kind=kOutput, calls=%fused_computation.112 | convolution fusion | flops 70787280 | bytes 1868992 | tf_op jit(solution)/shard_map/dot_general | solution.py:78
  22.2 0.0 copy-done
  22.2 0.8 %fusion.40 = (f32[48]{0:T(128)S(1)}, f32[48,176]{1,0:T(8,128)S(1)}) fusion(bf16[176,5120]{1,0:T(8,128)(2,1)S(1)} %copy-done, bf16[48,1280]{1,0:T(8,128)(2,1)S(1)} %get-tuple-element.28, bf16[48,1280]{1,0:T(8,128)(2,1)S(1)} %get-tuple-element.27, bf16[48,1280]{1,0:T(8,128)(2,1)S(1)} %get-tuple-element.26, bf16[48,1280]{1,0:T(8,128)(2,1)S(1)} %get-tuple-element.25), kind=kOutput, calls=%fused_computation.113 | convolution fusion | flops 88482000 | bytes 2327744 | tf_op jit(solution)/shard_map/dot_general | solution.py:75
  23.0 0.2 fusion.24
  23.3 0.1 broadcast_in_dim.7
  23.4 10.4 %all_to_all.5 = f32[32,2,128]{2,1,0:T(2,128)S(1)} all-to-all(f32[32,2,128]{2,1,0:T(2,128)S(1)} %broadcast_in_dim.8), channel_id=1, replica_groups=mesh['dp'=8,'vocab'=4] {'dp','vocab'}, dimensions={0} | all-to-all | bytes 65536 | tf_op jit(solution)/shard_map/all_to_all | solution.py:96
  33.8 0.1 fusion.38
  34.1 0.1 multiply_convert_fusion
  34.2 0.3 convolution_convert_fusion.1
  34.5 0.1 collective-permute-start.7
  34.6 0.4 fusion.26
  35.0 1.1 %collective-permute-done.7 = bf16[24,5120]{1,0:T(8,128)(2,1)S(1)} collective-permute-done((bf16[24,5120]{1,0:T(8,128)(2,1)S(1)}, bf16[24,5120]{1,0:T(8,128)(2,1)S(1)}, u32[]{:S(2)}, u32[]{:S(2)}) %collective-permute-start.7) | collective-permute-done | bytes 245792 | tf_op jit(solution)/shard_map/ppermute | solution.py:24
  36.2 0.7 %collective-permute-start.8 = (bf16[24,1280]{1,0:T(8,128)(2,1)S(1)}, bf16[24,1280]{1,0:T(8,128)(2,1)S(1)}, u32[]{:S(2)}, u32[]{:S(2)}) collective-permute-start(bf16[24,1280]{1,0:T(8,128)(2,1)S(1)} %get-tuple-element.35), channel_id=1, source_target_pairs={{0,3},{1,2},{2,1},{3,0},{4,7},{5,6},{6,5},{7,4},{8,11},{9,10},{10,... | collective-permute-start | bytes 184328 | tf_op jit(solution)/shard_map/ppermute | solution.py:24
  36.9 1.3 %collective-permute-start.9 = (bf16[24,1280]{1,0:T(8,128)(2,1)S(1)}, bf16[24,1280]{1,0:T(8,128)(2,1)S(1)}, u32[]{:S(2)}, u32[]{:S(2)}) collective-permute-start(bf16[24,1280]{1,0:T(8,128)(2,1)S(1)} %get-tuple-element.36), channel_id=1, source_target_pairs={{0,2},{1,3},{2,0},{3,1},{4,6},{5,7},{6,4},{7,5},{8,10},{9,11},{10,... | collective-permute-start | bytes 184328 | tf_op jit(solution)/shard_map/ppermute | solution.py:24
  38.2 1.5 %collective-permute-start.10 = (bf16[24,1280]{1,0:T(8,128)(2,1)S(1)}, bf16[24,1280]{1,0:T(8,128)(2,1)S(1)}, u32[]{:S(2)}, u32[]{:S(2)}) collective-permute-start(bf16[24,1280]{1,0:T(8,128)(2,1)S(1)} %get-tuple-element.37), channel_id=1, source_target_pairs={{0,1},{1,0},{2,3},{3,2},{4,5},{5,4},{6,7},{7,6},{8,9},{9,8},{10,11... | collective-permute-start | bytes 184328 | tf_op jit(solution)/shard_map/ppermute | solution.py:24
  39.7 1.9 %convolution_convert_fusion = bf16[176,5120]{1,0:T(8,128)(2,1)} fusion(bf16[48,176]{1,0:T(8,128)(2,1)S(1)} %multiply_convert_fusion, bf16[48,1280]{1,0:T(8,128)(2,1)S(1)} %get-tuple-element.28, bf16[48,1280]{1,0:T(8,128)(2,1)S(1)} %get-tuple-element.27, bf16[48,1280]{1,0:T(8,128)(2,1)S(1)} %get-tuple-element.26, bf16[48,1280]{1,0:T(8,128)(2,1)S(1)} %get-tuple-element.25), kind=kOutput, calls=%fused_computation | convolution fusion | flops 89374720 | bytes 2310656 | tf_op jit(solution)/shard_map/dot_general | solution.py:127
  41.6 0.3 collective-permute-done.8
  41.9 0.1 collective-permute-done.9
  41.9 0.5 collective-permute-done.10
  42.4 0.1 convert_add_fusion.1
  42.5 0.7 %collective-permute-start.11 = (bf16[6,1280]{1,0:T(8,128)(2,1)S(1)}, bf16[6,1280]{1,0:T(8,128)(2,1)S(1)}, u32[]{:S(2)}, u32[]{:S(2)}) collective-permute-start(bf16[6,1280]{1,0:T(8,128)(2,1)S(1)} %get-tuple-element.46), channel_id=1, source_target_pairs={{0,24},{4,28},{8,16},{12,20},{16,8},{20,12},{24,0},{28,4},{1,25},{... | collective-permute-start | bytes 46088 | tf_op jit(solution)/shard_map/ppermute | solution.py:24
  43.2 1.4 %collective-permute-start.12 = (bf16[6,1280]{1,0:T(8,128)(2,1)S(1)}, bf16[6,1280]{1,0:T(8,128)(2,1)S(1)}, u32[]{:S(2)}, u32[]{:S(2)}) collective-permute-start(bf16[6,1280]{1,0:T(8,128)(2,1)S(1)} %get-tuple-element.47), channel_id=1, source_target_pairs={{0,16},{4,20},{8,24},{12,28},{16,0},{20,4},{24,8},{28,12},{1,17},{... | collective-permute-start | bytes 46088 | tf_op jit(solution)/shard_map/ppermute | solution.py:24
  44.6 2.3 %collective-permute-start.13 = (bf16[6,1280]{1,0:T(8,128)(2,1)S(1)}, bf16[6,1280]{1,0:T(8,128)(2,1)S(1)}, u32[]{:S(2)}, u32[]{:S(2)}) collective-permute-start(bf16[6,1280]{1,0:T(8,128)(2,1)S(1)} %get-tuple-element.48), channel_id=1, source_target_pairs={{0,8},{4,12},{8,0},{12,4},{16,24},{20,28},{24,16},{28,20},{1,9},{5... | collective-permute-start | bytes 46088 | tf_op jit(solution)/shard_map/ppermute | solution.py:24
  47.0 1.2 %collective-permute-done.11 = bf16[6,1280]{1,0:T(8,128)(2,1)S(1)} collective-permute-done((bf16[6,1280]{1,0:T(8,128)(2,1)S(1)}, bf16[6,1280]{1,0:T(8,128)(2,1)S(1)}, u32[]{:S(2)}, u32[]{:S(2)}) %collective-permute-start.11) | collective-permute-done | bytes 15392 | tf_op jit(solution)/shard_map/ppermute | solution.py:24
  48.2 0.0 collective-permute-done.12
  48.2 0.6 %collective-permute-done.13 = bf16[6,1280]{1,0:T(8,128)(2,1)S(1)} collective-permute-done((bf16[6,1280]{1,0:T(8,128)(2,1)S(1)}, bf16[6,1280]{1,0:T(8,128)(2,1)S(1)}, u32[]{:S(2)}, u32[]{:S(2)}) %collective-permute-start.13) | collective-permute-done | bytes 15392 | tf_op jit(solution)/shard_map/ppermute | solution.py:24
  48.7 0.6 %add_convert_fusion = bf16[6,1280]{1,0:T(8,128)(2,1)} fusion(bf16[6,1280]{1,0:T(8,128)(2,1)S(1)} %collective-permute-done.13, bf16[6,1280]{1,0:T(8,128)(2,1)S(1)} %collective-permute-done.12, bf16[6,1280]{1,0:T(8,128)(2,1)S(1)} %collective-permute-done.11, pred[]{:T(512)S(6)} %eq.20, f32[24,1280]{1,0:T(8,128)S(1)} %convert_add_fusion.1, pred[]{:T(512)S(6)} %eq.21), kind=kLoop, calls=%fused_computation.68 | loop fusion | flops 76800 | bytes 184322 | tf_op jit(solution)/shard_map/convert_element_type | solution.py:133
  (15 shorter events, 0.3 us)
Async XLA Ops:
  0.6 21.6 %copy-start = (bf16[176,5120]{1,0:T(8,128)(2,1)S(1)}, bf16[176,5120]{1,0:T(8,128)(2,1)}, u32[]{:S(2)}) copy-start(bf16[176,5120]{1,0:T(8,128)(2,1)} %param.6) | copy-start | bytes 5406724
  1.6 6.4 %collective-permute-start.2 = (bf16[6,2304]{1,0:T(8,128)(2,1)S(1)}, bf16[6,2304]{1,0:T(8,128)(2,1)S(1)}, u32[]{:S(2)}, u32[]{:S(2)}) collective-permute-start(bf16[6,2304]{1,0:T(8,128)(2,1)S(1)} %pad_select_fusion), channel_id=1, source_target_pairs={{0,16},{4,20},{8,24},{12,28},{16,0},{20,4},{24,8},{28,12},{1,17},{... | collective-permute-start | bytes 82952 | tf_op jit(solution)/shard_map/ppermute | solution.py:24
  5.7 5.8 %collective-permute-start.1 = (bf16[6,2304]{1,0:T(8,128)(2,1)S(1)}, bf16[6,2304]{1,0:T(8,128)(2,1)S(1)}, u32[]{:S(2)}, u32[]{:S(2)}) collective-permute-start(bf16[6,2304]{1,0:T(8,128)(2,1)S(1)} %pad_select_fusion), channel_id=1, source_target_pairs={{0,24},{4,28},{8,16},{12,20},{16,8},{20,12},{24,0},{28,4},{1,25},{... | collective-permute-start | bytes 82952 | tf_op jit(solution)/shard_map/ppermute | solution.py:24
  7.0 4.4 %collective-permute-start = (bf16[6,2304]{1,0:T(8,128)(2,1)S(1)}, bf16[6,2304]{1,0:T(8,128)(2,1)S(1)}, u32[]{:S(2)}, u32[]{:S(2)}) collective-permute-start(bf16[6,2304]{1,0:T(8,128)(2,1)S(1)} %pad_select_fusion), channel_id=1, source_target_pairs={{0,8},{4,12},{8,0},{12,4},{16,24},{20,28},{24,16},{28,20},{1,9},{5... | collective-permute-start | bytes 82952 | tf_op jit(solution)/shard_map/ppermute | solution.py:24
  11.5 6.9 %collective-permute-start.5 = (bf16[1,24,2304]{2,1,0:T(8,128)(2,1)S(1)}, bf16[1,24,2304]{2,1,0:T(8,128)(2,1)S(1)}, u32[]{:S(2)}, u32[]{:S(2)}) collective-permute-start(bf16[1,24,2304]{2,1,0:T(8,128)(2,1)S(1)} %maximum_bitcast_fusion), channel_id=1, source_target_pairs={{0,3},{1,2},{2,1},{3,0},{4,7},{5,6},{6,5},{7,4},{8,11},{9,10},{10,... | collective-permute-start | bytes 331784 | tf_op jit(solution)/shard_map/ppermute | solution.py:24
  14.0 5.2 %collective-permute-start.4 = (bf16[1,24,2304]{2,1,0:T(8,128)(2,1)S(1)}, bf16[1,24,2304]{2,1,0:T(8,128)(2,1)S(1)}, u32[]{:S(2)}, u32[]{:S(2)}) collective-permute-start(bf16[1,24,2304]{2,1,0:T(8,128)(2,1)S(1)} %maximum_bitcast_fusion), channel_id=1, source_target_pairs={{0,2},{1,3},{2,0},{3,1},{4,6},{5,7},{6,4},{7,5},{8,10},{9,11},{10,... | collective-permute-start | bytes 331784 | tf_op jit(solution)/shard_map/ppermute | solution.py:24
  14.5 4.7 %collective-permute-start.3 = (bf16[1,24,2304]{2,1,0:T(8,128)(2,1)S(1)}, bf16[1,24,2304]{2,1,0:T(8,128)(2,1)S(1)}, u32[]{:S(2)}, u32[]{:S(2)}) collective-permute-start(bf16[1,24,2304]{2,1,0:T(8,128)(2,1)S(1)} %maximum_bitcast_fusion), channel_id=1, source_target_pairs={{0,1},{1,0},{2,3},{3,2},{4,5},{5,4},{6,7},{7,6},{8,9},{9,8},{10,11... | collective-permute-start | bytes 331784 | tf_op jit(solution)/shard_map/ppermute | solution.py:24
  19.5 1.9 %collective-permute-start.6 = (bf16[4,24,2304]{2,1,0:T(8,128)(2,1)S(1)}, bf16[4,24,2304]{2,1,0:T(8,128)(2,1)S(1)}, u32[]{:S(2)}, u32[]{:S(2)}) collective-permute-start(bf16[4,24,2304]{2,1,0:T(8,128)(2,1)S(1)} %pad_maximum_fusion.1), channel_id=1, source_target_pairs={{0,4},{4,0},{8,12},{12,8},{16,20},{20,16},{24,28},{28,24},{1,5},{5... | collective-permute-start | bytes 1327112 | tf_op jit(solution)/shard_map/ppermute | solution.py:24
  19.6 2.0 %copy-start.1 = (bf16[176,4096]{1,0:T(8,128)(2,1)S(1)}, bf16[176,4096]{1,0:T(8,128)(2,1)}, u32[]{:S(2)}) copy-start(bf16[176,4096]{1,0:T(8,128)(2,1)} %param.7) | copy-start | bytes 4325380
  34.5 1.6 %collective-permute-start.7 = (bf16[24,5120]{1,0:T(8,128)(2,1)S(1)}, bf16[24,5120]{1,0:T(8,128)(2,1)S(1)}, u32[]{:S(2)}, u32[]{:S(2)}) collective-permute-start(bf16[24,5120]{1,0:T(8,128)(2,1)S(1)} %convolution_convert_fusion.1), channel_id=1, source_target_pairs={{0,4},{4,0},{8,12},{12,8},{16,20},{20,16},{24,28},{28,24},{1,5},{5... | collective-permute-start | bytes 737288 | tf_op jit(solution)/shard_map/ppermute | solution.py:24
  36.2 5.7 %collective-permute-start.8 = (bf16[24,1280]{1,0:T(8,128)(2,1)S(1)}, bf16[24,1280]{1,0:T(8,128)(2,1)S(1)}, u32[]{:S(2)}, u32[]{:S(2)}) collective-permute-start(bf16[24,1280]{1,0:T(8,128)(2,1)S(1)} %get-tuple-element.35), channel_id=1, source_target_pairs={{0,3},{1,2},{2,1},{3,0},{4,7},{5,6},{6,5},{7,4},{8,11},{9,10},{10,... | collective-permute-start | bytes 184328 | tf_op jit(solution)/shard_map/ppermute | solution.py:24
  36.9 5.1 %collective-permute-start.9 = (bf16[24,1280]{1,0:T(8,128)(2,1)S(1)}, bf16[24,1280]{1,0:T(8,128)(2,1)S(1)}, u32[]{:S(2)}, u32[]{:S(2)}) collective-permute-start(bf16[24,1280]{1,0:T(8,128)(2,1)S(1)} %get-tuple-element.36), channel_id=1, source_target_pairs={{0,2},{1,3},{2,0},{3,1},{4,6},{5,7},{6,4},{7,5},{8,10},{9,11},{10,... | collective-permute-start | bytes 184328 | tf_op jit(solution)/shard_map/ppermute | solution.py:24
  38.2 4.2 %collective-permute-start.10 = (bf16[24,1280]{1,0:T(8,128)(2,1)S(1)}, bf16[24,1280]{1,0:T(8,128)(2,1)S(1)}, u32[]{:S(2)}, u32[]{:S(2)}) collective-permute-start(bf16[24,1280]{1,0:T(8,128)(2,1)S(1)} %get-tuple-element.37), channel_id=1, source_target_pairs={{0,1},{1,0},{2,3},{3,2},{4,5},{5,4},{6,7},{7,6},{8,9},{9,8},{10,11... | collective-permute-start | bytes 184328 | tf_op jit(solution)/shard_map/ppermute | solution.py:24
  42.5 5.6 %collective-permute-start.11 = (bf16[6,1280]{1,0:T(8,128)(2,1)S(1)}, bf16[6,1280]{1,0:T(8,128)(2,1)S(1)}, u32[]{:S(2)}, u32[]{:S(2)}) collective-permute-start(bf16[6,1280]{1,0:T(8,128)(2,1)S(1)} %get-tuple-element.46), channel_id=1, source_target_pairs={{0,24},{4,28},{8,16},{12,20},{16,8},{20,12},{24,0},{28,4},{1,25},{... | collective-permute-start | bytes 46088 | tf_op jit(solution)/shard_map/ppermute | solution.py:24
  43.2 5.0 %collective-permute-start.12 = (bf16[6,1280]{1,0:T(8,128)(2,1)S(1)}, bf16[6,1280]{1,0:T(8,128)(2,1)S(1)}, u32[]{:S(2)}, u32[]{:S(2)}) collective-permute-start(bf16[6,1280]{1,0:T(8,128)(2,1)S(1)} %get-tuple-element.47), channel_id=1, source_target_pairs={{0,16},{4,20},{8,24},{12,28},{16,0},{20,4},{24,8},{28,12},{1,17},{... | collective-permute-start | bytes 46088 | tf_op jit(solution)/shard_map/ppermute | solution.py:24
  44.6 4.1 %collective-permute-start.13 = (bf16[6,1280]{1,0:T(8,128)(2,1)S(1)}, bf16[6,1280]{1,0:T(8,128)(2,1)S(1)}, u32[]{:S(2)}, u32[]{:S(2)}) collective-permute-start(bf16[6,1280]{1,0:T(8,128)(2,1)S(1)} %get-tuple-element.48), channel_id=1, source_target_pairs={{0,8},{4,12},{8,0},{12,4},{16,24},{20,28},{24,16},{28,20},{1,9},{5... | collective-permute-start | bytes 46088 | tf_op jit(solution)/shard_map/ppermute | solution.py:24

commit v9 on v6

--- a/solution.py
+++ b/solution.py
@@ -46,6 +46,35 @@
             swap(parts[j].astype(jnp.bfloat16), axis, size, mask_of(j, group))
             for j in reversed(range(1, 1 << len(group)))
         ]
+        for part in landed:
+            total = total + part.astype(jnp.float32)
+    return total
+
+
+def scattered_mixed(total, axis, size, bits, dim):
+    index = lax.axis_index(axis)
+    for group in reversed(grouped(bits)):
+        parts = reorder(jnp.split(total, 1 << len(group), axis=dim), index, group)
+        total = parts[0]
+        parts = [part.astype(jnp.bfloat16) for part in parts]
+        if len(group) == 2:
+            bit = group[1]
+            upper = ((index >> bit) & 1) == 1
+            near, second, far = [mask_of(j, group) for j in (1, 2, 3)]
+            one = jnp.where(upper, parts[2], parts[3])
+            other = jnp.where(upper, parts[3], parts[2])
+            one, other, last = lax.optimization_barrier((one, other, parts[1]))
+            landed = [
+                lax.ppermute(one, axis, [
+                    (i, i ^ (second if (i >> bit) & 1 else far)) for i in range(size)
+                ]),
+                lax.ppermute(other, axis, [
+                    (i, i ^ (far if (i >> bit) & 1 else second)) for i in range(size)
+                ]),
+                swap(last, axis, size, near),
+            ]
+        else:
+            landed = [swap(parts[1], axis, size, mask_of(1, group))]
         for part in landed:
             total = total + part.astype(jnp.float32)
     return total
@@ -130,7 +159,7 @@
         ).astype(jnp.bfloat16)
         acc = scattered(acc, "vocab", vocab, vocab_bits, 1)
         acc, head_grad = lax.optimization_barrier((acc, head_grad))
-        acc = scattered(acc, "dp", dp, z_bits, 0)
+        acc = scattered_mixed(acc, "dp", dp, z_bits, 0)
         hidden_grad = acc.astype(jnp.bfloat16)
         return (hidden_grad, head_grad)
 

time: 49.6 us -> 51 us (1.028)
  blocking collectives: 10.4 us -> 0 us
  waiting for transfers between devices: 13.9 us -> 22.6 us
  starting transfers between devices: 17.5 us -> 19.9 us
  local copies, waits for them, and re-layouts: 0.24 us -> 0.86 us
    all_to_all x1 -> x0, blocking collectives: 10.4 us -> none  [on_device(): lax.all_to_all(jnp.broadcast_to(stats[None], (devices,) + stats.shape), (...]
    all_to_all x0 -> x1, waiting for transfers between devices: none -> 7.29 us  [on_device(): lax.all_to_all(jnp.broadcast_to(stats[None], (devices,) + stats.shape), (...]
    ppermute x14 -> x12, starting transfers between devices: 17.5 us -> 13.6 us  [swap(): return lax.ppermute(value, axis, [(i, i ^ mask) for i in range(size)])]
    all_to_all x0 -> x1, starting transfers between devices: none -> 3.34 us  [on_device(): lax.all_to_all(jnp.broadcast_to(stats[None], (devices,) + stats.shape), (...]
    ppermute x0 -> x2, starting transfers between devices: none -> 2.98 us  [the longest x1 2.31 us: scattered_mixed(): lax.ppermute(other, axis, [(i, i ^ (far if i >> bit & 1 else second)) for...]
    ppermute x0 -> x2, waiting for transfers between devices: none -> 2.69 us  [the longest x1 1.39 us: scattered_mixed(): lax.ppermute(one, axis, [(i, i ^ (second if i >> bit & 1 else far)) for i...]
    ppermute x14 -> x12, waiting for transfers between devices: 13.9 us -> 12.7 us  [swap(): return lax.ppermute(value, axis, [(i, i ^ mask) for i in range(size)])]
    broadcast_in_dim x2, local copies, waits for them, and re-layouts: 0.09 us -> 0.71 us  [on_device(): jnp.broadcast_to(stats[None], (devices,) + stats.shape)]
  transfers between devices with their start and end apart: 14 -> 15, of which waited for: 12 -> 14; matrix products, arithmetic and copies ran while one was open for 4% -> 4% of each run, Pallas kernels for 0% -> 0%
where the time goes in v9:
time: 51 us; the launch traced here: 50.9 us
  waiting for transfers between devices  22.6 us (44%)
  starting transfers between devices  19.9 us (39%)
  matrix products  4.03 us (8%)
  other arithmetic  2.58 us (5%)
  local copies, waits for them, and re-layouts  0.86 us (2%)
  between operations  0.82 us (2%)
    ppermute x12, starting transfers between devices, swap(): return lax.ppermute(value, axis, [(i, i ^ mask) for i in range(size)])  13.6 us
    ppermute x12, waiting for transfers between devices, swap(): return lax.ppermute(value, axis, [(i, i ^ mask) for i in range(size)])  12.7 us
    all_to_all x1, waiting for transfers between devices, on_device(): lax.all_to_all(jnp.broadcast_to(stats[None], (devices,) + stats.shape), (...  7.29 us
    all_to_all x1, starting transfers between devices, on_device(): lax.all_to_all(jnp.broadcast_to(stats[None], (devices,) + stats.shape), (...  3.34 us
    ppermute x1, starting transfers between devices, scattered_mixed(): lax.ppermute(other, axis, [(i, i ^ (far if i >> bit & 1 else second)) for...  2.31 us
    dot_general x1, matrix products, on_device(): lax.dot_general(logit_grad, student_full, (((0,), (0,)), ((), ())), prefe...  1.86 us
    ppermute x1, waiting for transfers between devices, scattered_mixed(): lax.ppermute(one, axis, [(i, i ^ (second if i >> bit & 1 else far)) for i...  1.39 us
    ppermute x1, waiting for transfers between devices, scattered_mixed(): lax.ppermute(other, axis, [(i, i ^ (far if i >> bit & 1 else second)) for...  1.3 us
  transfers between devices with their start and end apart: 15, of which 14 were waited for; matrix products, arithmetic and copies ran while one was open for 4% of the time, Pallas kernels for 0%

profile of v9, /device:TPU:0, one launch (start us, length us, event | category | flops | bytes accessed | tf_op | source)
XLA Modules:
  0.0 50.9 jit_solution(7911961673933609907)
XLA Ops:
  0.6 0.0 copy-start
  0.7 0.9 %pad_select_fusion = bf16[6,2304]{1,0:T(8,128)(2,1)S(1)} fusion(bf16[6,1024]{1,0:T(8,128)(2,1)} %param.5, bf16[6,1280]{1,0:T(8,128)(2,1)} %param.4, pred[2304]{0:T(1024)(128)(4,1)S(1)} %iota_compare_fusion), kind=kLoop, calls=%fused_computation.76 | loop fusion | flops 13824 | bytes 57600 | tf_op jit(solution)/shard_map/jit(_where)/select_n | solution.py:93
  1.6 5.1 %collective-permute-start.2 = (bf16[6,2304]{1,0:T(8,128)(2,1)S(1)}, bf16[6,2304]{1,0:T(8,128)(2,1)S(1)}, u32[]{:S(2)}, u32[]{:S(2)}) collective-permute-start(bf16[6,2304]{1,0:T(8,128)(2,1)S(1)} %pad_select_fusion), channel_id=1, source_target_pairs={{0,24},{4,28},{8,16},{12,20},{16,8},{20,12},{24,0},{28,4},{1,25},{... | collective-permute-start | bytes 82952 | tf_op jit(solution)/shard_map/ppermute | solution.py:24
  6.7 0.0 collective-permute-start.1
  6.7 0.6 %collective-permute-start = (bf16[6,2304]{1,0:T(8,128)(2,1)S(1)}, bf16[6,2304]{1,0:T(8,128)(2,1)S(1)}, u32[]{:S(2)}, u32[]{:S(2)}) collective-permute-start(bf16[6,2304]{1,0:T(8,128)(2,1)S(1)} %pad_select_fusion), channel_id=1, source_target_pairs={{0,8},{4,12},{8,0},{12,4},{16,24},{20,28},{24,16},{28,20},{1,9},{5... | collective-permute-start | bytes 82952 | tf_op jit(solution)/shard_map/ppermute | solution.py:24
  7.3 1.3 %collective-permute-done.2 = bf16[6,2304]{1,0:T(8,128)(2,1)S(1)} collective-permute-done((bf16[6,2304]{1,0:T(8,128)(2,1)S(1)}, bf16[6,2304]{1,0:T(8,128)(2,1)S(1)}, u32[]{:S(2)}, u32[]{:S(2)}) %collective-permute-start.2) | collective-permute-done | bytes 27680 | tf_op jit(solution)/shard_map/ppermute | solution.py:24
  8.6 2.9 %collective-permute-done.1 = bf16[6,2304]{1,0:T(8,128)(2,1)S(1)} collective-permute-done((bf16[6,2304]{1,0:T(8,128)(2,1)S(1)}, bf16[6,2304]{1,0:T(8,128)(2,1)S(1)}, u32[]{:S(2)}, u32[]{:S(2)}) %collective-permute-start.1) | collective-permute-done | bytes 27680 | tf_op jit(solution)/shard_map/ppermute | solution.py:24
  11.5 0.0 collective-permute-done
  11.6 0.1 maximum_bitcast_fusion
  11.6 2.5 %collective-permute-start.5 = (bf16[1,24,2304]{2,1,0:T(8,128)(2,1)S(1)}, bf16[1,24,2304]{2,1,0:T(8,128)(2,1)S(1)}, u32[]{:S(2)}, u32[]{:S(2)}) collective-permute-start(bf16[1,24,2304]{2,1,0:T(8,128)(2,1)S(1)} %maximum_bitcast_fusion), channel_id=1, source_target_pairs={{0,3},{1,2},{2,1},{3,0},{4,7},{5,6},{6,5},{7,4},{8,11},{9,10},{10,... | collective-permute-start | bytes 331784 | tf_op jit(solution)/shard_map/ppermute | solution.py:24
  14.1 0.5 collective-permute-start.4
  14.6 0.5 %collective-permute-start.3 = (bf16[1,24,2304]{2,1,0:T(8,128)(2,1)S(1)}, bf16[1,24,2304]{2,1,0:T(8,128)(2,1)S(1)}, u32[]{:S(2)}, u32[]{:S(2)}) collective-permute-start(bf16[1,24,2304]{2,1,0:T(8,128)(2,1)S(1)} %maximum_bitcast_fusion), channel_id=1, source_target_pairs={{0,1},{1,0},{2,3},{3,2},{4,5},{5,4},{6,7},{7,6},{8,9},{9,8},{10,11... | collective-permute-start | bytes 331784 | tf_op jit(solution)/shard_map/ppermute | solution.py:24
  15.2 3.3 %collective-permute-done.5 = bf16[1,24,2304]{2,1,0:T(8,128)(2,1)S(1)} collective-permute-done((bf16[1,24,2304]{2,1,0:T(8,128)(2,1)S(1)}, bf16[1,24,2304]{2,1,0:T(8,128)(2,1)S(1)}, u32[]{:S(2)}, u32[]{:S(2)}) %collective-permute-start.5) | collective-permute-done | bytes 110624 | tf_op jit(solution)/shard_map/ppermute | solution.py:24
  18.5 0.8 %collective-permute-done.4 = bf16[1,24,2304]{2,1,0:T(8,128)(2,1)S(1)} collective-permute-done((bf16[1,24,2304]{2,1,0:T(8,128)(2,1)S(1)}, bf16[1,24,2304]{2,1,0:T(8,128)(2,1)S(1)}, u32[]{:S(2)}, u32[]{:S(2)}) %collective-permute-start.4) | collective-permute-done | bytes 110624 | tf_op jit(solution)/shard_map/ppermute | solution.py:24
  19.3 0.1 collective-permute-done.3
  19.4 0.1 broadcast_select_fusion.9
  19.5 0.1 pad_maximum_fusion.1
  19.6 0.1 collective-permute-start.6
  19.7 0.0 copy-start.1
  19.7 1.8 %collective-permute-done.6 = bf16[4,24,2304]{2,1,0:T(8,128)(2,1)S(1)} collective-permute-done((bf16[4,24,2304]{2,1,0:T(8,128)(2,1)S(1)}, bf16[4,24,2304]{2,1,0:T(8,128)(2,1)S(1)}, u32[]{:S(2)}, u32[]{:S(2)}) %collective-permute-start.6) | collective-permute-done | bytes 442400 | tf_op jit(solution)/shard_map/ppermute | solution.py:24
  21.5 0.1 broadcast_select_fusion.1
  21.7 0.0 copy-done.1
  21.7 0.7 %fusion.39 = (f32[48]{0:T(128)S(1)}, f32[48,176]{1,0:T(8,128)S(1)}) fusion(bf16[176,4096]{1,0:T(8,128)(2,1)S(1)} %copy-done.1, bf16[48,1024]{1,0:T(8,128)(2,1)S(1)} %get-tuple-element.40, bf16[48,1024]{1,0:T(8,128)(2,1)S(1)} %get-tuple-element.41, bf16[48,1024]{1,0:T(8,128)(2,1)S(1)} %get-tuple-element.39, bf16[48,1024]{1,0:T(8,128)(2,1)S(1)} %get-tuple-element.38), kind=kOutput, calls=%fused_computation.114 | convolution fusion | flops 70787280 | bytes 1868992 | tf_op jit(solution)/shard_map/dot_general | solution.py:108
  22.3 0.0 copy-done
  22.4 0.8 %fusion.40 = (f32[48]{0:T(128)S(1)}, f32[48,176]{1,0:T(8,128)S(1)}) fusion(bf16[176,5120]{1,0:T(8,128)(2,1)S(1)} %copy-done, bf16[48,1280]{1,0:T(8,128)(2,1)S(1)} %get-tuple-element.37, bf16[48,1280]{1,0:T(8,128)(2,1)S(1)} %get-tuple-element.36, bf16[48,1280]{1,0:T(8,128)(2,1)S(1)} %get-tuple-element.35, bf16[48,1280]{1,0:T(8,128)(2,1)S(1)} %get-tuple-element.34), kind=kOutput, calls=%fused_computation.115 | convolution fusion | flops 88482000 | bytes 2327744 | tf_op jit(solution)/shard_map/dot_general | solution.py:105
  23.1 0.2 fusion.24
  23.4 0.1 broadcast_in_dim.7
  23.5 0.6 %broadcast_in_dim.8 = f32[32,2,128]{2,1,0:T(2,128)} broadcast(f32[2,128]{1,0:T(2,128)S(1)} %broadcast_in_dim.7), dimensions={1,2} | broadcast | bytes 33792 | tf_op jit(solution)/shard_map/broadcast_in_dim | solution.py:127
  24.1 3.3 %all-to-all-start = ((f32[32,2,128]{2,1,0:T(2,128)}), f32[32,2,128]{2,1,0:T(2,128)S(1)}, u32[]{:S(2)}, u32[]{:S(2)}) async-start(f32[32,2,128]{2,1,0:T(2,128)} %broadcast_in_dim.8), calls=%async_computation | async-start | bytes 65536 | tf_op jit(solution)/shard_map/all_to_all | solution.py:126
  27.5 7.3 %all-to-all-done = f32[32,2,128]{2,1,0:T(2,128)S(1)} async-done(((f32[32,2,128]{2,1,0:T(2,128)}), f32[32,2,128]{2,1,0:T(2,128)S(1)}, u32[]{:S(2)}, u32[]{:S(2)}) %all-to-all-start) | async-done | bytes 32800 | tf_op jit(solution)/shard_map/all_to_all | solution.py:126
  34.8 0.1 fusion.38
  35.0 0.1 multiply_convert_fusion
  35.1 0.3 convolution_convert_fusion.1
  35.5 0.1 collective-permute-start.7
  35.5 0.4 fusion.26
  35.9 1.1 %collective-permute-done.7 = bf16[24,5120]{1,0:T(8,128)(2,1)S(1)} collective-permute-done((bf16[24,5120]{1,0:T(8,128)(2,1)S(1)}, bf16[24,5120]{1,0:T(8,128)(2,1)S(1)}, u32[]{:S(2)}, u32[]{:S(2)}) %collective-permute-start.7) | collective-permute-done | bytes 245792 | tf_op jit(solution)/shard_map/ppermute | solution.py:24
  37.1 0.7 %collective-permute-start.8 = (bf16[24,1280]{1,0:T(8,128)(2,1)S(1)}, bf16[24,1280]{1,0:T(8,128)(2,1)S(1)}, u32[]{:S(2)}, u32[]{:S(2)}) collective-permute-start(bf16[24,1280]{1,0:T(8,128)(2,1)S(1)} %get-tuple-element.44), channel_id=1, source_target_pairs={{0,3},{1,2},{2,1},{3,0},{4,7},{5,6},{6,5},{7,4},{8,11},{9,10},{10,... | collective-permute-start | bytes 184328 | tf_op jit(solution)/shard_map/ppermute | solution.py:24
  37.8 1.3 %collective-permute-start.9 = (bf16[24,1280]{1,0:T(8,128)(2,1)S(1)}, bf16[24,1280]{1,0:T(8,128)(2,1)S(1)}, u32[]{:S(2)}, u32[]{:S(2)}) collective-permute-start(bf16[24,1280]{1,0:T(8,128)(2,1)S(1)} %get-tuple-element.45), channel_id=1, source_target_pairs={{0,2},{1,3},{2,0},{3,1},{4,6},{5,7},{6,4},{7,5},{8,10},{9,11},{10,... | collective-permute-start | bytes 184328 | tf_op jit(solution)/shard_map/ppermute | solution.py:24
  39.1 1.5 %collective-permute-start.10 = (bf16[24,1280]{1,0:T(8,128)(2,1)S(1)}, bf16[24,1280]{1,0:T(8,128)(2,1)S(1)}, u32[]{:S(2)}, u32[]{:S(2)}) collective-permute-start(bf16[24,1280]{1,0:T(8,128)(2,1)S(1)} %get-tuple-element.46), channel_id=1, source_target_pairs={{0,1},{1,0},{2,3},{3,2},{4,5},{5,4},{6,7},{7,6},{8,9},{9,8},{10,11... | collective-permute-start | bytes 184328 | tf_op jit(solution)/shard_map/ppermute | solution.py:24
  40.7 1.9 %convolution_convert_fusion = bf16[176,5120]{1,0:T(8,128)(2,1)} fusion(bf16[48,176]{1,0:T(8,128)(2,1)S(1)} %multiply_convert_fusion, bf16[48,1280]{1,0:T(8,128)(2,1)S(1)} %get-tuple-element.37, bf16[48,1280]{1,0:T(8,128)(2,1)S(1)} %get-tuple-element.36, bf16[48,1280]{1,0:T(8,128)(2,1)S(1)} %get-tuple-element.35, bf16[48,1280]{1,0:T(8,128)(2,1)S(1)} %get-tuple-element.34), kind=kOutput, calls=%fused_computation | convolution fusion | flops 89374720 | bytes 2310656 | tf_op jit(solution)/shard_map/dot_general | solution.py:157
  42.5 0.3 collective-permute-done.8
  42.8 0.1 collective-permute-done.9
  42.9 0.5 collective-permute-done.10
  43.4 0.1 convert_add_fusion.1
  43.5 0.7 %collective-permute-start.11 = (bf16[6,1280]{1,0:T(8,128)(2,1)S(1)}, bf16[6,1280]{1,0:T(8,128)(2,1)S(1)}, u32[]{:S(2)}, u32[]{:S(2)}) collective-permute-start(bf16[6,1280]{1,0:T(8,128)(2,1)S(1)} %broadcast_select_fusion.19), channel_id=1, source_target_pairs={{0,24},{4,28},{8,16},{12,20},{16,0},{20,4},{24,8},{28,12},{1,25},{... | collective-permute-start | bytes 46088 | tf_op jit(solution)/shard_map/ppermute | solution.py:68
  44.1 2.3 %collective-permute-start.12 = (bf16[6,1280]{1,0:T(8,128)(2,1)S(1)}, bf16[6,1280]{1,0:T(8,128)(2,1)S(1)}, u32[]{:S(2)}, u32[]{:S(2)}) collective-permute-start(bf16[6,1280]{1,0:T(8,128)(2,1)S(1)} %get-tuple-element.21), channel_id=1, source_target_pairs={{0,16},{4,20},{8,24},{12,28},{16,8},{20,12},{24,0},{28,4},{1,17},{... | collective-permute-start | bytes 46088 | tf_op jit(solution)/shard_map/ppermute | solution.py:71
  46.4 0.6 %collective-permute-start.13 = (bf16[6,1280]{1,0:T(8,128)(2,1)S(1)}, bf16[6,1280]{1,0:T(8,128)(2,1)S(1)}, u32[]{:S(2)}, u32[]{:S(2)}) collective-permute-start(bf16[6,1280]{1,0:T(8,128)(2,1)S(1)} %get-tuple-element.22), channel_id=1, source_target_pairs={{0,8},{4,12},{8,0},{12,4},{16,24},{20,28},{24,16},{28,20},{1,9},{5... | collective-permute-start | bytes 46088 | tf_op jit(solution)/shard_map/ppermute | solution.py:24
  47.0 1.4 %collective-permute-done.11 = bf16[6,1280]{1,0:T(8,128)(2,1)S(1)} collective-permute-done((bf16[6,1280]{1,0:T(8,128)(2,1)S(1)}, bf16[6,1280]{1,0:T(8,128)(2,1)S(1)}, u32[]{:S(2)}, u32[]{:S(2)}) %collective-permute-start.11) | collective-permute-done | bytes 15392 | tf_op jit(solution)/shard_map/ppermute | solution.py:68
  48.4 1.3 %collective-permute-done.12 = bf16[6,1280]{1,0:T(8,128)(2,1)S(1)} collective-permute-done((bf16[6,1280]{1,0:T(8,128)(2,1)S(1)}, bf16[6,1280]{1,0:T(8,128)(2,1)S(1)}, u32[]{:S(2)}, u32[]{:S(2)}) %collective-permute-start.12) | collective-permute-done | bytes 15392 | tf_op jit(solution)/shard_map/ppermute | solution.py:71
  49.7 0.5 collective-permute-done.13
  50.2 0.6 %add_convert_fusion = bf16[6,1280]{1,0:T(8,128)(2,1)} fusion(bf16[6,1280]{1,0:T(8,128)(2,1)S(1)} %collective-permute-done.13, bf16[6,1280]{1,0:T(8,128)(2,1)S(1)} %collective-permute-done.12, bf16[6,1280]{1,0:T(8,128)(2,1)S(1)} %collective-permute-done.11, pred[]{:T(512)S(6)} %eq.23, f32[24,1280]{1,0:T(8,128)S(1)} %convert_add_fusion.1, pred[]{:T(512)S(6)} %eq.24), kind=kLoop, calls=%fused_computation.68 | loop fusion | flops 76800 | bytes 184322 | tf_op jit(solution)/shard_map/convert_element_type | solution.py:163
  (15 shorter events, 0.3 us)
Async XLA Ops:
  0.6 21.7 %copy-start = (bf16[176,5120]{1,0:T(8,128)(2,1)S(1)}, bf16[176,5120]{1,0:T(8,128)(2,1)}, u32[]{:S(2)}) copy-start(bf16[176,5120]{1,0:T(8,128)(2,1)} %param.6) | copy-start | bytes 5406724
  1.6 7.1 %collective-permute-start.2 = (bf16[6,2304]{1,0:T(8,128)(2,1)S(1)}, bf16[6,2304]{1,0:T(8,128)(2,1)S(1)}, u32[]{:S(2)}, u32[]{:S(2)}) collective-permute-start(bf16[6,2304]{1,0:T(8,128)(2,1)S(1)} %pad_select_fusion), channel_id=1, source_target_pairs={{0,24},{4,28},{8,16},{12,20},{16,8},{20,12},{24,0},{28,4},{1,25},{... | collective-permute-start | bytes 82952 | tf_op jit(solution)/shard_map/ppermute | solution.py:24
  6.7 4.9 %collective-permute-start.1 = (bf16[6,2304]{1,0:T(8,128)(2,1)S(1)}, bf16[6,2304]{1,0:T(8,128)(2,1)S(1)}, u32[]{:S(2)}, u32[]{:S(2)}) collective-permute-start(bf16[6,2304]{1,0:T(8,128)(2,1)S(1)} %pad_select_fusion), channel_id=1, source_target_pairs={{0,16},{4,20},{8,24},{12,28},{16,0},{20,4},{24,8},{28,12},{1,17},{... | collective-permute-start | bytes 82952 | tf_op jit(solution)/shard_map/ppermute | solution.py:24
  6.7 4.9 %collective-permute-start = (bf16[6,2304]{1,0:T(8,128)(2,1)S(1)}, bf16[6,2304]{1,0:T(8,128)(2,1)S(1)}, u32[]{:S(2)}, u32[]{:S(2)}) collective-permute-start(bf16[6,2304]{1,0:T(8,128)(2,1)S(1)} %pad_select_fusion), channel_id=1, source_target_pairs={{0,8},{4,12},{8,0},{12,4},{16,24},{20,28},{24,16},{28,20},{1,9},{5... | collective-permute-start | bytes 82952 | tf_op jit(solution)/shard_map/ppermute | solution.py:24
  11.6 6.9 %collective-permute-start.5 = (bf16[1,24,2304]{2,1,0:T(8,128)(2,1)S(1)}, bf16[1,24,2304]{2,1,0:T(8,128)(2,1)S(1)}, u32[]{:S(2)}, u32[]{:S(2)}) collective-permute-start(bf16[1,24,2304]{2,1,0:T(8,128)(2,1)S(1)} %maximum_bitcast_fusion), channel_id=1, source_target_pairs={{0,3},{1,2},{2,1},{3,0},{4,7},{5,6},{6,5},{7,4},{8,11},{9,10},{10,... | collective-permute-start | bytes 331784 | tf_op jit(solution)/shard_map/ppermute | solution.py:24
  14.1 5.2 %collective-permute-start.4 = (bf16[1,24,2304]{2,1,0:T(8,128)(2,1)S(1)}, bf16[1,24,2304]{2,1,0:T(8,128)(2,1)S(1)}, u32[]{:S(2)}, u32[]{:S(2)}) collective-permute-start(bf16[1,24,2304]{2,1,0:T(8,128)(2,1)S(1)} %maximum_bitcast_fusion), channel_id=1, source_target_pairs={{0,2},{1,3},{2,0},{3,1},{4,6},{5,7},{6,4},{7,5},{8,10},{9,11},{10,... | collective-permute-start | bytes 331784 | tf_op jit(solution)/shard_map/ppermute | solution.py:24
  14.6 4.7 %collective-permute-start.3 = (bf16[1,24,2304]{2,1,0:T(8,128)(2,1)S(1)}, bf16[1,24,2304]{2,1,0:T(8,128)(2,1)S(1)}, u32[]{:S(2)}, u32[]{:S(2)}) collective-permute-start(bf16[1,24,2304]{2,1,0:T(8,128)(2,1)S(1)} %maximum_bitcast_fusion), channel_id=1, source_target_pairs={{0,1},{1,0},{2,3},{3,2},{4,5},{5,4},{6,7},{7,6},{8,9},{9,8},{10,11... | collective-permute-start | bytes 331784 | tf_op jit(solution)/shard_map/ppermute | solution.py:24
  19.6 1.9 %collective-permute-start.6 = (bf16[4,24,2304]{2,1,0:T(8,128)(2,1)S(1)}, bf16[4,24,2304]{2,1,0:T(8,128)(2,1)S(1)}, u32[]{:S(2)}, u32[]{:S(2)}) collective-permute-start(bf16[4,24,2304]{2,1,0:T(8,128)(2,1)S(1)} %pad_maximum_fusion.1), channel_id=1, source_target_pairs={{0,4},{4,0},{8,12},{12,8},{16,20},{20,16},{24,28},{28,24},{1,5},{5... | collective-permute-start | bytes 1327112 | tf_op jit(solution)/shard_map/ppermute | solution.py:24
  19.7 2.0 %copy-start.1 = (bf16[176,4096]{1,0:T(8,128)(2,1)S(1)}, bf16[176,4096]{1,0:T(8,128)(2,1)}, u32[]{:S(2)}) copy-start(bf16[176,4096]{1,0:T(8,128)(2,1)} %param.7) | copy-start | bytes 4325380
  24.1 10.6 %all-to-all-start = ((f32[32,2,128]{2,1,0:T(2,128)}), f32[32,2,128]{2,1,0:T(2,128)S(1)}, u32[]{:S(2)}, u32[]{:S(2)}) async-start(f32[32,2,128]{2,1,0:T(2,128)} %broadcast_in_dim.8), calls=%async_computation | async-start | bytes 65536 | tf_op jit(solution)/shard_map/all_to_all | solution.py:126
  35.5 1.6 %collective-permute-start.7 = (bf16[24,5120]{1,0:T(8,128)(2,1)S(1)}, bf16[24,5120]{1,0:T(8,128)(2,1)S(1)}, u32[]{:S(2)}, u32[]{:S(2)}) collective-permute-start(bf16[24,5120]{1,0:T(8,128)(2,1)S(1)} %convolution_convert_fusion.1), channel_id=1, source_target_pairs={{0,4},{4,0},{8,12},{12,8},{16,20},{20,16},{24,28},{28,24},{1,5},{5... | collective-permute-start | bytes 737288 | tf_op jit(solution)/shard_map/ppermute | solution.py:24
  37.1 5.7 %collective-permute-start.8 = (bf16[24,1280]{1,0:T(8,128)(2,1)S(1)}, bf16[24,1280]{1,0:T(8,128)(2,1)S(1)}, u32[]{:S(2)}, u32[]{:S(2)}) collective-permute-start(bf16[24,1280]{1,0:T(8,128)(2,1)S(1)} %get-tuple-element.44), channel_id=1, source_target_pairs={{0,3},{1,2},{2,1},{3,0},{4,7},{5,6},{6,5},{7,4},{8,11},{9,10},{10,... | collective-permute-start | bytes 184328 | tf_op jit(solution)/shard_map/ppermute | solution.py:24
  37.8 5.1 %collective-permute-start.9 = (bf16[24,1280]{1,0:T(8,128)(2,1)S(1)}, bf16[24,1280]{1,0:T(8,128)(2,1)S(1)}, u32[]{:S(2)}, u32[]{:S(2)}) collective-permute-start(bf16[24,1280]{1,0:T(8,128)(2,1)S(1)} %get-tuple-element.45), channel_id=1, source_target_pairs={{0,2},{1,3},{2,0},{3,1},{4,6},{5,7},{6,4},{7,5},{8,10},{9,11},{10,... | collective-permute-start | bytes 184328 | tf_op jit(solution)/shard_map/ppermute | solution.py:24
  39.1 4.2 %collective-permute-start.10 = (bf16[24,1280]{1,0:T(8,128)(2,1)S(1)}, bf16[24,1280]{1,0:T(8,128)(2,1)S(1)}, u32[]{:S(2)}, u32[]{:S(2)}) collective-permute-start(bf16[24,1280]{1,0:T(8,128)(2,1)S(1)} %get-tuple-element.46), channel_id=1, source_target_pairs={{0,1},{1,0},{2,3},{3,2},{4,5},{5,4},{6,7},{7,6},{8,9},{9,8},{10,11... | collective-permute-start | bytes 184328 | tf_op jit(solution)/shard_map/ppermute | solution.py:24
  43.5 5.0 %collective-permute-start.11 = (bf16[6,1280]{1,0:T(8,128)(2,1)S(1)}, bf16[6,1280]{1,0:T(8,128)(2,1)S(1)}, u32[]{:S(2)}, u32[]{:S(2)}) collective-permute-start(bf16[6,1280]{1,0:T(8,128)(2,1)S(1)} %broadcast_select_fusion.19), channel_id=1, source_target_pairs={{0,24},{4,28},{8,16},{12,20},{16,0},{20,4},{24,8},{28,12},{1,25},{... | collective-permute-start | bytes 46088 | tf_op jit(solution)/shard_map/ppermute | solution.py:68
  44.1 5.6 %collective-permute-start.12 = (bf16[6,1280]{1,0:T(8,128)(2,1)S(1)}, bf16[6,1280]{1,0:T(8,128)(2,1)S(1)}, u32[]{:S(2)}, u32[]{:S(2)}) collective-permute-start(bf16[6,1280]{1,0:T(8,128)(2,1)S(1)} %get-tuple-element.21), channel_id=1, source_target_pairs={{0,16},{4,20},{8,24},{12,28},{16,8},{20,12},{24,0},{28,4},{1,17},{... | collective-permute-start | bytes 46088 | tf_op jit(solution)/shard_map/ppermute | solution.py:71
  46.4 3.8 %collective-permute-start.13 = (bf16[6,1280]{1,0:T(8,128)(2,1)S(1)}, bf16[6,1280]{1,0:T(8,128)(2,1)S(1)}, u32[]{:S(2)}, u32[]{:S(2)}) collective-permute-start(bf16[6,1280]{1,0:T(8,128)(2,1)S(1)} %get-tuple-element.22), channel_id=1, source_target_pairs={{0,8},{4,12},{8,0},{12,4},{16,24},{20,28},{24,16},{28,20},{1,9},{5... | collective-permute-start | bytes 46088 | tf_op jit(solution)/shard_map/ppermute | solution.py:24

commit v10 on v6

--- a/solution.py
+++ b/solution.py
@@ -1,6 +1,8 @@
 import jax
 import jax.numpy as jnp
 from jax import lax
+from jax.experimental import pallas as pl
+from jax.experimental.pallas import tpu as pltpu
 from jax.sharding import PartitionSpec as P
 
 
@@ -51,6 +53,33 @@
     return total
 
 
+def side_by_side(left, right):
+    rows, width = left.shape[0], left.shape[1] + right.shape[1]
+    if left.shape[1] % 128:
+        return jnp.concatenate([left, right], axis=1)
+
+    def kernel(left_ref, right_ref, out_ref, sems):
+        copies = [
+            pltpu.make_async_copy(left_ref, out_ref.at[:, : left.shape[1]], sems.at[0]),
+            pltpu.make_async_copy(right_ref, out_ref.at[:, left.shape[1] :], sems.at[1]),
+        ]
+        for copy in copies:
+            copy.start()
+        for copy in copies:
+            copy.wait()
+
+    return pl.pallas_call(
+        kernel,
+        out_shape=jax.ShapeDtypeStruct((rows, width), left.dtype),
+        in_specs=[pl.BlockSpec(memory_space=pltpu.HBM)] * 2,
+        out_specs=pl.BlockSpec(memory_space=pltpu.VMEM),
+        scratch_shapes=[pltpu.SemaphoreType.DMA((2,))],
+        cost_estimate=pl.CostEstimate(
+            flops=0, bytes_accessed=4 * rows * width, transcendentals=0
+        ),
+    )(left, right)
+
+
 def build(dp, vocab):
     dp_bits = range(dp.bit_length() - 1)
     vocab_bits = range(vocab.bit_length() - 1)
@@ -60,12 +89,7 @@
         rows, share = student_hidden.shape
         teacher_share = teacher_hidden.shape[1]
         tokens = rows * dp
-        lane = lax.broadcasted_iota(jnp.int32, (rows, share + teacher_share), 1)
-        packed = jnp.where(
-            lane < share,
-            jnp.pad(student_hidden, ((0, 0), (0, teacher_share))),
-            jnp.pad(teacher_hidden, ((0, 0), (share, 0))),
-        )
+        packed = side_by_side(student_hidden, teacher_hidden)
         by_z = gathered(packed, "dp", dp, z_bits, 0)
         by_vocab = gathered(by_z[None], "vocab", vocab, vocab_bits, 0)
         whole = gathered(by_vocab, "dp", dp, core, 1)

time: 49.6 us -> 51.3 us (1.034)
  Pallas kernels: 0 us -> 1.5 us
    pallas_call x0 -> x1, Pallas kernels: none -> 1.5 us  [side_by_side(): pl.pallas_call(kernel, out_shape=jax.ShapeDtypeStruct((rows, width), left...]
    select_n x1 -> x0, other arithmetic: 0.89 us -> none  [on_device(): jnp.where(lane < share, jnp.pad(student_hidden, ((0, 0), (0, teacher_shar...]
    select_n x3, other arithmetic: 0.26 us -> 1.03 us  [reorder(): jnp.where(lower, parts[j], parts[j ^ 1 << k])]
where the time goes in v10:
time: 51.3 us; the launch traced here: 51 us
  starting transfers between devices  17.5 us (34%)
  waiting for transfers between devices  14.1 us (27%)
  blocking collectives  10.4 us (20%)
  matrix products  4.03 us (8%)
  other arithmetic  2.43 us (5%)
  Pallas kernels  1.5 us (3%)
  between operations  0.81 us (2%)
    ppermute x14, starting transfers between devices, swap(): return lax.ppermute(value, axis, [(i, i ^ mask) for i in range(size)])  17.5 us
    ppermute x14, waiting for transfers between devices, swap(): return lax.ppermute(value, axis, [(i, i ^ mask) for i in range(size)])  14.1 us
    all_to_all x1, blocking collectives, on_device(): lax.all_to_all(jnp.broadcast_to(stats[None], (devices,) + stats.shape), (...  10.4 us
    dot_general x1, matrix products, on_device(): lax.dot_general(logit_grad, student_full, (((0,), (0,)), ((), ())), prefe...  1.87 us
    pallas_call x1, Pallas kernels, side_by_side(): pl.pallas_call(kernel, out_shape=jax.ShapeDtypeStruct((rows, width), left...  1.5 us
  transfers between devices with their start and end apart: 14, of which 12 were waited for; matrix products, arithmetic and copies ran while one was open for 4% of the time, Pallas kernels for 0%

profile of v10, /device:TPU:0, one launch (start us, length us, event | category | flops | bytes accessed | tf_op | source)
XLA Modules:
  0.0 51.0 jit_solution(13286395883878948386)
XLA Ops:
  0.6 0.0 copy-start
  0.6 1.5 %shard_map.59 = bf16[6,2304]{1,0:T(8,128)(2,1)} custom-call(bf16[6,1280]{1,0:T(8,128)(2,1)} %left_ref.1, bf16[6,1024]{1,0:T(8,128)(2,1)} %right_ref.1), custom_call_target="tpu_custom_call" | custom-call | bytes 55296 | tf_op jit(solution)/shard_map/pallas_call | solution.py:71
  2.1 5.1 %collective-permute-start.2 = (bf16[6,2304]{1,0:T(8,128)(2,1)}, bf16[6,2304]{1,0:T(8,128)(2,1)S(1)}, u32[]{:S(2)}, u32[]{:S(2)}) collective-permute-start(bf16[6,2304]{1,0:T(8,128)(2,1)} %shard_map.59), channel_id=1, source_target_pairs={{0,24},{4,28},{8,16},{12,20},{16,8},{20,12},{24,0},{28,4},{1,25},{... | collective-permute-start | bytes 82952 | tf_op jit(solution)/shard_map/ppermute | solution.py:26
  7.3 0.0 collective-permute-start.1
  7.3 0.6 %collective-permute-start = (bf16[6,2304]{1,0:T(8,128)(2,1)}, bf16[6,2304]{1,0:T(8,128)(2,1)S(1)}, u32[]{:S(2)}, u32[]{:S(2)}) collective-permute-start(bf16[6,2304]{1,0:T(8,128)(2,1)} %shard_map.59), channel_id=1, source_target_pairs={{0,8},{4,12},{8,0},{12,4},{16,24},{20,28},{24,16},{28,20},{1,9},{5... | collective-permute-start | bytes 82952 | tf_op jit(solution)/shard_map/ppermute | solution.py:26
  7.9 1.5 %collective-permute-done.2 = bf16[6,2304]{1,0:T(8,128)(2,1)S(1)} collective-permute-done((bf16[6,2304]{1,0:T(8,128)(2,1)}, bf16[6,2304]{1,0:T(8,128)(2,1)S(1)}, u32[]{:S(2)}, u32[]{:S(2)}) %collective-permute-start.2) | collective-permute-done | bytes 27680 | tf_op jit(solution)/shard_map/ppermute | solution.py:26
  9.4 2.9 %collective-permute-done.1 = bf16[6,2304]{1,0:T(8,128)(2,1)S(1)} collective-permute-done((bf16[6,2304]{1,0:T(8,128)(2,1)}, bf16[6,2304]{1,0:T(8,128)(2,1)S(1)}, u32[]{:S(2)}, u32[]{:S(2)}) %collective-permute-start.1) | collective-permute-done | bytes 27680 | tf_op jit(solution)/shard_map/ppermute | solution.py:26
  12.3 0.0 collective-permute-done
  12.3 0.8 %broadcast_select_fusion.17 = (bf16[6,2304]{1,0:T(8,128)(2,1)S(1)}, bf16[6,2304]{1,0:T(8,128)(2,1)S(1)}, bf16[6,2304]{1,0:T(8,128)(2,1)S(1)}, bf16[6,2304]{1,0:T(8,128)(2,1)S(1)}) fusion(pred[]{:T(512)S(6)} %eq.20, bf16[6,2304]{1,0:T(8,128)(2,1)} %shard_map.59, bf16[6,2304]{1,0:T(8,128)(2,1)S(1)} %collective-permute-done, pred[]{:T(512)S(6)} %eq.21, ...), kind=kLoop, calls=%fused_computation.83 | loop fusion | flops 110592 | bytes 221186 | tf_op jit(solution)/shard_map/jit(_where)/select_n | solution.py:21
  13.1 0.1 maximum_bitcast_fusion
  13.2 2.5 %collective-permute-start.5 = (bf16[1,24,2304]{2,1,0:T(8,128)(2,1)S(1)}, bf16[1,24,2304]{2,1,0:T(8,128)(2,1)S(1)}, u32[]{:S(2)}, u32[]{:S(2)}) collective-permute-start(bf16[1,24,2304]{2,1,0:T(8,128)(2,1)S(1)} %maximum_bitcast_fusion), channel_id=1, source_target_pairs={{0,3},{1,2},{2,1},{3,0},{4,7},{5,6},{6,5},{7,4},{8,11},{9,10},{10,... | collective-permute-start | bytes 331784 | tf_op jit(solution)/shard_map/ppermute | solution.py:26
  15.7 0.5 collective-permute-start.4
  16.2 0.5 %collective-permute-start.3 = (bf16[1,24,2304]{2,1,0:T(8,128)(2,1)S(1)}, bf16[1,24,2304]{2,1,0:T(8,128)(2,1)S(1)}, u32[]{:S(2)}, u32[]{:S(2)}) collective-permute-start(bf16[1,24,2304]{2,1,0:T(8,128)(2,1)S(1)} %maximum_bitcast_fusion), channel_id=1, source_target_pairs={{0,1},{1,0},{2,3},{3,2},{4,5},{5,4},{6,7},{7,6},{8,9},{9,8},{10,11... | collective-permute-start | bytes 331784 | tf_op jit(solution)/shard_map/ppermute | solution.py:26
  16.7 3.3 %collective-permute-done.5 = bf16[1,24,2304]{2,1,0:T(8,128)(2,1)S(1)} collective-permute-done((bf16[1,24,2304]{2,1,0:T(8,128)(2,1)S(1)}, bf16[1,24,2304]{2,1,0:T(8,128)(2,1)S(1)}, u32[]{:S(2)}, u32[]{:S(2)}) %collective-permute-start.5) | collective-permute-done | bytes 110624 | tf_op jit(solution)/shard_map/ppermute | solution.py:26
  20.1 0.8 %collective-permute-done.4 = bf16[1,24,2304]{2,1,0:T(8,128)(2,1)S(1)} collective-permute-done((bf16[1,24,2304]{2,1,0:T(8,128)(2,1)S(1)}, bf16[1,24,2304]{2,1,0:T(8,128)(2,1)S(1)}, u32[]{:S(2)}, u32[]{:S(2)}) %collective-permute-start.4) | collective-permute-done | bytes 110624 | tf_op jit(solution)/shard_map/ppermute | solution.py:26
  20.9 0.1 collective-permute-done.3
  21.0 0.1 broadcast_select_fusion.9
  21.1 0.1 pad_maximum_fusion.1
  21.2 0.1 collective-permute-start.6
  21.3 0.0 copy-start.1
  21.3 1.8 %collective-permute-done.6 = bf16[4,24,2304]{2,1,0:T(8,128)(2,1)S(1)} collective-permute-done((bf16[4,24,2304]{2,1,0:T(8,128)(2,1)S(1)}, bf16[4,24,2304]{2,1,0:T(8,128)(2,1)S(1)}, u32[]{:S(2)}, u32[]{:S(2)}) %collective-permute-start.6) | collective-permute-done | bytes 442400 | tf_op jit(solution)/shard_map/ppermute | solution.py:26
  23.0 0.1 broadcast_select_fusion.1
  23.2 0.0 copy-done.1
  23.2 0.7 %fusion.39 = (f32[48]{0:T(128)S(1)}, f32[48,176]{1,0:T(8,128)S(1)}) fusion(bf16[176,4096]{1,0:T(8,128)(2,1)S(1)} %copy-done.1, bf16[48,1024]{1,0:T(8,128)(2,1)S(1)} %get-tuple-element.31, bf16[48,1024]{1,0:T(8,128)(2,1)S(1)} %get-tuple-element.32, bf16[48,1024]{1,0:T(8,128)(2,1)S(1)} %get-tuple-element.30, bf16[48,1024]{1,0:T(8,128)(2,1)S(1)} %get-tuple-element.29), kind=kOutput, calls=%fused_computation.110 | convolution fusion | flops 70787280 | bytes 1868992 | tf_op jit(solution)/shard_map/dot_general | solution.py:103
  23.9 0.0 copy-done
  23.9 0.8 %fusion.40 = (f32[48]{0:T(128)S(1)}, f32[48,176]{1,0:T(8,128)S(1)}) fusion(bf16[176,5120]{1,0:T(8,128)(2,1)S(1)} %copy-done, bf16[48,1280]{1,0:T(8,128)(2,1)S(1)} %get-tuple-element.28, bf16[48,1280]{1,0:T(8,128)(2,1)S(1)} %get-tuple-element.27, bf16[48,1280]{1,0:T(8,128)(2,1)S(1)} %get-tuple-element.26, bf16[48,1280]{1,0:T(8,128)(2,1)S(1)} %get-tuple-element.25), kind=kOutput, calls=%fused_computation.111 | convolution fusion | flops 88482000 | bytes 2327744 | tf_op jit(solution)/shard_map/dot_general | solution.py:100
  24.7 0.2 fusion.24
  25.0 0.1 broadcast_in_dim.7
  25.1 10.4 %all_to_all.5 = f32[32,2,128]{2,1,0:T(2,128)S(1)} all-to-all(f32[32,2,128]{2,1,0:T(2,128)S(1)} %broadcast_in_dim.8), channel_id=1, replica_groups=mesh['dp'=8,'vocab'=4] {'dp','vocab'}, dimensions={0} | all-to-all | bytes 65536 | tf_op jit(solution)/shard_map/all_to_all | solution.py:121
  35.5 0.1 fusion.38
  35.8 0.1 multiply_convert_fusion
  35.9 0.3 convolution_convert_fusion.1
  36.2 0.1 collective-permute-start.7
  36.3 0.4 fusion.26
  36.6 1.1 %collective-permute-done.7 = bf16[24,5120]{1,0:T(8,128)(2,1)S(1)} collective-permute-done((bf16[24,5120]{1,0:T(8,128)(2,1)S(1)}, bf16[24,5120]{1,0:T(8,128)(2,1)S(1)}, u32[]{:S(2)}, u32[]{:S(2)}) %collective-permute-start.7) | collective-permute-done | bytes 245792 | tf_op jit(solution)/shard_map/ppermute | solution.py:26
  37.9 0.7 %collective-permute-start.8 = (bf16[24,1280]{1,0:T(8,128)(2,1)S(1)}, bf16[24,1280]{1,0:T(8,128)(2,1)S(1)}, u32[]{:S(2)}, u32[]{:S(2)}) collective-permute-start(bf16[24,1280]{1,0:T(8,128)(2,1)S(1)} %get-tuple-element.35), channel_id=1, source_target_pairs={{0,3},{1,2},{2,1},{3,0},{4,7},{5,6},{6,5},{7,4},{8,11},{9,10},{10,... | collective-permute-start | bytes 184328 | tf_op jit(solution)/shard_map/ppermute | solution.py:26
  38.5 1.3 %collective-permute-start.9 = (bf16[24,1280]{1,0:T(8,128)(2,1)S(1)}, bf16[24,1280]{1,0:T(8,128)(2,1)S(1)}, u32[]{:S(2)}, u32[]{:S(2)}) collective-permute-start(bf16[24,1280]{1,0:T(8,128)(2,1)S(1)} %get-tuple-element.36), channel_id=1, source_target_pairs={{0,2},{1,3},{2,0},{3,1},{4,6},{5,7},{6,4},{7,5},{8,10},{9,11},{10,... | collective-permute-start | bytes 184328 | tf_op jit(solution)/shard_map/ppermute | solution.py:26
  39.9 1.5 %collective-permute-start.10 = (bf16[24,1280]{1,0:T(8,128)(2,1)S(1)}, bf16[24,1280]{1,0:T(8,128)(2,1)S(1)}, u32[]{:S(2)}, u32[]{:S(2)}) collective-permute-start(bf16[24,1280]{1,0:T(8,128)(2,1)S(1)} %get-tuple-element.37), channel_id=1, source_target_pairs={{0,1},{1,0},{2,3},{3,2},{4,5},{5,4},{6,7},{7,6},{8,9},{9,8},{10,11... | collective-permute-start | bytes 184328 | tf_op jit(solution)/shard_map/ppermute | solution.py:26
  41.4 1.9 %convolution_convert_fusion = bf16[176,5120]{1,0:T(8,128)(2,1)} fusion(bf16[48,176]{1,0:T(8,128)(2,1)S(1)} %multiply_convert_fusion, bf16[48,1280]{1,0:T(8,128)(2,1)S(1)} %get-tuple-element.28, bf16[48,1280]{1,0:T(8,128)(2,1)S(1)} %get-tuple-element.27, bf16[48,1280]{1,0:T(8,128)(2,1)S(1)} %get-tuple-element.26, bf16[48,1280]{1,0:T(8,128)(2,1)S(1)} %get-tuple-element.25), kind=kOutput, calls=%fused_computation | convolution fusion | flops 89374720 | bytes 2310656 | tf_op jit(solution)/shard_map/dot_general | solution.py:152
  43.3 0.3 collective-permute-done.8
  43.6 0.1 collective-permute-done.9
  43.6 0.5 collective-permute-done.10
  44.2 0.7 %collective-permute-start.11 = (bf16[6,1280]{1,0:T(8,128)(2,1)S(1)}, bf16[6,1280]{1,0:T(8,128)(2,1)S(1)}, u32[]{:S(2)}, u32[]{:S(2)}) collective-permute-start(bf16[6,1280]{1,0:T(8,128)(2,1)S(1)} %get-tuple-element.46), channel_id=1, source_target_pairs={{0,24},{4,28},{8,16},{12,20},{16,8},{20,12},{24,0},{28,4},{1,25},{... | collective-permute-start | bytes 46088 | tf_op jit(solution)/shard_map/ppermute | solution.py:26
  44.9 1.4 %collective-permute-start.12 = (bf16[6,1280]{1,0:T(8,128)(2,1)S(1)}, bf16[6,1280]{1,0:T(8,128)(2,1)S(1)}, u32[]{:S(2)}, u32[]{:S(2)}) collective-permute-start(bf16[6,1280]{1,0:T(8,128)(2,1)S(1)} %get-tuple-element.47), channel_id=1, source_target_pairs={{0,16},{4,20},{8,24},{12,28},{16,0},{20,4},{24,8},{28,12},{1,17},{... | collective-permute-start | bytes 46088 | tf_op jit(solution)/shard_map/ppermute | solution.py:26
  46.3 2.3 %collective-permute-start.13 = (bf16[6,1280]{1,0:T(8,128)(2,1)S(1)}, bf16[6,1280]{1,0:T(8,128)(2,1)S(1)}, u32[]{:S(2)}, u32[]{:S(2)}) collective-permute-start(bf16[6,1280]{1,0:T(8,128)(2,1)S(1)} %get-tuple-element.48), channel_id=1, source_target_pairs={{0,8},{4,12},{8,0},{12,4},{16,24},{20,28},{24,16},{28,20},{1,9},{5... | collective-permute-start | bytes 46088 | tf_op jit(solution)/shard_map/ppermute | solution.py:26
  48.6 1.2 %collective-permute-done.11 = bf16[6,1280]{1,0:T(8,128)(2,1)S(1)} collective-permute-done((bf16[6,1280]{1,0:T(8,128)(2,1)S(1)}, bf16[6,1280]{1,0:T(8,128)(2,1)S(1)}, u32[]{:S(2)}, u32[]{:S(2)}) %collective-permute-start.11) | collective-permute-done | bytes 15392 | tf_op jit(solution)/shard_map/ppermute | solution.py:26
  49.8 0.0 collective-permute-done.12
  49.8 0.6 %collective-permute-done.13 = bf16[6,1280]{1,0:T(8,128)(2,1)S(1)} collective-permute-done((bf16[6,1280]{1,0:T(8,128)(2,1)S(1)}, bf16[6,1280]{1,0:T(8,128)(2,1)S(1)}, u32[]{:S(2)}, u32[]{:S(2)}) %collective-permute-start.13) | collective-permute-done | bytes 15392 | tf_op jit(solution)/shard_map/ppermute | solution.py:26
  50.4 0.6 %add_convert_fusion = bf16[6,1280]{1,0:T(8,128)(2,1)} fusion(bf16[6,1280]{1,0:T(8,128)(2,1)S(1)} %collective-permute-done.13, bf16[6,1280]{1,0:T(8,128)(2,1)S(1)} %collective-permute-done.12, bf16[6,1280]{1,0:T(8,128)(2,1)S(1)} %collective-permute-done.11, pred[]{:T(512)S(6)} %eq.20, f32[24,1280]{1,0:T(8,128)S(1)} %convert_add_fusion.1, pred[]{:T(512)S(6)} %eq.21), kind=kLoop, calls=%fused_computation.68 | loop fusion | flops 76800 | bytes 184322 | tf_op jit(solution)/shard_map/convert_element_type | solution.py:158
  (14 shorter events, 0.3 us)
Async XLA Ops:
  0.6 23.3 %copy-start = (bf16[176,5120]{1,0:T(8,128)(2,1)S(1)}, bf16[176,5120]{1,0:T(8,128)(2,1)}, u32[]{:S(2)}) copy-start(bf16[176,5120]{1,0:T(8,128)(2,1)} %param.6) | copy-start | bytes 5406724
  2.1 7.3 %collective-permute-start.2 = (bf16[6,2304]{1,0:T(8,128)(2,1)}, bf16[6,2304]{1,0:T(8,128)(2,1)S(1)}, u32[]{:S(2)}, u32[]{:S(2)}) collective-permute-start(bf16[6,2304]{1,0:T(8,128)(2,1)} %shard_map.59), channel_id=1, source_target_pairs={{0,24},{4,28},{8,16},{12,20},{16,8},{20,12},{24,0},{28,4},{1,25},{... | collective-permute-start | bytes 82952 | tf_op jit(solution)/shard_map/ppermute | solution.py:26
  7.3 5.1 %collective-permute-start.1 = (bf16[6,2304]{1,0:T(8,128)(2,1)}, bf16[6,2304]{1,0:T(8,128)(2,1)S(1)}, u32[]{:S(2)}, u32[]{:S(2)}) collective-permute-start(bf16[6,2304]{1,0:T(8,128)(2,1)} %shard_map.59), channel_id=1, source_target_pairs={{0,16},{4,20},{8,24},{12,28},{16,0},{20,4},{24,8},{28,12},{1,17},{... | collective-permute-start | bytes 82952 | tf_op jit(solution)/shard_map/ppermute | solution.py:26
  7.3 5.1 %collective-permute-start = (bf16[6,2304]{1,0:T(8,128)(2,1)}, bf16[6,2304]{1,0:T(8,128)(2,1)S(1)}, u32[]{:S(2)}, u32[]{:S(2)}) collective-permute-start(bf16[6,2304]{1,0:T(8,128)(2,1)} %shard_map.59), channel_id=1, source_target_pairs={{0,8},{4,12},{8,0},{12,4},{16,24},{20,28},{24,16},{28,20},{1,9},{5... | collective-permute-start | bytes 82952 | tf_op jit(solution)/shard_map/ppermute | solution.py:26
  13.2 6.9 %collective-permute-start.5 = (bf16[1,24,2304]{2,1,0:T(8,128)(2,1)S(1)}, bf16[1,24,2304]{2,1,0:T(8,128)(2,1)S(1)}, u32[]{:S(2)}, u32[]{:S(2)}) collective-permute-start(bf16[1,24,2304]{2,1,0:T(8,128)(2,1)S(1)} %maximum_bitcast_fusion), channel_id=1, source_target_pairs={{0,3},{1,2},{2,1},{3,0},{4,7},{5,6},{6,5},{7,4},{8,11},{9,10},{10,... | collective-permute-start | bytes 331784 | tf_op jit(solution)/shard_map/ppermute | solution.py:26
  15.7 5.2 %collective-permute-start.4 = (bf16[1,24,2304]{2,1,0:T(8,128)(2,1)S(1)}, bf16[1,24,2304]{2,1,0:T(8,128)(2,1)S(1)}, u32[]{:S(2)}, u32[]{:S(2)}) collective-permute-start(bf16[1,24,2304]{2,1,0:T(8,128)(2,1)S(1)} %maximum_bitcast_fusion), channel_id=1, source_target_pairs={{0,2},{1,3},{2,0},{3,1},{4,6},{5,7},{6,4},{7,5},{8,10},{9,11},{10,... | collective-permute-start | bytes 331784 | tf_op jit(solution)/shard_map/ppermute | solution.py:26
  16.2 4.7 %collective-permute-start.3 = (bf16[1,24,2304]{2,1,0:T(8,128)(2,1)S(1)}, bf16[1,24,2304]{2,1,0:T(8,128)(2,1)S(1)}, u32[]{:S(2)}, u32[]{:S(2)}) collective-permute-start(bf16[1,24,2304]{2,1,0:T(8,128)(2,1)S(1)} %maximum_bitcast_fusion), channel_id=1, source_target_pairs={{0,1},{1,0},{2,3},{3,2},{4,5},{5,4},{6,7},{7,6},{8,9},{9,8},{10,11... | collective-permute-start | bytes 331784 | tf_op jit(solution)/shard_map/ppermute | solution.py:26
  21.2 1.9 %collective-permute-start.6 = (bf16[4,24,2304]{2,1,0:T(8,128)(2,1)S(1)}, bf16[4,24,2304]{2,1,0:T(8,128)(2,1)S(1)}, u32[]{:S(2)}, u32[]{:S(2)}) collective-permute-start(bf16[4,24,2304]{2,1,0:T(8,128)(2,1)S(1)} %pad_maximum_fusion.1), channel_id=1, source_target_pairs={{0,4},{4,0},{8,12},{12,8},{16,20},{20,16},{24,28},{28,24},{1,5},{5... | collective-permute-start | bytes 1327112 | tf_op jit(solution)/shard_map/ppermute | solution.py:26
  21.3 2.0 %copy-start.1 = (bf16[176,4096]{1,0:T(8,128)(2,1)S(1)}, bf16[176,4096]{1,0:T(8,128)(2,1)}, u32[]{:S(2)}) copy-start(bf16[176,4096]{1,0:T(8,128)(2,1)} %param.7) | copy-start | bytes 4325380
  36.2 1.6 %collective-permute-start.7 = (bf16[24,5120]{1,0:T(8,128)(2,1)S(1)}, bf16[24,5120]{1,0:T(8,128)(2,1)S(1)}, u32[]{:S(2)}, u32[]{:S(2)}) collective-permute-start(bf16[24,5120]{1,0:T(8,128)(2,1)S(1)} %convolution_convert_fusion.1), channel_id=1, source_target_pairs={{0,4},{4,0},{8,12},{12,8},{16,20},{20,16},{24,28},{28,24},{1,5},{5... | collective-permute-start | bytes 737288 | tf_op jit(solution)/shard_map/ppermute | solution.py:26
  37.9 5.7 %collective-permute-start.8 = (bf16[24,1280]{1,0:T(8,128)(2,1)S(1)}, bf16[24,1280]{1,0:T(8,128)(2,1)S(1)}, u32[]{:S(2)}, u32[]{:S(2)}) collective-permute-start(bf16[24,1280]{1,0:T(8,128)(2,1)S(1)} %get-tuple-element.35), channel_id=1, source_target_pairs={{0,3},{1,2},{2,1},{3,0},{4,7},{5,6},{6,5},{7,4},{8,11},{9,10},{10,... | collective-permute-start | bytes 184328 | tf_op jit(solution)/shard_map/ppermute | solution.py:26
  38.5 5.1 %collective-permute-start.9 = (bf16[24,1280]{1,0:T(8,128)(2,1)S(1)}, bf16[24,1280]{1,0:T(8,128)(2,1)S(1)}, u32[]{:S(2)}, u32[]{:S(2)}) collective-permute-start(bf16[24,1280]{1,0:T(8,128)(2,1)S(1)} %get-tuple-element.36), channel_id=1, source_target_pairs={{0,2},{1,3},{2,0},{3,1},{4,6},{5,7},{6,4},{7,5},{8,10},{9,11},{10,... | collective-permute-start | bytes 184328 | tf_op jit(solution)/shard_map/ppermute | solution.py:26
  39.9 4.2 %collective-permute-start.10 = (bf16[24,1280]{1,0:T(8,128)(2,1)S(1)}, bf16[24,1280]{1,0:T(8,128)(2,1)S(1)}, u32[]{:S(2)}, u32[]{:S(2)}) collective-permute-start(bf16[24,1280]{1,0:T(8,128)(2,1)S(1)} %get-tuple-element.37), channel_id=1, source_target_pairs={{0,1},{1,0},{2,3},{3,2},{4,5},{5,4},{6,7},{7,6},{8,9},{9,8},{10,11... | collective-permute-start | bytes 184328 | tf_op jit(solution)/shard_map/ppermute | solution.py:26
  44.2 5.6 %collective-permute-start.11 = (bf16[6,1280]{1,0:T(8,128)(2,1)S(1)}, bf16[6,1280]{1,0:T(8,128)(2,1)S(1)}, u32[]{:S(2)}, u32[]{:S(2)}) collective-permute-start(bf16[6,1280]{1,0:T(8,128)(2,1)S(1)} %get-tuple-element.46), channel_id=1, source_target_pairs={{0,24},{4,28},{8,16},{12,20},{16,8},{20,12},{24,0},{28,4},{1,25},{... | collective-permute-start | bytes 46088 | tf_op jit(solution)/shard_map/ppermute | solution.py:26
  44.9 5.0 %collective-permute-start.12 = (bf16[6,1280]{1,0:T(8,128)(2,1)S(1)}, bf16[6,1280]{1,0:T(8,128)(2,1)S(1)}, u32[]{:S(2)}, u32[]{:S(2)}) collective-permute-start(bf16[6,1280]{1,0:T(8,128)(2,1)S(1)} %get-tuple-element.47), channel_id=1, source_target_pairs={{0,16},{4,20},{8,24},{12,28},{16,0},{20,4},{24,8},{28,12},{1,17},{... | collective-permute-start | bytes 46088 | tf_op jit(solution)/shard_map/ppermute | solution.py:26
  46.3 4.1 %collective-permute-start.13 = (bf16[6,1280]{1,0:T(8,128)(2,1)S(1)}, bf16[6,1280]{1,0:T(8,128)(2,1)S(1)}, u32[]{:S(2)}, u32[]{:S(2)}) collective-permute-start(bf16[6,1280]{1,0:T(8,128)(2,1)S(1)} %get-tuple-element.48), channel_id=1, source_target_pairs={{0,8},{4,12},{8,0},{12,4},{16,24},{20,28},{24,16},{28,20},{1,9},{5... | collective-permute-start | bytes 46088 | tf_op jit(solution)/shard_map/ppermute | solution.py:26

commit v11 on v6

--- a/solution.py
+++ b/solution.py
@@ -31,8 +31,9 @@
             j: swap(value, axis, size, mask_of(j, group))
             for j in reversed(range(1, 1 << len(group)))
         }
-        parts = lax.optimization_barrier([landed[j] for j in range(1, 1 << len(group))])
-        parts = [value] + list(parts)
+        order = sorted(landed, key=lambda j: (j == 3, -j if axis == "vocab" else j))
+        landed = dict(zip(order, lax.optimization_barrier([landed[j] for j in order])))
+        parts = [value] + [landed[j] for j in sorted(order)]
         value = jnp.concatenate(reorder(parts, index, group), axis=dim)
     return value
 

time: 49.6 us -> 49.7 us (level)
  no operation moved by 1% of the time
where the time goes in v11:
time: 49.7 us; the launch traced here: 49.5 us
  starting transfers between devices  17.5 us (35%)
  waiting for transfers between devices  13.9 us (28%)
  blocking collectives  10.5 us (21%)
  matrix products  4.03 us (8%)
  other arithmetic  2.57 us (5%)
  between operations  0.81 us (2%)
    ppermute x14, starting transfers between devices, swap(): return lax.ppermute(value, axis, [(i, i ^ mask) for i in range(size)])  17.5 us
    ppermute x14, waiting for transfers between devices, swap(): return lax.ppermute(value, axis, [(i, i ^ mask) for i in range(size)])  13.9 us
    all_to_all x1, blocking collectives, on_device(): lax.all_to_all(jnp.broadcast_to(stats[None], (devices,) + stats.shape), (...  10.5 us
    dot_general x1, matrix products, on_device(): lax.dot_general(logit_grad, student_full, (((0,), (0,)), ((), ())), prefe...  1.86 us
  transfers between devices with their start and end apart: 14, of which 12 were waited for; matrix products, arithmetic and copies ran while one was open for 4% of the time, Pallas kernels for 0%

profile of v11, /device:TPU:0, one launch (start us, length us, event | category | flops | bytes accessed | tf_op | source)
XLA Modules:
  0.0 49.5 jit_solution(17500801081852712481)
XLA Ops:
  0.6 0.0 copy-start
  0.7 0.9 %pad_select_fusion = bf16[6,2304]{1,0:T(8,128)(2,1)S(1)} fusion(bf16[6,1024]{1,0:T(8,128)(2,1)} %param.5, bf16[6,1280]{1,0:T(8,128)(2,1)} %param.4, pred[2304]{0:T(1024)(128)(4,1)S(1)} %iota_compare_fusion), kind=kLoop, calls=%fused_computation.76 | loop fusion | flops 13824 | bytes 57600 | tf_op jit(solution)/shard_map/jit(_where)/select_n | solution.py:65
  1.6 5.1 %collective-permute-start.2 = (bf16[6,2304]{1,0:T(8,128)(2,1)S(1)}, bf16[6,2304]{1,0:T(8,128)(2,1)S(1)}, u32[]{:S(2)}, u32[]{:S(2)}) collective-permute-start(bf16[6,2304]{1,0:T(8,128)(2,1)S(1)} %pad_select_fusion), channel_id=1, source_target_pairs={{0,24},{4,28},{8,16},{12,20},{16,8},{20,12},{24,0},{28,4},{1,25},{... | collective-permute-start | bytes 82952 | tf_op jit(solution)/shard_map/ppermute | solution.py:24
  6.7 0.0 collective-permute-start.1
  6.7 0.6 %collective-permute-start = (bf16[6,2304]{1,0:T(8,128)(2,1)S(1)}, bf16[6,2304]{1,0:T(8,128)(2,1)S(1)}, u32[]{:S(2)}, u32[]{:S(2)}) collective-permute-start(bf16[6,2304]{1,0:T(8,128)(2,1)S(1)} %pad_select_fusion), channel_id=1, source_target_pairs={{0,8},{4,12},{8,0},{12,4},{16,24},{20,28},{24,16},{28,20},{1,9},{5... | collective-permute-start | bytes 82952 | tf_op jit(solution)/shard_map/ppermute | solution.py:24
  7.3 1.3 %collective-permute-done.2 = bf16[6,2304]{1,0:T(8,128)(2,1)S(1)} collective-permute-done((bf16[6,2304]{1,0:T(8,128)(2,1)S(1)}, bf16[6,2304]{1,0:T(8,128)(2,1)S(1)}, u32[]{:S(2)}, u32[]{:S(2)}) %collective-permute-start.2) | collective-permute-done | bytes 27680 | tf_op jit(solution)/shard_map/ppermute | solution.py:24
  8.6 2.9 %collective-permute-done.1 = bf16[6,2304]{1,0:T(8,128)(2,1)S(1)} collective-permute-done((bf16[6,2304]{1,0:T(8,128)(2,1)S(1)}, bf16[6,2304]{1,0:T(8,128)(2,1)S(1)}, u32[]{:S(2)}, u32[]{:S(2)}) %collective-permute-start.1) | collective-permute-done | bytes 27680 | tf_op jit(solution)/shard_map/ppermute | solution.py:24
  11.5 0.0 collective-permute-done
  11.6 0.1 maximum_bitcast_fusion
  11.6 2.5 %collective-permute-start.5 = (bf16[1,24,2304]{2,1,0:T(8,128)(2,1)S(1)}, bf16[1,24,2304]{2,1,0:T(8,128)(2,1)S(1)}, u32[]{:S(2)}, u32[]{:S(2)}) collective-permute-start(bf16[1,24,2304]{2,1,0:T(8,128)(2,1)S(1)} %maximum_bitcast_fusion), channel_id=1, source_target_pairs={{0,3},{1,2},{2,1},{3,0},{4,7},{5,6},{6,5},{7,4},{8,11},{9,10},{10,... | collective-permute-start | bytes 331784 | tf_op jit(solution)/shard_map/ppermute | solution.py:24
  14.1 0.5 %collective-permute-start.4 = (bf16[1,24,2304]{2,1,0:T(8,128)(2,1)S(1)}, bf16[1,24,2304]{2,1,0:T(8,128)(2,1)S(1)}, u32[]{:S(2)}, u32[]{:S(2)}) collective-permute-start(bf16[1,24,2304]{2,1,0:T(8,128)(2,1)S(1)} %maximum_bitcast_fusion), channel_id=1, source_target_pairs={{0,1},{1,0},{2,3},{3,2},{4,5},{5,4},{6,7},{7,6},{8,9},{9,8},{10,11... | collective-permute-start | bytes 331784 | tf_op jit(solution)/shard_map/ppermute | solution.py:24
  14.7 0.5 %collective-permute-start.3 = (bf16[1,24,2304]{2,1,0:T(8,128)(2,1)S(1)}, bf16[1,24,2304]{2,1,0:T(8,128)(2,1)S(1)}, u32[]{:S(2)}, u32[]{:S(2)}) collective-permute-start(bf16[1,24,2304]{2,1,0:T(8,128)(2,1)S(1)} %maximum_bitcast_fusion), channel_id=1, source_target_pairs={{0,2},{1,3},{2,0},{3,1},{4,6},{5,7},{6,4},{7,5},{8,10},{9,11},{10,... | collective-permute-start | bytes 331784 | tf_op jit(solution)/shard_map/ppermute | solution.py:24
  15.2 2.3 %collective-permute-done.5 = bf16[1,24,2304]{2,1,0:T(8,128)(2,1)S(1)} collective-permute-done((bf16[1,24,2304]{2,1,0:T(8,128)(2,1)S(1)}, bf16[1,24,2304]{2,1,0:T(8,128)(2,1)S(1)}, u32[]{:S(2)}, u32[]{:S(2)}) %collective-permute-start.5) | collective-permute-done | bytes 110624 | tf_op jit(solution)/shard_map/ppermute | solution.py:24
  17.4 1.4 %collective-permute-done.4 = bf16[1,24,2304]{2,1,0:T(8,128)(2,1)S(1)} collective-permute-done((bf16[1,24,2304]{2,1,0:T(8,128)(2,1)S(1)}, bf16[1,24,2304]{2,1,0:T(8,128)(2,1)S(1)}, u32[]{:S(2)}, u32[]{:S(2)}) %collective-permute-start.4) | collective-permute-done | bytes 110624 | tf_op jit(solution)/shard_map/ppermute | solution.py:24
  18.9 0.5 %collective-permute-done.3 = bf16[1,24,2304]{2,1,0:T(8,128)(2,1)S(1)} collective-permute-done((bf16[1,24,2304]{2,1,0:T(8,128)(2,1)S(1)}, bf16[1,24,2304]{2,1,0:T(8,128)(2,1)S(1)}, u32[]{:S(2)}, u32[]{:S(2)}) %collective-permute-start.3) | collective-permute-done | bytes 110624 | tf_op jit(solution)/shard_map/ppermute | solution.py:24
  19.4 0.1 broadcast_select_fusion.9
  19.6 0.1 pad_maximum_fusion.1
  19.6 0.1 collective-permute-start.6
  19.7 0.0 copy-start.1
  19.7 1.8 %collective-permute-done.6 = bf16[4,24,2304]{2,1,0:T(8,128)(2,1)S(1)} collective-permute-done((bf16[4,24,2304]{2,1,0:T(8,128)(2,1)S(1)}, bf16[4,24,2304]{2,1,0:T(8,128)(2,1)S(1)}, u32[]{:S(2)}, u32[]{:S(2)}) %collective-permute-start.6) | collective-permute-done | bytes 442400 | tf_op jit(solution)/shard_map/ppermute | solution.py:24
  21.5 0.1 broadcast_select_fusion.1
  21.7 0.0 copy-done.1
  21.7 0.7 %fusion.39 = (f32[48]{0:T(128)S(1)}, f32[48,176]{1,0:T(8,128)S(1)}) fusion(bf16[176,4096]{1,0:T(8,128)(2,1)S(1)} %copy-done.1, bf16[48,1024]{1,0:T(8,128)(2,1)S(1)} %get-tuple-element.31, bf16[48,1024]{1,0:T(8,128)(2,1)S(1)} %get-tuple-element.32, bf16[48,1024]{1,0:T(8,128)(2,1)S(1)} %get-tuple-element.30, bf16[48,1024]{1,0:T(8,128)(2,1)S(1)} %get-tuple-element.29), kind=kOutput, calls=%fused_computation.112 | convolution fusion | flops 70787280 | bytes 1868992 | tf_op jit(solution)/shard_map/dot_general | solution.py:80
  22.4 0.0 copy-done
  22.4 0.8 %fusion.40 = (f32[48]{0:T(128)S(1)}, f32[48,176]{1,0:T(8,128)S(1)}) fusion(bf16[176,5120]{1,0:T(8,128)(2,1)S(1)} %copy-done, bf16[48,1280]{1,0:T(8,128)(2,1)S(1)} %get-tuple-element.28, bf16[48,1280]{1,0:T(8,128)(2,1)S(1)} %get-tuple-element.27, bf16[48,1280]{1,0:T(8,128)(2,1)S(1)} %get-tuple-element.26, bf16[48,1280]{1,0:T(8,128)(2,1)S(1)} %get-tuple-element.25), kind=kOutput, calls=%fused_computation.113 | convolution fusion | flops 88482000 | bytes 2327744 | tf_op jit(solution)/shard_map/dot_general | solution.py:77
  23.2 0.2 fusion.24
  23.4 0.1 broadcast_in_dim.7
  23.5 10.5 %all_to_all.5 = f32[32,2,128]{2,1,0:T(2,128)S(1)} all-to-all(f32[32,2,128]{2,1,0:T(2,128)S(1)} %broadcast_in_dim.8), channel_id=1, replica_groups=mesh['dp'=8,'vocab'=4] {'dp','vocab'}, dimensions={0} | all-to-all | bytes 65536 | tf_op jit(solution)/shard_map/all_to_all | solution.py:98
  34.0 0.1 fusion.38
  34.2 0.1 multiply_convert_fusion
  34.3 0.3 convolution_convert_fusion.1
  34.7 0.1 collective-permute-start.7
  34.8 0.4 fusion.26
  35.1 1.1 %collective-permute-done.7 = bf16[24,5120]{1,0:T(8,128)(2,1)S(1)} collective-permute-done((bf16[24,5120]{1,0:T(8,128)(2,1)S(1)}, bf16[24,5120]{1,0:T(8,128)(2,1)S(1)}, u32[]{:S(2)}, u32[]{:S(2)}) %collective-permute-start.7) | collective-permute-done | bytes 245792 | tf_op jit(solution)/shard_map/ppermute | solution.py:24
  36.4 0.7 %collective-permute-start.8 = (bf16[24,1280]{1,0:T(8,128)(2,1)S(1)}, bf16[24,1280]{1,0:T(8,128)(2,1)S(1)}, u32[]{:S(2)}, u32[]{:S(2)}) collective-permute-start(bf16[24,1280]{1,0:T(8,128)(2,1)S(1)} %get-tuple-element.35), channel_id=1, source_target_pairs={{0,3},{1,2},{2,1},{3,0},{4,7},{5,6},{6,5},{7,4},{8,11},{9,10},{10,... | collective-permute-start | bytes 184328 | tf_op jit(solution)/shard_map/ppermute | solution.py:24
  37.0 1.3 %collective-permute-start.9 = (bf16[24,1280]{1,0:T(8,128)(2,1)S(1)}, bf16[24,1280]{1,0:T(8,128)(2,1)S(1)}, u32[]{:S(2)}, u32[]{:S(2)}) collective-permute-start(bf16[24,1280]{1,0:T(8,128)(2,1)S(1)} %get-tuple-element.36), channel_id=1, source_target_pairs={{0,2},{1,3},{2,0},{3,1},{4,6},{5,7},{6,4},{7,5},{8,10},{9,11},{10,... | collective-permute-start | bytes 184328 | tf_op jit(solution)/shard_map/ppermute | solution.py:24
  38.4 1.5 %collective-permute-start.10 = (bf16[24,1280]{1,0:T(8,128)(2,1)S(1)}, bf16[24,1280]{1,0:T(8,128)(2,1)S(1)}, u32[]{:S(2)}, u32[]{:S(2)}) collective-permute-start(bf16[24,1280]{1,0:T(8,128)(2,1)S(1)} %get-tuple-element.37), channel_id=1, source_target_pairs={{0,1},{1,0},{2,3},{3,2},{4,5},{5,4},{6,7},{7,6},{8,9},{9,8},{10,11... | collective-permute-start | bytes 184328 | tf_op jit(solution)/shard_map/ppermute | solution.py:24
  39.9 1.9 %convolution_convert_fusion = bf16[176,5120]{1,0:T(8,128)(2,1)} fusion(bf16[48,176]{1,0:T(8,128)(2,1)S(1)} %multiply_convert_fusion, bf16[48,1280]{1,0:T(8,128)(2,1)S(1)} %get-tuple-element.28, bf16[48,1280]{1,0:T(8,128)(2,1)S(1)} %get-tuple-element.27, bf16[48,1280]{1,0:T(8,128)(2,1)S(1)} %get-tuple-element.26, bf16[48,1280]{1,0:T(8,128)(2,1)S(1)} %get-tuple-element.25), kind=kOutput, calls=%fused_computation | convolution fusion | flops 89374720 | bytes 2310656 | tf_op jit(solution)/shard_map/dot_general | solution.py:129
  41.8 0.3 collective-permute-done.8
  42.0 0.1 collective-permute-done.9
  42.1 0.5 collective-permute-done.10
  42.6 0.1 convert_add_fusion.1
  42.7 0.7 %collective-permute-start.11 = (bf16[6,1280]{1,0:T(8,128)(2,1)S(1)}, bf16[6,1280]{1,0:T(8,128)(2,1)S(1)}, u32[]{:S(2)}, u32[]{:S(2)}) collective-permute-start(bf16[6,1280]{1,0:T(8,128)(2,1)S(1)} %get-tuple-element.46), channel_id=1, source_target_pairs={{0,24},{4,28},{8,16},{12,20},{16,8},{20,12},{24,0},{28,4},{1,25},{... | collective-permute-start | bytes 46088 | tf_op jit(solution)/shard_map/ppermute | solution.py:24
  43.4 1.4 %collective-permute-start.12 = (bf16[6,1280]{1,0:T(8,128)(2,1)S(1)}, bf16[6,1280]{1,0:T(8,128)(2,1)S(1)}, u32[]{:S(2)}, u32[]{:S(2)}) collective-permute-start(bf16[6,1280]{1,0:T(8,128)(2,1)S(1)} %get-tuple-element.47), channel_id=1, source_target_pairs={{0,16},{4,20},{8,24},{12,28},{16,0},{20,4},{24,8},{28,12},{1,17},{... | collective-permute-start | bytes 46088 | tf_op jit(solution)/shard_map/ppermute | solution.py:24
  44.8 2.3 %collective-permute-start.13 = (bf16[6,1280]{1,0:T(8,128)(2,1)S(1)}, bf16[6,1280]{1,0:T(8,128)(2,1)S(1)}, u32[]{:S(2)}, u32[]{:S(2)}) collective-permute-start(bf16[6,1280]{1,0:T(8,128)(2,1)S(1)} %get-tuple-element.48), channel_id=1, source_target_pairs={{0,8},{4,12},{8,0},{12,4},{16,24},{20,28},{24,16},{28,20},{1,9},{5... | collective-permute-start | bytes 46088 | tf_op jit(solution)/shard_map/ppermute | solution.py:24
  47.1 1.2 %collective-permute-done.11 = bf16[6,1280]{1,0:T(8,128)(2,1)S(1)} collective-permute-done((bf16[6,1280]{1,0:T(8,128)(2,1)S(1)}, bf16[6,1280]{1,0:T(8,128)(2,1)S(1)}, u32[]{:S(2)}, u32[]{:S(2)}) %collective-permute-start.11) | collective-permute-done | bytes 15392 | tf_op jit(solution)/shard_map/ppermute | solution.py:24
  48.3 0.0 collective-permute-done.12
  48.3 0.6 %collective-permute-done.13 = bf16[6,1280]{1,0:T(8,128)(2,1)S(1)} collective-permute-done((bf16[6,1280]{1,0:T(8,128)(2,1)S(1)}, bf16[6,1280]{1,0:T(8,128)(2,1)S(1)}, u32[]{:S(2)}, u32[]{:S(2)}) %collective-permute-start.13) | collective-permute-done | bytes 15392 | tf_op jit(solution)/shard_map/ppermute | solution.py:24
  48.9 0.6 %add_convert_fusion = bf16[6,1280]{1,0:T(8,128)(2,1)} fusion(bf16[6,1280]{1,0:T(8,128)(2,1)S(1)} %collective-permute-done.13, bf16[6,1280]{1,0:T(8,128)(2,1)S(1)} %collective-permute-done.12, bf16[6,1280]{1,0:T(8,128)(2,1)S(1)} %collective-permute-done.11, pred[]{:T(512)S(6)} %eq.20, f32[24,1280]{1,0:T(8,128)S(1)} %convert_add_fusion.1, pred[]{:T(512)S(6)} %eq.21), kind=kLoop, calls=%fused_computation.68 | loop fusion | flops 76800 | bytes 184322 | tf_op jit(solution)/shard_map/convert_element_type | solution.py:135
  (15 shorter events, 0.3 us)
Async XLA Ops:
  0.6 21.7 %copy-start = (bf16[176,5120]{1,0:T(8,128)(2,1)S(1)}, bf16[176,5120]{1,0:T(8,128)(2,1)}, u32[]{:S(2)}) copy-start(bf16[176,5120]{1,0:T(8,128)(2,1)} %param.6) | copy-start | bytes 5406724
  1.6 7.1 %collective-permute-start.2 = (bf16[6,2304]{1,0:T(8,128)(2,1)S(1)}, bf16[6,2304]{1,0:T(8,128)(2,1)S(1)}, u32[]{:S(2)}, u32[]{:S(2)}) collective-permute-start(bf16[6,2304]{1,0:T(8,128)(2,1)S(1)} %pad_select_fusion), channel_id=1, source_target_pairs={{0,24},{4,28},{8,16},{12,20},{16,8},{20,12},{24,0},{28,4},{1,25},{... | collective-permute-start | bytes 82952 | tf_op jit(solution)/shard_map/ppermute | solution.py:24
  6.7 4.9 %collective-permute-start.1 = (bf16[6,2304]{1,0:T(8,128)(2,1)S(1)}, bf16[6,2304]{1,0:T(8,128)(2,1)S(1)}, u32[]{:S(2)}, u32[]{:S(2)}) collective-permute-start(bf16[6,2304]{1,0:T(8,128)(2,1)S(1)} %pad_select_fusion), channel_id=1, source_target_pairs={{0,16},{4,20},{8,24},{12,28},{16,0},{20,4},{24,8},{28,12},{1,17},{... | collective-permute-start | bytes 82952 | tf_op jit(solution)/shard_map/ppermute | solution.py:24
  6.7 4.9 %collective-permute-start = (bf16[6,2304]{1,0:T(8,128)(2,1)S(1)}, bf16[6,2304]{1,0:T(8,128)(2,1)S(1)}, u32[]{:S(2)}, u32[]{:S(2)}) collective-permute-start(bf16[6,2304]{1,0:T(8,128)(2,1)S(1)} %pad_select_fusion), channel_id=1, source_target_pairs={{0,8},{4,12},{8,0},{12,4},{16,24},{20,28},{24,16},{28,20},{1,9},{5... | collective-permute-start | bytes 82952 | tf_op jit(solution)/shard_map/ppermute | solution.py:24
  11.6 5.8 %collective-permute-start.5 = (bf16[1,24,2304]{2,1,0:T(8,128)(2,1)S(1)}, bf16[1,24,2304]{2,1,0:T(8,128)(2,1)S(1)}, u32[]{:S(2)}, u32[]{:S(2)}) collective-permute-start(bf16[1,24,2304]{2,1,0:T(8,128)(2,1)S(1)} %maximum_bitcast_fusion), channel_id=1, source_target_pairs={{0,3},{1,2},{2,1},{3,0},{4,7},{5,6},{6,5},{7,4},{8,11},{9,10},{10,... | collective-permute-start | bytes 331784 | tf_op jit(solution)/shard_map/ppermute | solution.py:24
  14.1 4.7 %collective-permute-start.4 = (bf16[1,24,2304]{2,1,0:T(8,128)(2,1)S(1)}, bf16[1,24,2304]{2,1,0:T(8,128)(2,1)S(1)}, u32[]{:S(2)}, u32[]{:S(2)}) collective-permute-start(bf16[1,24,2304]{2,1,0:T(8,128)(2,1)S(1)} %maximum_bitcast_fusion), channel_id=1, source_target_pairs={{0,1},{1,0},{2,3},{3,2},{4,5},{5,4},{6,7},{7,6},{8,9},{9,8},{10,11... | collective-permute-start | bytes 331784 | tf_op jit(solution)/shard_map/ppermute | solution.py:24
  14.7 4.7 %collective-permute-start.3 = (bf16[1,24,2304]{2,1,0:T(8,128)(2,1)S(1)}, bf16[1,24,2304]{2,1,0:T(8,128)(2,1)S(1)}, u32[]{:S(2)}, u32[]{:S(2)}) collective-permute-start(bf16[1,24,2304]{2,1,0:T(8,128)(2,1)S(1)} %maximum_bitcast_fusion), channel_id=1, source_target_pairs={{0,2},{1,3},{2,0},{3,1},{4,6},{5,7},{6,4},{7,5},{8,10},{9,11},{10,... | collective-permute-start | bytes 331784 | tf_op jit(solution)/shard_map/ppermute | solution.py:24
  19.6 1.9 %collective-permute-start.6 = (bf16[4,24,2304]{2,1,0:T(8,128)(2,1)S(1)}, bf16[4,24,2304]{2,1,0:T(8,128)(2,1)S(1)}, u32[]{:S(2)}, u32[]{:S(2)}) collective-permute-start(bf16[4,24,2304]{2,1,0:T(8,128)(2,1)S(1)} %pad_maximum_fusion.1), channel_id=1, source_target_pairs={{0,4},{4,0},{8,12},{12,8},{16,20},{20,16},{24,28},{28,24},{1,5},{5... | collective-permute-start | bytes 1327112 | tf_op jit(solution)/shard_map/ppermute | solution.py:24
  19.7 2.0 %copy-start.1 = (bf16[176,4096]{1,0:T(8,128)(2,1)S(1)}, bf16[176,4096]{1,0:T(8,128)(2,1)}, u32[]{:S(2)}) copy-start(bf16[176,4096]{1,0:T(8,128)(2,1)} %param.7) | copy-start | bytes 4325380
  34.7 1.6 %collective-permute-start.7 = (bf16[24,5120]{1,0:T(8,128)(2,1)S(1)}, bf16[24,5120]{1,0:T(8,128)(2,1)S(1)}, u32[]{:S(2)}, u32[]{:S(2)}) collective-permute-start(bf16[24,5120]{1,0:T(8,128)(2,1)S(1)} %convolution_convert_fusion.1), channel_id=1, source_target_pairs={{0,4},{4,0},{8,12},{12,8},{16,20},{20,16},{24,28},{28,24},{1,5},{5... | collective-permute-start | bytes 737288 | tf_op jit(solution)/shard_map/ppermute | solution.py:24
  36.4 5.7 %collective-permute-start.8 = (bf16[24,1280]{1,0:T(8,128)(2,1)S(1)}, bf16[24,1280]{1,0:T(8,128)(2,1)S(1)}, u32[]{:S(2)}, u32[]{:S(2)}) collective-permute-start(bf16[24,1280]{1,0:T(8,128)(2,1)S(1)} %get-tuple-element.35), channel_id=1, source_target_pairs={{0,3},{1,2},{2,1},{3,0},{4,7},{5,6},{6,5},{7,4},{8,11},{9,10},{10,... | collective-permute-start | bytes 184328 | tf_op jit(solution)/shard_map/ppermute | solution.py:24
  37.0 5.1 %collective-permute-start.9 = (bf16[24,1280]{1,0:T(8,128)(2,1)S(1)}, bf16[24,1280]{1,0:T(8,128)(2,1)S(1)}, u32[]{:S(2)}, u32[]{:S(2)}) collective-permute-start(bf16[24,1280]{1,0:T(8,128)(2,1)S(1)} %get-tuple-element.36), channel_id=1, source_target_pairs={{0,2},{1,3},{2,0},{3,1},{4,6},{5,7},{6,4},{7,5},{8,10},{9,11},{10,... | collective-permute-start | bytes 184328 | tf_op jit(solution)/shard_map/ppermute | solution.py:24
  38.4 4.2 %collective-permute-start.10 = (bf16[24,1280]{1,0:T(8,128)(2,1)S(1)}, bf16[24,1280]{1,0:T(8,128)(2,1)S(1)}, u32[]{:S(2)}, u32[]{:S(2)}) collective-permute-start(bf16[24,1280]{1,0:T(8,128)(2,1)S(1)} %get-tuple-element.37), channel_id=1, source_target_pairs={{0,1},{1,0},{2,3},{3,2},{4,5},{5,4},{6,7},{7,6},{8,9},{9,8},{10,11... | collective-permute-start | bytes 184328 | tf_op jit(solution)/shard_map/ppermute | solution.py:24
  42.7 5.6 %collective-permute-start.11 = (bf16[6,1280]{1,0:T(8,128)(2,1)S(1)}, bf16[6,1280]{1,0:T(8,128)(2,1)S(1)}, u32[]{:S(2)}, u32[]{:S(2)}) collective-permute-start(bf16[6,1280]{1,0:T(8,128)(2,1)S(1)} %get-tuple-element.46), channel_id=1, source_target_pairs={{0,24},{4,28},{8,16},{12,20},{16,8},{20,12},{24,0},{28,4},{1,25},{... | collective-permute-start | bytes 46088 | tf_op jit(solution)/shard_map/ppermute | solution.py:24
  43.4 5.0 %collective-permute-start.12 = (bf16[6,1280]{1,0:T(8,128)(2,1)S(1)}, bf16[6,1280]{1,0:T(8,128)(2,1)S(1)}, u32[]{:S(2)}, u32[]{:S(2)}) collective-permute-start(bf16[6,1280]{1,0:T(8,128)(2,1)S(1)} %get-tuple-element.47), channel_id=1, source_target_pairs={{0,16},{4,20},{8,24},{12,28},{16,0},{20,4},{24,8},{28,12},{1,17},{... | collective-permute-start | bytes 46088 | tf_op jit(solution)/shard_map/ppermute | solution.py:24
  44.8 4.1 %collective-permute-start.13 = (bf16[6,1280]{1,0:T(8,128)(2,1)S(1)}, bf16[6,1280]{1,0:T(8,128)(2,1)S(1)}, u32[]{:S(2)}, u32[]{:S(2)}) collective-permute-start(bf16[6,1280]{1,0:T(8,128)(2,1)S(1)} %get-tuple-element.48), channel_id=1, source_target_pairs={{0,8},{4,12},{8,0},{12,4},{16,24},{20,28},{24,16},{28,20},{1,9},{5... | collective-permute-start | bytes 46088 | tf_op jit(solution)/shard_map/ppermute | solution.py:24
